TPU v7x, 32 devices: a whole 2x2x4 slice. The times are simulated.
32 devices in a mesh: leaf: 2 (over y), blk: 16 (over z, x, core).
Axes of the slice: x: 2, y: 2, z: 4, core: 2. Of those that a mesh axis runs over, the one named last changes fastest.
Arguments:
- right_sides: bfloat16 [2, 16, 4, 512, 32], P('leaf', 'blk'), may hold values from -6 to 6
- inverses: bfloat16 [2, 16, 4, 512, 512], P('leaf', 'blk')
- couplings: bfloat16 [2, 16, 3, 256, 512], P('leaf', 'blk'), may hold values from -0.25 to 0.25
- widths: int32 [2, 16, 4], P('leaf', 'blk'), may hold values from 1 to 4, as said below
- targets: int32 [3, 2, 16, 64], replicated, may hold values from 0 to 4095, as said below
Outputs:
- solution: bfloat16 [2, 16, 4, 512, 32], P('leaf', 'blk')
Inputs may be any that keep to these rules, and one draw needn't show every extreme that they name: `widths`: at every level some device has 4 live block units. `targets`: every piece names live rows of its target supernode. At level l, with partner group g XOR 2 ** (l % log2(2)), devices (g, j) and (partner, j) together send at most 9 pieces to owners of blk index d, counting both groups. For each such pair of groups there are one blk index h and one of the two groups such that every pair (g, j), (partner, j) sends exactly 9 pieces to index h of that group, all from one of its two devices.
All inputs are finite; a program needn't handle non-finite values.
Results may differ from a plain program's by a relative error of at most 0.012.
Values may be sent and summed in bfloat16 or wider, within the bound.
No kernel may reach another device: no remote copies, remote signals or barrier semaphores. Data moves between devices by JAX's collectives and lax.ppermute only.
A program may use at most 64 MiB of HBM per device.

v0:
```python
import jax
import jax.numpy as jnp
from jax import lax
from jax.sharding import PartitionSpec as P

BLOCK = 128


def partner_2(array, axis, distance):
    return lax.ppermute(array, axis, [(i, i ^ 1 << distance) for i in range(lax.axis_size(axis))])


def plain_dot(left, right):
    return jnp.dot(left, right, preferred_element_type=jnp.float32)


def trans_dot(left, right):
    return lax.dot_general(
        left, right, (((0,), (0,)), ((), ())), preferred_element_type=jnp.float32
    )


def decode_codes(code_list, blk_count, place_count):
    side_bit = code_list // (blk_count * place_count)
    dest_blk = code_list // place_count % blk_count
    row_place = code_list % place_count
    return (side_bit, dest_blk, row_place)


def rank_pieces(dest_blk, valid):
    position = jnp.arange(dest_blk.shape[-1])
    earlier = position[:, None] < position[None, :]
    matches = (dest_blk[..., :, None] == dest_blk[..., None, :]) & valid[..., :, None] & earlier
    return jnp.sum(matches.astype(jnp.int32), axis=-2)


def send_matrix(dest_blk, rank, valid, slot_cap, slot_count):
    slot_of = dest_blk * slot_cap + rank
    chosen = (jnp.arange(slot_count)[:, None] == slot_of[None, :]) & valid[None, :]
    return chosen.astype(jnp.bfloat16)


def receive_matrix(rank, row_place, used, slot_cap, place_count):
    place_hot = ((row_place[:, :, None] == jnp.arange(place_count)) & used[:, :, None]).astype(
        jnp.float32
    )
    rank_hot = (rank[:, :, None] == jnp.arange(slot_cap)).astype(jnp.float32)
    layout = jnp.einsum("skq,skc->qsc", place_hot, rank_hot)
    return layout.reshape(place_count, -1).astype(jnp.bfloat16)


def pick_row(table, index):
    return lax.dynamic_index_in_dim(table, index, 0, keepdims=False)


def shards(right_sides, inverses, couplings, widths, targets):
    blk_count = lax.axis_size("blk")
    leaf_count = lax.axis_size("leaf")
    leaf_bits = leaf_count.bit_length() - 1
    group_index = lax.axis_index("leaf")
    owner_index = lax.axis_index("blk")
    right_side = right_sides[0, 0]
    inverse = inverses[0, 0]
    coupling = couplings[0, 0]
    live_blocks = widths[0, 0]
    levels, node_width, col_count = right_side.shape
    piece_count = targets.shape[3]
    piece_rows = coupling.shape[1] // piece_count
    place_count = node_width // piece_rows
    flat_width = piece_rows * col_count
    slot_cap = max(3, (2 * piece_count + blk_count - 1) // blk_count + 1)
    slot_count = blk_count * slot_cap
    row_index = jnp.arange(node_width)
    row_masks = [
        (row_index < live_blocks[level] * BLOCK).astype(jnp.float32)[:, None]
        for level in range(levels)
    ]
    forward = []
    routes = []
    incoming = None
    for level in range(levels):
        if level == 0:
            residual = right_side[0]
        else:
            residual = (right_side[level].astype(jnp.float32) - incoming).astype(jnp.bfloat16)
        solved = (row_masks[level] * plain_dot(inverse[level], residual)).astype(jnp.bfloat16)
        forward.append(solved)
        if level + 1 < levels:
            pieces = (
                plain_dot(coupling[level], solved)
                .astype(jnp.bfloat16)
                .reshape(piece_count, flat_width)
            )
            leaf_bit = level % leaf_bits
            partner = jnp.bitwise_xor(group_index, 1 << leaf_bit)
            own_table = pick_row(targets[level], group_index)
            pair_table = pick_row(targets[level], partner)
            own_side, own_dest, own_place = decode_codes(own_table, blk_count, place_count)
            pair_side, pair_dest, pair_place = decode_codes(pair_table, blk_count, place_count)
            mine_dest = pick_row(own_dest, owner_index)
            every_piece = jnp.ones(mine_dest.shape, bool)
            mine_rank = rank_pieces(mine_dest[None], every_piece[None])[0]
            sender = send_matrix(mine_dest, mine_rank, every_piece, slot_cap, slot_count)
            buffer = plain_dot(sender, pieces).astype(jnp.bfloat16)
            arrived_slots = lax.all_to_all(buffer, "blk", split_axis=0, concat_axis=0, tiled=True)
            partner_slots = partner_2(arrived_slots, "leaf", leaf_bit)
            every_row = jnp.ones(own_dest.shape, bool)
            own_rank = rank_pieces(own_dest, every_row)
            pair_rank = rank_pieces(pair_dest, every_row)
            own_take = receive_matrix(
                own_rank,
                own_place,
                (own_dest == owner_index) & (own_side == 0),
                slot_cap,
                place_count,
            )
            pair_take = receive_matrix(
                pair_rank,
                pair_place,
                (pair_dest == owner_index) & (pair_side == 1),
                slot_cap,
                place_count,
            )
            incoming = (
                plain_dot(own_take, arrived_slots) + plain_dot(pair_take, partner_slots)
            ).reshape(node_width, col_count)
            routes.append((sender, own_take, pair_take))
    solution = [None] * levels
    for level in reversed(range(levels)):
        if level + 1 == levels:
            back_side = forward[level]
        else:
            above_rows = solution[level + 1].reshape(place_count, flat_width)
            leaf_bit = level % leaf_bits
            sender, own_take, pair_take = routes[level]
            own_reply = trans_dot(own_take, above_rows)
            pair_reply = trans_dot(pair_take, above_rows).astype(jnp.bfloat16)
            handed = partner_2(pair_reply, "leaf", leaf_bit)
            merged = (own_reply + handed.astype(jnp.float32)).astype(jnp.bfloat16)
            returned = lax.all_to_all(merged, "blk", split_axis=0, concat_axis=0, tiled=True)
            gathered = trans_dot(sender, returned).astype(jnp.bfloat16)
            rows_in = gathered.reshape(piece_count * piece_rows, col_count)
            back_side = (
                forward[level].astype(jnp.float32) - trans_dot(coupling[level], rows_in)
            ).astype(jnp.bfloat16)
        masked = back_side * row_masks[level].astype(jnp.bfloat16)
        solution[level] = (row_masks[level] * trans_dot(inverse[level], masked)).astype(
            jnp.bfloat16
        )
    return jnp.stack(solution, axis=0)[None, None]


def solution(mesh):
    return jax.shard_map(
        shards,
        mesh=mesh,
        in_specs=(
            P("leaf", "blk", None, None, None),
            P("leaf", "blk", None, None, None),
            P("leaf", "blk", None, None, None),
            P("leaf", "blk", None),
            P(),
        ),
        out_specs=P("leaf", "blk", None, None, None),
        check_vma=False,
    )
```

profile of v0, /device:TPU:0, one launch (start us, length us, event | category | flops | bytes accessed | tf_op | source)
XLA Modules:
  0.0 118.0 jit_solution(18279386885978566561)
XLA Ops:
  0.0 0.8 fusion.177
  0.8 1.5 %fusion.178 = (s32[1,1,1]{2,1,0:T(1,128)}, s32[1,1,1]{2,1,0:T(1,128)}, s32[1,1,1]{2,1,0:T(1,128)}, s32[1,1,1]{2,1,0:T(1,128)}) fusion(s32[1,1,4]{2,1,0:T(1,128)} %param.8), kind=kLoop, calls=%fused_computation.314 | loop fusion | bytes 32 | tf_op jit(solution)/shard_map/slice | solution.py:75
  2.9 0.5 fusion.157
  3.4 1.3 %fusion.16 = bf16[512,32]{0,1:T(8,128)(2,1)S(1)} fusion(bf16[1,1,4,512,512]{4,3,2,1,0:T(8,128)(2,1)} %param.6, bf16[1,1,4,512,32]{3,4,2,1,0:T(8,128)(2,1)} %param.5, f32[512]{0:T(512)S(1)} %get-tuple-element.62), kind=kOutput, calls=%fused_computation.45 | convolution fusion | flops 16809984 | bytes 591872 | tf_op jit(solution)/shard_map/dot_general | solution.py:14
  4.7 1.1 fusion.29
  6.5 0.7 all_to_all.48
  7.1 7.4 %all-to-all-start = ((bf16[16,9,128]{2,1,0:T(8,128)(2,1)}), bf16[16,9,128]{2,1,0:T(8,128)(2,1)S(1)}, u32[]{:S(2)}, u32[]{:S(2)}) async-start(bf16[16,9,128]{2,1,0:T(8,128)(2,1)} %all_to_all.48), calls=%async_computation | async-start | bytes 131072 | tf_op jit(solution)/shard_map/all_to_all | solution.py:105
  14.5 0.8 slice_convert_fusion.2
  16.3 1.2 %convert_reduce_fusion = (s32[16,64]{1,0:T(8,128)S(1)}, s32[16,64]{1,0:T(8,128)S(1)}, s32[16,64]{1,0:T(8,128)S(1)}, s32[16,64]{1,0:T(8,128)S(1)}, s32[16,64]{1,0:T(8,128)S(1)}, /*index=5*/s32[16,64]{1,0:T(8,128)S(1)}) fusion(s32[16,64]{1,0:T(8,128)S(1)} %get-tuple-element.12, pred[64,64]{1,0:T(8,128)(4,1)S(1)} %iota_compare_fusion.27, ...), kind=kLoop, calls=%fused_computation.76 | loop fusion | flops 1566720 | bytes 53248 | tf_op jit(solution)/shard_map/reduce_sum | solution.py:34
  17.6 0.5 fusion.1
  18.9 0.5 fusion.3
  20.0 0.5 fusion.5
  21.1 0.6 fusion.165
  21.8 0.5 fusion.4
  22.2 0.5 fusion.2
  22.7 0.5 fusion
  23.1 0.6 all_to_all.50
  23.8 1.5 %collective-permute-start = (bf16[144,128]{1,0:T(8,128)(2,1)}, bf16[144,128]{1,0:T(8,128)(2,1)S(1)}, u32[]{:S(2)}, u32[]{:S(2)}) collective-permute-start(bf16[144,128]{1,0:T(8,128)(2,1)} %all_to_all.50), channel_id=1, source_target_pairs={{0,16},{16,0},{1,17},{17,1},{2,18},{18,2},{3,19},{19,3},{4,20},{20... | collective-permute-start | bytes 110600 | tf_op jit(solution)/shard_map/ppermute | solution.py:10
  25.3 0.2 convolution_bitcast_fusion.3
  25.5 2.5 %collective-permute-done = bf16[144,128]{1,0:T(8,128)(2,1)S(1)} collective-permute-done((bf16[144,128]{1,0:T(8,128)(2,1)}, bf16[144,128]{1,0:T(8,128)(2,1)S(1)}, u32[]{:S(2)}, u32[]{:S(2)}) %collective-permute-start) | collective-permute-done | bytes 36896 | tf_op jit(solution)/shard_map/ppermute | solution.py:10
  28.0 0.2 fusion.10
  28.3 0.2 fusion.11
  29.0 0.8 convolution_convert_fusion.10
  29.8 0.7 all_to_all.51
  30.5 6.0 %all-to-all-start.1 = ((bf16[16,9,128]{2,1,0:T(8,128)(2,1)}), bf16[16,9,128]{2,1,0:T(8,128)(2,1)S(1)}, u32[]{:S(2)}, u32[]{:S(2)}) async-start(bf16[16,9,128]{2,1,0:T(8,128)(2,1)} %all_to_all.51), calls=%async_computation.1 | async-start | bytes 131072 | tf_op jit(solution)/shard_map/all_to_all | solution.py:105
  36.5 0.6 fusion.159
  37.1 6.3 %all-to-all-done.1 = bf16[16,9,128]{2,1,0:T(8,128)(2,1)S(1)} async-done(((bf16[16,9,128]{2,1,0:T(8,128)(2,1)}), bf16[16,9,128]{2,1,0:T(8,128)(2,1)S(1)}, u32[]{:S(2)}, u32[]{:S(2)}) %all-to-all-start.1) | async-done | bytes 36896 | tf_op jit(solution)/shard_map/all_to_all | solution.py:105
  43.4 0.6 all_to_all.53
  44.0 1.5 %collective-permute-start.1 = (bf16[144,128]{1,0:T(8,128)(2,1)}, bf16[144,128]{1,0:T(8,128)(2,1)S(1)}, u32[]{:S(2)}, u32[]{:S(2)}) collective-permute-start(bf16[144,128]{1,0:T(8,128)(2,1)} %all_to_all.53), channel_id=1, source_target_pairs={{0,16},{16,0},{1,17},{17,1},{2,18},{18,2},{3,19},{19,3},{4,20},{20... | collective-permute-start | bytes 110600 | tf_op jit(solution)/shard_map/ppermute | solution.py:10
  45.5 0.2 convolution_bitcast_fusion.2
  45.7 2.5 %collective-permute-done.1 = bf16[144,128]{1,0:T(8,128)(2,1)S(1)} collective-permute-done((bf16[144,128]{1,0:T(8,128)(2,1)}, bf16[144,128]{1,0:T(8,128)(2,1)S(1)}, u32[]{:S(2)}, u32[]{:S(2)}) %collective-permute-start.1) | collective-permute-done | bytes 36896 | tf_op jit(solution)/shard_map/ppermute | solution.py:10
  48.2 0.2 fusion.12
  48.5 0.9 fusion.13
  49.9 0.7 convolution_convert_fusion.9
  50.6 0.7 all_to_all.54
  51.3 3.5 %all-to-all-start.2 = ((bf16[16,9,128]{2,1,0:T(8,128)(2,1)}), bf16[16,9,128]{2,1,0:T(8,128)(2,1)S(1)}, u32[]{:S(2)}, u32[]{:S(2)}) async-start(bf16[16,9,128]{2,1,0:T(8,128)(2,1)} %all_to_all.54), calls=%async_computation.2 | async-start | bytes 131072 | tf_op jit(solution)/shard_map/all_to_all | solution.py:105
  54.8 0.6 fusion.160
  55.4 6.3 %all-to-all-done.2 = bf16[16,9,128]{2,1,0:T(8,128)(2,1)S(1)} async-done(((bf16[16,9,128]{2,1,0:T(8,128)(2,1)}), bf16[16,9,128]{2,1,0:T(8,128)(2,1)S(1)}, u32[]{:S(2)}, u32[]{:S(2)}) %all-to-all-start.2) | async-done | bytes 36896 | tf_op jit(solution)/shard_map/all_to_all | solution.py:105
  61.7 0.6 all_to_all.56
  62.3 1.5 %collective-permute-start.2 = (bf16[144,128]{1,0:T(8,128)(2,1)}, bf16[144,128]{1,0:T(8,128)(2,1)S(1)}, u32[]{:S(2)}, u32[]{:S(2)}) collective-permute-start(bf16[144,128]{1,0:T(8,128)(2,1)} %all_to_all.56), channel_id=1, source_target_pairs={{0,16},{16,0},{1,17},{17,1},{2,18},{18,2},{3,19},{19,3},{4,20},{20... | collective-permute-start | bytes 110600 | tf_op jit(solution)/shard_map/ppermute | solution.py:10
  63.8 0.2 convolution_bitcast_fusion.1
  64.0 2.5 %collective-permute-done.2 = bf16[144,128]{1,0:T(8,128)(2,1)S(1)} collective-permute-done((bf16[144,128]{1,0:T(8,128)(2,1)}, bf16[144,128]{1,0:T(8,128)(2,1)S(1)}, u32[]{:S(2)}, u32[]{:S(2)}) %collective-permute-start.2) | collective-permute-done | bytes 36896 | tf_op jit(solution)/shard_map/ppermute | solution.py:10
  66.5 0.2 fusion.14
  66.8 1.2 fusion.17
  68.4 1.6 %collective-permute-start.3 = (bf16[144,128]{1,0:T(8,128)(2,1)S(1)}, bf16[144,128]{1,0:T(8,128)(2,1)S(1)}, u32[]{:S(2)}, u32[]{:S(2)}) collective-permute-start(bf16[144,128]{1,0:T(8,128)(2,1)S(1)} %convolution_convert_fusion.8), channel_id=1, source_target_pairs={{0,16},{16,0},{1,17},{17,1},{2,18},{18,2},{3,19},{19,3},{4,20},{20... | collective-permute-start | bytes 110600 | tf_op jit(solution)/shard_map/ppermute | solution.py:10
  70.0 2.4 %collective-permute-done.3 = bf16[144,128]{1,0:T(8,128)(2,1)S(1)} collective-permute-done((bf16[144,128]{1,0:T(8,128)(2,1)S(1)}, bf16[144,128]{1,0:T(8,128)(2,1)S(1)}, u32[]{:S(2)}, u32[]{:S(2)}) %collective-permute-start.3) | collective-permute-done | bytes 36896 | tf_op jit(solution)/shard_map/ppermute | solution.py:10
  72.6 0.7 all_to_all.57
  73.2 3.5 %all-to-all-start.3 = ((bf16[16,9,128]{2,1,0:T(8,128)(2,1)}), bf16[16,9,128]{2,1,0:T(8,128)(2,1)S(1)}, u32[]{:S(2)}, u32[]{:S(2)}) async-start(bf16[16,9,128]{2,1,0:T(8,128)(2,1)} %all_to_all.57), calls=%async_computation.3 | async-start | bytes 131072 | tf_op jit(solution)/shard_map/all_to_all | solution.py:140
  76.7 6.8 %all-to-all-done.3 = bf16[16,9,128]{2,1,0:T(8,128)(2,1)S(1)} async-done(((bf16[16,9,128]{2,1,0:T(8,128)(2,1)}), bf16[16,9,128]{2,1,0:T(8,128)(2,1)S(1)}, u32[]{:S(2)}, u32[]{:S(2)}) %all-to-all-start.3) | async-done | bytes 36896 | tf_op jit(solution)/shard_map/all_to_all | solution.py:140
  83.6 0.8 convolution_convert_fusion.14
  84.6 1.0 fusion.19
  86.0 1.6 %collective-permute-start.4 = (bf16[144,128]{1,0:T(8,128)(2,1)S(1)}, bf16[144,128]{1,0:T(8,128)(2,1)S(1)}, u32[]{:S(2)}, u32[]{:S(2)}) collective-permute-start(bf16[144,128]{1,0:T(8,128)(2,1)S(1)} %convolution_convert_fusion.7), channel_id=1, source_target_pairs={{0,16},{16,0},{1,17},{17,1},{2,18},{18,2},{3,19},{19,3},{4,20},{20... | collective-permute-start | bytes 110600 | tf_op jit(solution)/shard_map/ppermute | solution.py:10
  87.6 2.4 %collective-permute-done.4 = bf16[144,128]{1,0:T(8,128)(2,1)S(1)} collective-permute-done((bf16[144,128]{1,0:T(8,128)(2,1)S(1)}, bf16[144,128]{1,0:T(8,128)(2,1)S(1)}, u32[]{:S(2)}, u32[]{:S(2)}) %collective-permute-start.4) | collective-permute-done | bytes 36896 | tf_op jit(solution)/shard_map/ppermute | solution.py:10
  90.1 0.7 all_to_all.60
  90.8 3.5 %all-to-all-start.4 = ((bf16[16,9,128]{2,1,0:T(8,128)(2,1)}), bf16[16,9,128]{2,1,0:T(8,128)(2,1)S(1)}, u32[]{:S(2)}, u32[]{:S(2)}) async-start(bf16[16,9,128]{2,1,0:T(8,128)(2,1)} %all_to_all.60), calls=%async_computation.4 | async-start | bytes 131072 | tf_op jit(solution)/shard_map/all_to_all | solution.py:140
  94.3 6.8 %all-to-all-done.4 = bf16[16,9,128]{2,1,0:T(8,128)(2,1)S(1)} async-done(((bf16[16,9,128]{2,1,0:T(8,128)(2,1)}), bf16[16,9,128]{2,1,0:T(8,128)(2,1)S(1)}, u32[]{:S(2)}, u32[]{:S(2)}) %all-to-all-start.4) | async-done | bytes 36896 | tf_op jit(solution)/shard_map/all_to_all | solution.py:140
  101.2 0.9 convolution_convert_fusion.13
  102.2 0.3 fusion.21
  102.9 1.6 %collective-permute-start.5 = (bf16[144,128]{1,0:T(8,128)(2,1)S(1)}, bf16[144,128]{1,0:T(8,128)(2,1)S(1)}, u32[]{:S(2)}, u32[]{:S(2)}) collective-permute-start(bf16[144,128]{1,0:T(8,128)(2,1)S(1)} %convolution_convert_fusion.6), channel_id=1, source_target_pairs={{0,16},{16,0},{1,17},{17,1},{2,18},{18,2},{3,19},{19,3},{4,20},{20... | collective-permute-start | bytes 110600 | tf_op jit(solution)/shard_map/ppermute | solution.py:10
  104.6 2.4 %collective-permute-done.5 = bf16[144,128]{1,0:T(8,128)(2,1)S(1)} collective-permute-done((bf16[144,128]{1,0:T(8,128)(2,1)S(1)}, bf16[144,128]{1,0:T(8,128)(2,1)S(1)}, u32[]{:S(2)}, u32[]{:S(2)}) %collective-permute-start.5) | collective-permute-done | bytes 36896 | tf_op jit(solution)/shard_map/ppermute | solution.py:10
  107.2 9.5 %all_to_all.72 = bf16[16,9,128]{2,1,0:T(8,128)(2,1)S(1)} all-to-all(bf16[16,9,128]{2,1,0:T(8,128)(2,1)S(1)} %all_to_all.63), channel_id=1, replica_groups=mesh['leaf'=2,'blk'=16] {'blk'}, dimensions={0} | all-to-all | bytes 73728 | tf_op jit(solution)/shard_map/all_to_all | solution.py:140
  116.7 0.2 convolution_convert_fusion.12
  117.0 0.3 fusion.26
  117.3 0.7 maximum_bitcast_fusion
  (77 shorter events, 5.2 us)
Async XLA Ops:
  3.4 1.3 %copy-start.2 = (f32[512]{0:T(512)}, f32[512]{0:T(512)S(1)}, u32[]{:S(2)}) copy-start(f32[512]{0:T(512)S(1)} %get-tuple-element.62) | copy-start | bytes 6148
  6.3 9.8 %copy-start.4 = (s32[64]{0:T(128)}, s32[64]{0:T(128)S(1)}, u32[]{:S(2)}) copy-start(s32[64]{0:T(128)S(1)} %fusion.167) | copy-start | bytes 772
  7.1 16.0 %all-to-all-start = ((bf16[16,9,128]{2,1,0:T(8,128)(2,1)}), bf16[16,9,128]{2,1,0:T(8,128)(2,1)S(1)}, u32[]{:S(2)}, u32[]{:S(2)}) async-start(bf16[16,9,128]{2,1,0:T(8,128)(2,1)} %all_to_all.48), calls=%async_computation | async-start | bytes 131072 | tf_op jit(solution)/shard_map/all_to_all | solution.py:105
  16.1 12.2 %copy-start = (bf16[1,1,4,512,512]{4,3,2,1,0:T(8,128)(2,1)S(1)}, bf16[1,1,4,512,512]{4,3,2,1,0:T(8,128)(2,1)}, u32[]{:S(2)}) copy-start(bf16[1,1,4,512,512]{4,3,2,1,0:T(8,128)(2,1)} %param.6) | copy-start | bytes 6291460
  18.0 10.5 %copy-start.1 = (bf16[1,1,3,256,512]{4,3,2,1,0:T(8,128)(2,1)S(1)}, bf16[1,1,3,256,512]{4,3,2,1,0:T(8,128)(2,1)}, u32[]{:S(2)}) copy-start(bf16[1,1,3,256,512]{4,3,2,1,0:T(8,128)(2,1)} %param.7) | copy-start | bytes 2359300
  23.8 4.2 %collective-permute-start = (bf16[144,128]{1,0:T(8,128)(2,1)}, bf16[144,128]{1,0:T(8,128)(2,1)S(1)}, u32[]{:S(2)}, u32[]{:S(2)}) collective-permute-start(bf16[144,128]{1,0:T(8,128)(2,1)} %all_to_all.50), channel_id=1, source_target_pairs={{0,16},{16,0},{1,17},{17,1},{2,18},{18,2},{3,19},{19,3},{4,20},{20... | collective-permute-start | bytes 110600 | tf_op jit(solution)/shard_map/ppermute | solution.py:10
  30.5 12.9 %all-to-all-start.1 = ((bf16[16,9,128]{2,1,0:T(8,128)(2,1)}), bf16[16,9,128]{2,1,0:T(8,128)(2,1)S(1)}, u32[]{:S(2)}, u32[]{:S(2)}) async-start(bf16[16,9,128]{2,1,0:T(8,128)(2,1)} %all_to_all.51), calls=%async_computation.1 | async-start | bytes 131072 | tf_op jit(solution)/shard_map/all_to_all | solution.py:105
  44.0 4.2 %collective-permute-start.1 = (bf16[144,128]{1,0:T(8,128)(2,1)}, bf16[144,128]{1,0:T(8,128)(2,1)S(1)}, u32[]{:S(2)}, u32[]{:S(2)}) collective-permute-start(bf16[144,128]{1,0:T(8,128)(2,1)} %all_to_all.53), channel_id=1, source_target_pairs={{0,16},{16,0},{1,17},{17,1},{2,18},{18,2},{3,19},{19,3},{4,20},{20... | collective-permute-start | bytes 110600 | tf_op jit(solution)/shard_map/ppermute | solution.py:10
  51.3 10.4 %all-to-all-start.2 = ((bf16[16,9,128]{2,1,0:T(8,128)(2,1)}), bf16[16,9,128]{2,1,0:T(8,128)(2,1)S(1)}, u32[]{:S(2)}, u32[]{:S(2)}) async-start(bf16[16,9,128]{2,1,0:T(8,128)(2,1)} %all_to_all.54), calls=%async_computation.2 | async-start | bytes 131072 | tf_op jit(solution)/shard_map/all_to_all | solution.py:105
  62.3 4.2 %collective-permute-start.2 = (bf16[144,128]{1,0:T(8,128)(2,1)}, bf16[144,128]{1,0:T(8,128)(2,1)S(1)}, u32[]{:S(2)}, u32[]{:S(2)}) collective-permute-start(bf16[144,128]{1,0:T(8,128)(2,1)} %all_to_all.56), channel_id=1, source_target_pairs={{0,16},{16,0},{1,17},{17,1},{2,18},{18,2},{3,19},{19,3},{4,20},{20... | collective-permute-start | bytes 110600 | tf_op jit(solution)/shard_map/ppermute | solution.py:10
  68.4 4.0 %collective-permute-start.3 = (bf16[144,128]{1,0:T(8,128)(2,1)S(1)}, bf16[144,128]{1,0:T(8,128)(2,1)S(1)}, u32[]{:S(2)}, u32[]{:S(2)}) collective-permute-start(bf16[144,128]{1,0:T(8,128)(2,1)S(1)} %convolution_convert_fusion.8), channel_id=1, source_target_pairs={{0,16},{16,0},{1,17},{17,1},{2,18},{18,2},{3,19},{19,3},{4,20},{20... | collective-permute-start | bytes 110600 | tf_op jit(solution)/shard_map/ppermute | solution.py:10
  73.2 10.4 %all-to-all-start.3 = ((bf16[16,9,128]{2,1,0:T(8,128)(2,1)}), bf16[16,9,128]{2,1,0:T(8,128)(2,1)S(1)}, u32[]{:S(2)}, u32[]{:S(2)}) async-start(bf16[16,9,128]{2,1,0:T(8,128)(2,1)} %all_to_all.57), calls=%async_computation.3 | async-start | bytes 131072 | tf_op jit(solution)/shard_map/all_to_all | solution.py:140
  83.6 33.0 %copy-start.5 = (s32[64]{0:T(128)S(1)}, s32[64]{0:T(128)}, u32[]{:S(2)}) copy-start(s32[64]{0:T(128)} %copy-done.4) | copy-start | bytes 772
  84.4 32.5 %copy-start.3 = (f32[512]{0:T(512)S(1)}, f32[512]{0:T(512)}, u32[]{:S(2)}) copy-start(f32[512]{0:T(512)} %copy-done.2) | copy-start | bytes 6148
  84.5 32.5 %copy-start.6 = (bf16[512]{0:T(512)(128)(2,1)S(1)}, bf16[512]{0:T(512)(128)(2,1)}, u32[]{:S(2)}) copy-start(bf16[512]{0:T(512)(128)(2,1)} %get-tuple-element.63) | copy-start | bytes 3076
  86.0 4.0 %collective-permute-start.4 = (bf16[144,128]{1,0:T(8,128)(2,1)S(1)}, bf16[144,128]{1,0:T(8,128)(2,1)S(1)}, u32[]{:S(2)}, u32[]{:S(2)}) collective-permute-start(bf16[144,128]{1,0:T(8,128)(2,1)S(1)} %convolution_convert_fusion.7), channel_id=1, source_target_pairs={{0,16},{16,0},{1,17},{17,1},{2,18},{18,2},{3,19},{19,3},{4,20},{20... | collective-permute-start | bytes 110600 | tf_op jit(solution)/shard_map/ppermute | solution.py:10
  90.8 10.4 %all-to-all-start.4 = ((bf16[16,9,128]{2,1,0:T(8,128)(2,1)}), bf16[16,9,128]{2,1,0:T(8,128)(2,1)S(1)}, u32[]{:S(2)}, u32[]{:S(2)}) async-start(bf16[16,9,128]{2,1,0:T(8,128)(2,1)} %all_to_all.60), calls=%async_computation.4 | async-start | bytes 131072 | tf_op jit(solution)/shard_map/all_to_all | solution.py:140
  102.9 4.0 %collective-permute-start.5 = (bf16[144,128]{1,0:T(8,128)(2,1)S(1)}, bf16[144,128]{1,0:T(8,128)(2,1)S(1)}, u32[]{:S(2)}, u32[]{:S(2)}) collective-permute-start(bf16[144,128]{1,0:T(8,128)(2,1)S(1)} %convolution_convert_fusion.6), channel_id=1, source_target_pairs={{0,16},{16,0},{1,17},{17,1},{2,18},{18,2},{3,19},{19,3},{4,20},{20... | collective-permute-start | bytes 110600 | tf_op jit(solution)/shard_map/ppermute | solution.py:10
where the time goes:
time: 119 us; the launch traced here: 118 us
  waiting for transfers between devices  40.9 us (34%)
  starting transfers between devices  33.2 us (28%)
  matrix products  15.1 us (13%)
  local copies, waits for them, and re-layouts  10.7 us (9%)
  blocking collectives  9.48 us (8%)
  other arithmetic  5.58 us (5%)
  between operations  3.14 us (3%)
    all_to_all x3, starting transfers between devices, shards(): lax.all_to_all(buffer, 'blk', split_axis=0, concat_axis=0, tiled=True)  16.9 us
    ppermute x6, waiting for transfers between devices, partner_2(): lax.ppermute(array, axis, [(i, i ^ 1 << distance) for i in range(lax.axis...  14.6 us
    all_to_all x2, waiting for transfers between devices, shards(): lax.all_to_all(merged, 'blk', split_axis=0, concat_axis=0, tiled=True)  13.7 us
    all_to_all x3, waiting for transfers between devices, shards(): lax.all_to_all(buffer, 'blk', split_axis=0, concat_axis=0, tiled=True)  12.6 us
    all_to_all x1, blocking collectives, shards(): lax.all_to_all(merged, 'blk', split_axis=0, concat_axis=0, tiled=True)  9.48 us
    ppermute x6, starting transfers between devices, partner_2(): lax.ppermute(array, axis, [(i, i ^ 1 << distance) for i in range(lax.axis...  9.31 us
    all_to_all x2, starting transfers between devices, shards(): lax.all_to_all(merged, 'blk', split_axis=0, concat_axis=0, tiled=True)  7.01 us
    dot_general x15, matrix products, plain_dot(): return jnp.dot(left, right, preferred_element_type=jnp.float32)  6.8 us
  transfers between devices with their start and end apart: 11, of which 10 were waited for; matrix products, arithmetic and copies ran while one was open for 7% of the time, Pallas kernels for 0%

commit v1 on v0

v1 whole, which is shorter than its diff:
```python
import functools

import jax
import jax.numpy as jnp
from jax import lax
from jax.experimental import pallas as pl
from jax.experimental.pallas import tpu as pltpu
from jax.sharding import Mesh, PartitionSpec as P

BLOCK = 128
MESSAGE = 16
LANES = 128
F32 = jnp.float32
BF16 = jnp.bfloat16


def iota(shape, axis):
    return lax.broadcasted_iota(jnp.int32, shape, axis)


def ones_where(condition):
    return jnp.where(condition, 1.0, 0.0).astype(BF16)


def dot(left, right):
    return jnp.dot(left, right, preferred_element_type=F32)


def trans_dot(left, right):
    return lax.dot_general(left, right, (((0,), (0,)), ((), ())), preferred_element_type=F32)


class Sizes:
    def __init__(self, right_sides, couplings, targets, groups, owners):
        self.levels, self.width, self.columns = right_sides.shape[-3:]
        self.rows = couplings.shape[-2]
        self.pieces = targets.shape[-1]
        self.groups, self.owners = groups, owners
        self.leaf_bits = groups.bit_length() - 1
        self.sub = self.rows // self.pieces
        self.places = self.width // self.sub
        self.slots = 2 * owners * MESSAGE
        self.cap = max(3, (2 * self.pieces + owners - 1) // owners + 1)


def live(widths, level, shape, axis):
    return iota(shape, axis) < widths[0, 0, level] * BLOCK


def own_lanes(sizes, rows):
    shape = (rows, LANES)
    return iota(shape, 1) // sizes.columns == iota(shape, 0) % sizes.sub


def keep_own(sizes, value):
    return jnp.where(own_lanes(sizes, value.shape[0]), value, jnp.zeros_like(value))


def spread(sizes, value):
    value = keep_own(sizes, value)
    step = sizes.columns
    while step < LANES:
        value = value + pltpu.roll(value, step, 1)
        step *= 2
    return value


def repeat_columns(sizes, value):
    return jnp.concatenate([value] * (LANES // sizes.columns), axis=1)


def position(sizes, level, where):
    group, owner = where[0], where[1]
    bit = level % sizes.leaf_bits
    return group, owner, bit


def send_slots(sizes, level, where, targets):
    group, owner, bit = position(sizes, level, where)
    count = sizes.pieces
    table = targets[level, group]
    mine = jnp.sum(jnp.where(iota(table.shape, 0) == owner, table, 0), axis=0, keepdims=True)
    key_row = mine // sizes.places
    square = (count, count)
    diagonal = iota(square, 0) == iota(square, 1)
    keys_down = jnp.broadcast_to(key_row, square)
    key_col = jnp.sum(jnp.where(diagonal, keys_down, 0).astype(F32), axis=1, keepdims=True).astype(jnp.int32)
    same = keys_down == key_col
    rank_row = jnp.sum(jnp.where(same & (iota(square, 0) < iota(square, 1)), 1.0, 0.0), axis=0, keepdims=True)
    rank_col = jnp.sum(jnp.where(same & (iota(square, 1) < iota(square, 0)), 1.0, 0.0), axis=1, keepdims=True)

    def slot(key, rank):
        side, dest = key // sizes.owners, key % sizes.owners
        half = jnp.bitwise_xor(side, lax.shift_right_logical(group, bit) & 1)
        return (half * sizes.owners + dest) * MESSAGE + rank.astype(jnp.int32)

    return slot(key_row, rank_row), slot(key_col, rank_col)


def send_rows(sizes, level, where, targets):
    _, slot_col = send_slots(sizes, level, where, targets)
    shape = (sizes.pieces, sizes.rows)
    chosen = iota(shape, 1) // sizes.sub == iota(shape, 0)
    wide = jnp.sum(jnp.where(chosen, slot_col, 0).astype(F32), axis=0, keepdims=True).astype(jnp.int32)
    return ones_where(iota((sizes.slots, sizes.rows), 0) == wide)


def send_columns(sizes, level, where, targets):
    slot_row, _ = send_slots(sizes, level, where, targets)
    shape = (sizes.rows, sizes.pieces)
    chosen = iota(shape, 0) // sizes.sub == iota(shape, 1)
    wide = jnp.sum(jnp.where(chosen, slot_row, 0).astype(F32), axis=1, keepdims=True).astype(jnp.int32)
    return ones_where(iota((sizes.rows, sizes.slots), 1) == wide)


def take_table(sizes, level, where, targets):
    group, owner, bit = position(sizes, level, where)
    own_half = lax.shift_right_logical(group, bit) & 1
    first = group - own_half * 2**bit
    tables = []
    for half in range(2):
        codes = targets[level, first + half * 2**bit]
        wanted = jnp.bitwise_xor(own_half, half) * sizes.owners + owner
        tables.append(jnp.where(codes // sizes.places == wanted, codes % sizes.places + 1, 0))
    place = jnp.concatenate(tables, axis=0).astype(F32)
    square = (sizes.pieces, sizes.pieces)
    earlier = ones_where(iota(square, 0) < iota(square, 1))
    rank = dot(ones_where(place > 0), earlier)
    return place, rank


def take_rows(sizes, level, where, targets):
    place, rank = take_table(sizes, level, where, targets)
    shape = (2 * sizes.owners, sizes.slots)
    offset = iota(shape, 1) - iota(shape, 0) * MESSAGE
    spot = jnp.zeros(shape, F32)
    for each in range(sizes.cap):
        held = jnp.sum(jnp.where(rank == each, place, 0.0), axis=1, keepdims=True)
        spot = jnp.where(offset == each, held, spot)
    spot = jnp.sum(spot, axis=0, keepdims=True).astype(jnp.int32)
    return ones_where(iota((sizes.width, sizes.slots), 0) // sizes.sub + 1 == spot)


def take_columns(sizes, level, where, targets):
    place, rank = take_table(sizes, level, where, targets)
    shape = (sizes.slots, 2 * sizes.owners)
    source = ones_where(iota(shape, 0) // MESSAGE == iota(shape, 1))
    places = dot(source, place.astype(BF16))
    ranks = dot(source, rank.astype(BF16))
    wanted = (iota(places.shape, 0) % MESSAGE).astype(F32)
    spot = jnp.sum(jnp.where(ranks == wanted, places, 0.0), axis=1, keepdims=True).astype(jnp.int32)
    return ones_where(iota((sizes.slots, sizes.width), 1) // sizes.sub + 1 == spot)


def coupled_inverse(sizes, level, widths, inverse, coupling):
    kept = jnp.where(live(widths, level, coupling.shape, 1), coupling, jnp.zeros_like(coupling))
    return dot(kept, inverse).astype(BF16)


def solve_forward(sizes, level, widths, inverse, residual):
    product = dot(inverse, residual)
    return jnp.where(live(widths, level, product.shape, 0), product, 0.0).astype(BF16)


def solve_backward(sizes, level, widths, inverse, side):
    product = trans_dot(inverse, side)
    return jnp.where(live(widths, level, product.shape, 0), product, 0.0)


def start_kernel(sizes, where, widths, right, inverse, coupling, targets, buffer, forward):
    residual = repeat_columns(sizes, right[0, 0, 0])
    solved = solve_forward(sizes, 0, widths, inverse[0, 0, 0], residual)
    pieces = keep_own(sizes, dot(coupling[0, 0, 0], solved).astype(BF16))
    buffer[...] = dot(send_rows(sizes, 0, where, targets), pieces).astype(BF16)
    forward[...] = solved


def up_plan_kernel(sizes, level, where, widths, right, inverse, coupling, targets, after, side, product, sender, taker):
    side[...] = repeat_columns(sizes, right[0, 0, 0])
    product[...] = coupled_inverse(sizes, level, widths, inverse[0, 0, 0], coupling[0, 0, 0])
    sender[...] = send_rows(sizes, level, where, targets)
    taker[...] = take_rows(sizes, level - 1, where, targets)


def up_kernel(sizes, arrived, side, product, sender, taker, buffer, residual):
    incoming = spread(sizes, dot(taker[...], arrived[...]))
    left = (side[...].astype(F32) - incoming).astype(BF16)
    residual[...] = left
    pieces = keep_own(sizes, dot(product[...], left).astype(BF16))
    buffer[...] = dot(sender[...], pieces).astype(BF16)


def top_plan_kernel(sizes, level, where, widths, right, inverse, targets, after, side, product, taker, returner):
    side[...] = repeat_columns(sizes, right[0, 0, 0])
    block = inverse[0, 0, 0]
    kept = jnp.where(live(widths, level, block.shape, 0), block, jnp.zeros_like(block))
    full = trans_dot(block, kept)
    product[...] = jnp.where(live(widths, level, full.shape, 0), full, 0.0).astype(BF16)
    taker[...] = take_rows(sizes, level - 1, where, targets)
    returner[...] = take_columns(sizes, level - 1, where, targets)


def top_kernel(sizes, arrived, side, product, taker, returner, buffer, solved):
    incoming = spread(sizes, dot(taker[...], arrived[...]))
    left = (side[...].astype(F32) - incoming).astype(BF16)
    value = dot(product[...], left).astype(BF16)
    buffer[...] = dot(returner[...], keep_own(sizes, value)).astype(BF16)
    solved[...] = value


def down_plan_kernel(sizes, level, where, widths, inverse, coupling, targets, state, after, side, product, picker, *returner):
    block = inverse[0, 0, 0]
    forward = state[...]
    if level > 0:
        forward = solve_forward(sizes, level, widths, block, forward)
    side[...] = solve_backward(sizes, level, widths, block, forward)
    full = coupled_inverse(sizes, level, widths, block, coupling[0, 0, 0]).T
    product[...] = jnp.where(live(widths, level, full.shape, 0), full, jnp.zeros_like(full))
    picker[...] = send_columns(sizes, level, where, targets)
    if level > 0:
        returner[0][...] = take_columns(sizes, level - 1, where, targets)


def down_kernel(sizes, arrived, side, product, picker, returner, buffer, solved):
    gathered = spread(sizes, dot(picker[...], arrived[...])).astype(BF16)
    value = (side[...] - dot(product[...], gathered)).astype(BF16)
    buffer[...] = dot(returner[...], keep_own(sizes, value)).astype(BF16)
    solved[...] = value


def last_kernel(sizes, arrived, side, product, picker, first, second, third, out):
    gathered = spread(sizes, dot(picker[...], arrived[...])).astype(BF16)
    value = (side[...] - dot(product[...], gathered)).astype(BF16)
    out[0, 0, 0] = value[:, : sizes.columns]
    for level, solved in enumerate((first, second, third)):
        out[0, 0, level + 1] = solved[:, : sizes.columns]


def level_spec(array, level):
    return pl.BlockSpec((1, 1, 1) + array.shape[3:], lambda step: (0, 0, level, 0, 0))


def whole_spec(shape):
    return pl.BlockSpec(shape, lambda step: (0,) * len(shape))


SCALARS = pl.BlockSpec(memory_space=pltpu.SMEM)
ANYWHERE = pl.BlockSpec(memory_space=pl.ANY)


def call(kernel, name, operands, specs, outs, cost):
    return pl.pallas_call(
        kernel,
        grid=(1,),
        in_specs=[whole_spec(one.shape) if spec is None else spec for one, spec in zip(operands, specs)],
        out_specs=[whole_spec(shape) for shape, _ in outs],
        out_shape=[jax.ShapeDtypeStruct(shape, kind) for shape, kind in outs],
        compiler_params=pltpu.CompilerParams(vmem_limit_bytes=24 * 2**20),
        cost_estimate=pl.CostEstimate(flops=cost, bytes_accessed=2**20, transcendentals=0),
        name=name,
    )(*operands)


def shards(leaf_axes, right_sides, inverses, couplings, widths, targets):
    groups = 1
    group = 0
    for axis in leaf_axes:
        groups *= lax.axis_size(axis)
        group = group * lax.axis_size(axis) + lax.axis_index(axis)
    sizes = Sizes(right_sides, couplings, targets, groups, lax.axis_size("blk"))
    where = jnp.stack([group, lax.axis_index("blk")]).astype(jnp.int32)
    width, slots, rows = sizes.width, sizes.slots, sizes.rows
    top = sizes.levels - 1
    vector = ((width, LANES), BF16)
    message = ((slots, LANES), BF16)
    small, large = 10**6, 10**9

    def exchange(buffer, level):
        pair = leaf_axes[len(leaf_axes) - 1 - level % sizes.leaf_bits]
        blocks = buffer.reshape(2 * sizes.owners, MESSAGE, LANES)
        moved = lax.all_to_all(blocks, (pair, "blk"), split_axis=0, concat_axis=0, tiled=True)
        return moved.reshape(slots, LANES)

    buffer, state = call(
        functools.partial(start_kernel, sizes),
        "start",
        (where, widths, right_sides, inverses, couplings, targets),
        (SCALARS, SCALARS, level_spec(right_sides, 0), level_spec(inverses, 0), level_spec(couplings, 0), None),
        (message, vector),
        large,
    )
    states = [state]
    for level in range(1, top):
        plan = call(
            functools.partial(up_plan_kernel, sizes, level),
            f"up_plan_{level}",
            (where, widths, right_sides, inverses, couplings, targets, buffer),
            (
                SCALARS,
                SCALARS,
                level_spec(right_sides, level),
                level_spec(inverses, level),
                level_spec(couplings, level),
                None,
                ANYWHERE,
            ),
            (vector, ((rows, width), BF16), ((slots, rows), BF16), ((width, slots), BF16)),
            large,
        )
        arrived = exchange(buffer, level - 1)
        buffer, state = call(
            functools.partial(up_kernel, sizes),
            f"up_{level}",
            (arrived, *plan),
            (None,) * 5,
            (message, vector),
            small,
        )
        states.append(state)
    plan = call(
        functools.partial(top_plan_kernel, sizes, top),
        "top_plan",
        (where, widths, right_sides, inverses, targets, buffer),
        (SCALARS, SCALARS, level_spec(right_sides, top), level_spec(inverses, top), None, ANYWHERE),
        (vector, ((width, width), BF16), ((width, slots), BF16), ((slots, width), BF16)),
        large,
    )
    arrived = exchange(buffer, top - 1)
    buffer, solved = call(
        functools.partial(top_kernel, sizes),
        "top",
        (arrived, *plan),
        (None,) * 5,
        (message, vector),
        small,
    )
    solution = [solved]
    for level in reversed(range(top)):
        back = (((slots, width), BF16),) if level else ()
        plan = call(
            functools.partial(down_plan_kernel, sizes, level),
            f"down_plan_{level}",
            (where, widths, inverses, couplings, targets, states[level], buffer),
            (SCALARS, SCALARS, level_spec(inverses, level), level_spec(couplings, level), None, None, ANYWHERE),
            (((width, LANES), F32), ((width, rows), BF16), ((rows, slots), BF16), *back),
            large,
        )
        arrived = exchange(buffer, level)
        if level:
            buffer, solved = call(
                functools.partial(down_kernel, sizes),
                f"down_{level}",
                (arrived, *plan),
                (None,) * 5,
                (message, vector),
                small,
            )
            solution.insert(0, solved)
    (out,) = call(
        functools.partial(last_kernel, sizes),
        "last",
        (arrived, *plan, *solution),
        (None,) * (4 + len(solution)),
        ((right_sides.shape, BF16),),
        small,
    )
    return out


def solution(mesh):
    groups, owners = mesh.devices.shape
    bits = groups.bit_length() - 1
    leaf_axes = tuple(f"leaf{bit}" for bit in reversed(range(bits)))
    split = Mesh(mesh.devices.reshape((2,) * bits + (owners,)), leaf_axes + ("blk",))
    return jax.shard_map(
        functools.partial(shards, leaf_axes),
        mesh=split,
        in_specs=(
            P(leaf_axes, "blk", None, None, None),
            P(leaf_axes, "blk", None, None, None),
            P(leaf_axes, "blk", None, None, None),
            P(leaf_axes, "blk", None),
            P(),
        ),
        out_specs=P(leaf_axes, "blk", None, None, None),
        check_vma=False,
    )
```

time: 119 us -> 87.6 us (0.74)
  Pallas kernels: 0 us -> 19.4 us
  matrix products: 15.1 us -> 0 us
  starting transfers between devices: 33.2 us -> 20.2 us
  waiting for transfers between devices: 40.9 us -> 31.3 us
  blocking collectives: 9.48 us -> 0 us
  other arithmetic: 5.58 us -> 0.08 us
  local copies, waits for them, and re-layouts: 10.7 us -> 15.7 us
  between operations: 3.14 us -> 0.21 us
    pallas_call x0 -> x13, Pallas kernels: none -> 19.4 us  [call(): pl.pallas_call(kernel, grid=(1,), in_specs=[whole_spec(one.shape) if spec...]
    dot_general x34 -> x0, matrix products: 15.1 us -> none  [the longest x15 6.8 us: plain_dot(): return jnp.dot(left, right, preferred_element_type=jnp.float32)]
    unnamed x14 -> x31, local copies, waits for them, and re-layouts: 0.03 us -> 14.9 us
    ppermute x6 -> x0, waiting for transfers between devices: 14.6 us -> none  [partner_2(): lax.ppermute(array, axis, [(i, i ^ 1 << distance) for i in range(lax.axis...]
    all_to_all x1 -> x0, blocking collectives: 9.48 us -> none  [shards(): lax.all_to_all(merged, 'blk', split_axis=0, concat_axis=0, tiled=True)]
    ppermute x6 -> x0, starting transfers between devices: 9.31 us -> none  [partner_2(): lax.ppermute(array, axis, [(i, i ^ 1 << distance) for i in range(lax.axis...]
    all_to_all x12 -> x0, local copies, waits for them, and re-layouts: 5.35 us -> none  [the longest x6 3.9 us: shards(): lax.all_to_all(buffer, 'blk', split_axis=0, concat_axis=0, tiled=True)]
    all_to_all x5 -> x6, waiting for transfers between devices: 26.3 us -> 31.3 us  [exchange(): lax.all_to_all(blocks, (pair, 'blk'), split_axis=0, concat_axis=0, tiled=...]
  transfers between devices with their start and end apart: 11 -> 6, of which waited for: 10 -> 6; matrix products, arithmetic and copies ran while one was open for 7% -> 0% of each run, Pallas kernels for 0% -> 10%
where the time goes in v1:
time: 87.6 us; the launch traced here: 86.8 us
  waiting for transfers between devices  31.3 us (36%)
  starting transfers between devices  20.2 us (23%)
  Pallas kernels  19.4 us (22%)
  local copies, waits for them, and re-layouts  15.7 us (18%)
    all_to_all x6, waiting for transfers between devices, exchange(): lax.all_to_all(blocks, (pair, 'blk'), split_axis=0, concat_axis=0, tiled=...  31.3 us
    all_to_all x6, starting transfers between devices, exchange(): lax.all_to_all(blocks, (pair, 'blk'), split_axis=0, concat_axis=0, tiled=...  20.2 us
    pallas_call x13, Pallas kernels, call(): pl.pallas_call(kernel, grid=(1,), in_specs=[whole_spec(one.shape) if spec...  19.4 us
    unnamed x31, local copies, waits for them, and re-layouts  14.9 us
  transfers between devices with their start and end apart: 6, of which 6 were waited for; matrix products, arithmetic and copies ran while one was open for 0% of the time, Pallas kernels for 10%

profile of v1, /device:TPU:0, one launch (start us, length us, event | category | flops | bytes accessed | tf_op | source)
XLA Modules:
  0.0 86.8 jit_solution(10376095575264329025)
XLA Ops:
  0.0 1.2 %copy.6.right = bf16[1,1,4,512,32]{4,3,2,1,0:T(8,128)(2,1)S(1)} copy(bf16[1,1,4,512,32]{3,4,2,1,0:T(8,128)(2,1)} %param.5) | data formatting | bytes 262144 | tf_op args[0]
  1.2 0.0 copy-start.12
  1.2 0.1 pad_add_fusion.where
  1.3 0.0 copy-start
  1.3 1.6 %copy-done = bf16[1,1,4,512,512]{4,3,2,1,0:T(8,128)(2,1)S(1)} copy-done((bf16[1,1,4,512,512]{4,3,2,1,0:T(8,128)(2,1)S(1)}, bf16[1,1,4,512,512]{4,3,2,1,0:T(8,128)(2,1)}, u32[]{:S(2)}) %copy-start) | copy-done | bytes 2097176
  2.9 0.0 copy-start.7
  2.9 1.1 %copy-done.7 = bf16[1,1,3,256,512]{4,3,2,1,0:T(8,128)(2,1)S(1)} copy-done((bf16[1,1,3,256,512]{4,3,2,1,0:T(8,128)(2,1)S(1)}, bf16[1,1,3,256,512]{4,3,2,1,0:T(8,128)(2,1)}, u32[]{:S(2)}) %copy-start.7) | copy-done | bytes 786456
  4.0 0.0 copy-start.9
  4.0 0.8 copy-done.9
  4.8 0.0 copy-start.11
  4.8 0.7 copy-done.11
  5.5 0.0 copy-start.8
  5.5 2.1 %start.1 = (bf16[512,128]{1,0:T(8,128)(2,1)}, bf16[512,128]{1,0:T(8,128)(2,1)S(1)}) custom-call(s32[2]{0:T(128)S(1)} %pad_add_fusion.where, s32[1,1,4]{2,1,0:T(1,128)S(1)} %copy-done.11, bf16[1,1,4,512,32]{4,3,2,1,0:T(8,128)(2,1)S(1)} %copy.6.right, bf16[1,1,4,512,512]{4,3,2,1,0:T(8,128)(2,1)S(1)} %copy-done, bf16[1,1,3,256,512]{4,3,2,1,0:T(8,128)(2,1)S(1)} %copy-done.7, ...), custom_call_target="tpu_custom_call" | custom-call | flops 1000000000 | bytes 1048576 | tf_op jit(solution)/shard_map/start/pallas_call | solution.py:252
  7.6 0.0 copy-start.13
  7.6 7.3 %all-to-all-start = ((bf16[32,16,128]{2,1,0:T(8,128)(2,1)}), bf16[32,16,128]{2,1,0:T(8,128)(2,1)S(1)}, u32[]{:S(2)}, u32[]{:S(2)}) async-start(bf16[32,16,128]{2,1,0:T(8,128)(2,1)} %bitcast.2), calls=%async_computation | async-start | bytes 262144 | tf_op jit(solution)/shard_map/all_to_all | solution.py:281
  14.9 0.0 copy-done.12
  14.9 0.0 copy-done.8
  14.9 0.0 copy-start.1
  14.9 1.6 %copy-done.1 = bf16[1,1,4,512,512]{4,3,2,1,0:T(8,128)(2,1)S(1)} copy-done((bf16[1,1,4,512,512]{4,3,2,1,0:T(8,128)(2,1)S(1)}, bf16[1,1,4,512,512]{4,3,2,1,0:T(8,128)(2,1)}, u32[]{:S(2)}) %copy-start.1) | copy-done | bytes 2097176
  16.5 1.3 %up_plan_1.1 = (bf16[512,128]{1,0:T(8,128)(2,1)S(1)}, bf16[256,512]{1,0:T(8,128)(2,1)S(1)}, bf16[512,256]{1,0:T(8,128)(2,1)S(1)}, bf16[512,512]{1,0:T(8,128)(2,1)S(1)}) custom-call(s32[2]{0:T(128)S(1)} %pad_add_fusion.where, s32[1,1,4]{2,1,0:T(1,128)S(1)} %copy-done.12, bf16[1,1,4,512,32]{4,3,2,1,0:T(8,128)(2,1)S(1)} %copy.6.right, ...), custom_call_target="tpu_custom_call" | custom-call | flops 1000000000 | bytes 1048576 | tf_op jit(solution)/shard_map/up_plan_1/pallas_call | solution.py:252
  17.8 5.3 %all-to-all-done = bf16[32,16,128]{2,1,0:T(8,128)(2,1)S(1)} async-done(((bf16[32,16,128]{2,1,0:T(8,128)(2,1)}), bf16[32,16,128]{2,1,0:T(8,128)(2,1)S(1)}, u32[]{:S(2)}, u32[]{:S(2)}) %all-to-all-start) | async-done | bytes 131104 | tf_op jit(solution)/shard_map/all_to_all | solution.py:281
  23.1 0.0 copy-done.13
  23.1 1.7 %up_1.1 = (bf16[512,128]{1,0:T(8,128)(2,1)}, bf16[512,128]{1,0:T(8,128)(2,1)S(1)}) custom-call(bf16[512,128]{1,0:T(8,128)(2,1)S(1)} %bitcast.16, bf16[512,128]{1,0:T(8,128)(2,1)S(1)} %get-tuple-element.41.side, bf16[256,512]{1,0:T(8,128)(2,1)S(1)} %get-tuple-element.42.product, bf16[512,256]{1,0:T(8,128)(2,1)S(1)} %get-tuple-element.43.sender, ...), custom_call_target="tpu_custom_call" | custom-call | flops 1000000 | bytes 1048576 | tf_op jit(solution)/shard_map/up_1/pallas_call | solution.py:252
  24.9 2.6 %all-to-all-start.1 = ((bf16[32,16,128]{2,1,0:T(8,128)(2,1)}), bf16[32,16,128]{2,1,0:T(8,128)(2,1)S(1)}, u32[]{:S(2)}, u32[]{:S(2)}) async-start(bf16[32,16,128]{2,1,0:T(8,128)(2,1)} %bitcast.4), calls=%async_computation.1 | async-start | bytes 262144 | tf_op jit(solution)/shard_map/all_to_all | solution.py:281
  27.4 0.0 copy-start.2
  27.5 1.6 %copy-done.2 = bf16[1,1,4,512,512]{4,3,2,1,0:T(8,128)(2,1)S(1)} copy-done((bf16[1,1,4,512,512]{4,3,2,1,0:T(8,128)(2,1)S(1)}, bf16[1,1,4,512,512]{4,3,2,1,0:T(8,128)(2,1)}, u32[]{:S(2)}) %copy-start.2) | copy-done | bytes 2097176
  29.0 0.0 copy-start.10
  29.0 1.3 %up_plan_2.1 = (bf16[512,128]{1,0:T(8,128)(2,1)S(1)}, bf16[256,512]{1,0:T(8,128)(2,1)S(1)}, bf16[512,256]{1,0:T(8,128)(2,1)S(1)}, bf16[512,512]{1,0:T(8,128)(2,1)S(1)}) custom-call(s32[2]{0:T(128)S(1)} %pad_add_fusion.where, s32[1,1,4]{2,1,0:T(1,128)S(1)} %copy-done.12, bf16[1,1,4,512,32]{4,3,2,1,0:T(8,128)(2,1)S(1)} %copy.6.right, ...), custom_call_target="tpu_custom_call" | custom-call | flops 1000000000 | bytes 1048576 | tf_op jit(solution)/shard_map/up_plan_2/pallas_call | solution.py:252
  30.3 5.3 %all-to-all-done.1 = bf16[32,16,128]{2,1,0:T(8,128)(2,1)S(1)} async-done(((bf16[32,16,128]{2,1,0:T(8,128)(2,1)}), bf16[32,16,128]{2,1,0:T(8,128)(2,1)S(1)}, u32[]{:S(2)}, u32[]{:S(2)}) %all-to-all-start.1) | async-done | bytes 131104 | tf_op jit(solution)/shard_map/all_to_all | solution.py:281
  35.7 1.7 %up_2.1 = (bf16[512,128]{1,0:T(8,128)(2,1)}, bf16[512,128]{1,0:T(8,128)(2,1)S(1)}) custom-call(bf16[512,128]{1,0:T(8,128)(2,1)S(1)} %bitcast.17, bf16[512,128]{1,0:T(8,128)(2,1)S(1)} %get-tuple-element.46.side, bf16[256,512]{1,0:T(8,128)(2,1)S(1)} %get-tuple-element.47.product, bf16[512,256]{1,0:T(8,128)(2,1)S(1)} %get-tuple-element.48.sender, ...), custom_call_target="tpu_custom_call" | custom-call | flops 1000000 | bytes 1048576 | tf_op jit(solution)/shard_map/up_2/pallas_call | solution.py:252
  37.4 2.6 %all-to-all-start.2 = ((bf16[32,16,128]{2,1,0:T(8,128)(2,1)}), bf16[32,16,128]{2,1,0:T(8,128)(2,1)S(1)}, u32[]{:S(2)}, u32[]{:S(2)}) async-start(bf16[32,16,128]{2,1,0:T(8,128)(2,1)} %bitcast.6), calls=%async_computation.2 | async-start | bytes 262144 | tf_op jit(solution)/shard_map/all_to_all | solution.py:281
  40.0 0.0 copy-done.10
  40.0 0.0 copy-start.3
  40.0 1.6 %copy-done.3 = bf16[1,1,4,512,512]{4,3,2,1,0:T(8,128)(2,1)S(1)} copy-done((bf16[1,1,4,512,512]{4,3,2,1,0:T(8,128)(2,1)S(1)}, bf16[1,1,4,512,512]{4,3,2,1,0:T(8,128)(2,1)}, u32[]{:S(2)}) %copy-start.3) | copy-done | bytes 2097176
  41.6 1.5 %top_plan.1 = (bf16[512,128]{1,0:T(8,128)(2,1)S(1)}, bf16[512,512]{1,0:T(8,128)(2,1)S(1)}, bf16[512,512]{1,0:T(8,128)(2,1)S(1)}, bf16[512,512]{1,0:T(8,128)(2,1)S(1)}) custom-call(s32[2]{0:T(128)S(1)} %pad_add_fusion.where, s32[1,1,4]{2,1,0:T(1,128)S(1)} %copy-done.12, bf16[1,1,4,512,32]{4,3,2,1,0:T(8,128)(2,1)S(1)} %copy.6.right, ...), custom_call_target="tpu_custom_call" | custom-call | flops 1000000000 | bytes 1048576 | tf_op jit(solution)/shard_map/top_plan/pallas_call | solution.py:252
  43.1 5.1 %all-to-all-done.2 = bf16[32,16,128]{2,1,0:T(8,128)(2,1)S(1)} async-done(((bf16[32,16,128]{2,1,0:T(8,128)(2,1)}), bf16[32,16,128]{2,1,0:T(8,128)(2,1)S(1)}, u32[]{:S(2)}, u32[]{:S(2)}) %all-to-all-start.2) | async-done | bytes 131104 | tf_op jit(solution)/shard_map/all_to_all | solution.py:281
  48.2 1.7 %top.1 = (bf16[512,128]{1,0:T(8,128)(2,1)}, bf16[512,128]{1,0:T(8,128)(2,1)S(1)}) custom-call(bf16[512,128]{1,0:T(8,128)(2,1)S(1)} %bitcast.15, bf16[512,128]{1,0:T(8,128)(2,1)S(1)} %get-tuple-element.51.side, bf16[512,512]{1,0:T(8,128)(2,1)S(1)} %get-tuple-element.52.product, bf16[512,512]{1,0:T(8,128)(2,1)S(1)} %get-tuple-element.53.taker, ...), custom_call_target="tpu_custom_call" | custom-call | flops 1000000 | bytes 1048576 | tf_op jit(solution)/shard_map/top/pallas_call | solution.py:252
  49.9 2.6 %all-to-all-start.3 = ((bf16[32,16,128]{2,1,0:T(8,128)(2,1)}), bf16[32,16,128]{2,1,0:T(8,128)(2,1)S(1)}, u32[]{:S(2)}, u32[]{:S(2)}) async-start(bf16[32,16,128]{2,1,0:T(8,128)(2,1)} %bitcast.8), calls=%async_computation.3 | async-start | bytes 262144 | tf_op jit(solution)/shard_map/all_to_all | solution.py:281
  52.5 0.0 copy-start.4
  52.5 1.6 %copy-done.4 = bf16[1,1,4,512,512]{4,3,2,1,0:T(8,128)(2,1)S(1)} copy-done((bf16[1,1,4,512,512]{4,3,2,1,0:T(8,128)(2,1)S(1)}, bf16[1,1,4,512,512]{4,3,2,1,0:T(8,128)(2,1)}, u32[]{:S(2)}) %copy-start.4) | copy-done | bytes 2097176
  54.1 1.6 %down_plan_2.1 = (f32[512,128]{1,0:T(8,128)S(1)}, bf16[512,256]{1,0:T(8,128)(2,1)S(1)}, bf16[256,512]{1,0:T(8,128)(2,1)S(1)}, bf16[512,512]{1,0:T(8,128)(2,1)S(1)}) custom-call(s32[2]{0:T(128)S(1)} %pad_add_fusion.where, s32[1,1,4]{2,1,0:T(1,128)S(1)} %copy-done.12, bf16[1,1,4,512,512]{4,3,2,1,0:T(8,128)(2,1)S(1)} %copy-done.4, ...), custom_call_target="tpu_custom_call" | custom-call | flops 1000000000 | bytes 1048576 | tf_op jit(solution)/shard_map/down_plan_2/pallas_call | solution.py:252
  55.7 5.0 %all-to-all-done.3 = bf16[32,16,128]{2,1,0:T(8,128)(2,1)S(1)} async-done(((bf16[32,16,128]{2,1,0:T(8,128)(2,1)}), bf16[32,16,128]{2,1,0:T(8,128)(2,1)S(1)}, u32[]{:S(2)}, u32[]{:S(2)}) %all-to-all-start.3) | async-done | bytes 131104 | tf_op jit(solution)/shard_map/all_to_all | solution.py:281
  60.7 1.5 %down_2.1 = (bf16[512,128]{1,0:T(8,128)(2,1)}, bf16[512,128]{1,0:T(8,128)(2,1)S(1)}) custom-call(bf16[512,128]{1,0:T(8,128)(2,1)S(1)} %bitcast.18, f32[512,128]{1,0:T(8,128)S(1)} %get-tuple-element.57.side, bf16[512,256]{1,0:T(8,128)(2,1)S(1)} %get-tuple-element.58.product, bf16[256,512]{1,0:T(8,128)(2,1)S(1)} %get-tuple-element.59.picker, ...), custom_call_target="tpu_custom_call" | custom-call | flops 1000000 | bytes 1048576 | tf_op jit(solution)/shard_map/down_2/pallas_call | solution.py:252
  62.3 2.6 %all-to-all-start.4 = ((bf16[32,16,128]{2,1,0:T(8,128)(2,1)}), bf16[32,16,128]{2,1,0:T(8,128)(2,1)S(1)}, u32[]{:S(2)}, u32[]{:S(2)}) async-start(bf16[32,16,128]{2,1,0:T(8,128)(2,1)} %bitcast.10), calls=%async_computation.4 | async-start | bytes 262144 | tf_op jit(solution)/shard_map/all_to_all | solution.py:281
  64.9 0.0 copy-start.5
  64.9 1.6 %copy-done.5 = bf16[1,1,4,512,512]{4,3,2,1,0:T(8,128)(2,1)S(1)} copy-done((bf16[1,1,4,512,512]{4,3,2,1,0:T(8,128)(2,1)S(1)}, bf16[1,1,4,512,512]{4,3,2,1,0:T(8,128)(2,1)}, u32[]{:S(2)}) %copy-start.5) | copy-done | bytes 2097176
  66.5 0.0 copy-start.14
  66.5 1.6 %down_plan_1.1 = (f32[512,128]{1,0:T(8,128)S(1)}, bf16[512,256]{1,0:T(8,128)(2,1)S(1)}, bf16[256,512]{1,0:T(8,128)(2,1)S(1)}, bf16[512,512]{1,0:T(8,128)(2,1)S(1)}) custom-call(s32[2]{0:T(128)S(1)} %pad_add_fusion.where, s32[1,1,4]{2,1,0:T(1,128)S(1)} %copy-done.12, bf16[1,1,4,512,512]{4,3,2,1,0:T(8,128)(2,1)S(1)} %copy-done.5, ...), custom_call_target="tpu_custom_call" | custom-call | flops 1000000000 | bytes 1048576 | tf_op jit(solution)/shard_map/down_plan_1/pallas_call | solution.py:252
  68.1 5.0 %all-to-all-done.4 = bf16[32,16,128]{2,1,0:T(8,128)(2,1)S(1)} async-done(((bf16[32,16,128]{2,1,0:T(8,128)(2,1)}), bf16[32,16,128]{2,1,0:T(8,128)(2,1)S(1)}, u32[]{:S(2)}, u32[]{:S(2)}) %all-to-all-start.4) | async-done | bytes 131104 | tf_op jit(solution)/shard_map/all_to_all | solution.py:281
  73.1 1.5 %down_1.1 = (bf16[512,128]{1,0:T(8,128)(2,1)}, bf16[512,128]{1,0:T(8,128)(2,1)S(1)}) custom-call(bf16[512,128]{1,0:T(8,128)(2,1)S(1)} %bitcast.19, f32[512,128]{1,0:T(8,128)S(1)} %get-tuple-element.63.side, bf16[512,256]{1,0:T(8,128)(2,1)S(1)} %get-tuple-element.64.product, bf16[256,512]{1,0:T(8,128)(2,1)S(1)} %get-tuple-element.65.picker, ...), custom_call_target="tpu_custom_call" | custom-call | flops 1000000 | bytes 1048576 | tf_op jit(solution)/shard_map/down_1/pallas_call | solution.py:252
  74.6 2.6 %all-to-all-start.5 = ((bf16[32,16,128]{2,1,0:T(8,128)(2,1)}), bf16[32,16,128]{2,1,0:T(8,128)(2,1)S(1)}, u32[]{:S(2)}, u32[]{:S(2)}) async-start(bf16[32,16,128]{2,1,0:T(8,128)(2,1)} %bitcast.12), calls=%async_computation.5 | async-start | bytes 262144 | tf_op jit(solution)/shard_map/all_to_all | solution.py:281
  77.2 0.0 copy-done.14
  77.2 0.0 copy-start.6
  77.2 1.6 %copy-done.6 = bf16[1,1,4,512,512]{4,3,2,1,0:T(8,128)(2,1)S(1)} copy-done((bf16[1,1,4,512,512]{4,3,2,1,0:T(8,128)(2,1)S(1)}, bf16[1,1,4,512,512]{4,3,2,1,0:T(8,128)(2,1)}, u32[]{:S(2)}) %copy-start.6) | copy-done | bytes 2097176
  78.8 1.1 %down_plan_0.1 = (f32[512,128]{1,0:T(8,128)S(1)}, bf16[512,256]{1,0:T(8,128)(2,1)S(1)}, bf16[256,512]{1,0:T(8,128)(2,1)S(1)}) custom-call(s32[2]{0:T(128)S(1)} %pad_add_fusion.where, s32[1,1,4]{2,1,0:T(1,128)S(1)} %copy-done.12, bf16[1,1,4,512,512]{4,3,2,1,0:T(8,128)(2,1)S(1)} %copy-done.6, bf16[1,1,3,256,512]{4,3,2,1,0:T(8,128)(2,1)S(1)} %copy-done.8, ...), custom_call_target="tpu_custom_call" | custom-call | flops 1000000000 | bytes 1048576 | tf_op jit(solution)/shard_map/down_plan_0/pallas_call | solution.py:252
  79.9 5.6 %all-to-all-done.5 = bf16[32,16,128]{2,1,0:T(8,128)(2,1)S(1)} async-done(((bf16[32,16,128]{2,1,0:T(8,128)(2,1)}), bf16[32,16,128]{2,1,0:T(8,128)(2,1)S(1)}, u32[]{:S(2)}, u32[]{:S(2)}) %all-to-all-start.5) | async-done | bytes 131104 | tf_op jit(solution)/shard_map/all_to_all | solution.py:281
  85.4 0.5 last.1
  86.0 0.8 copy.10
Async XLA Ops:
  1.2 13.7 %copy-start.12 = (s32[1,1,4]{2,1,0:T(1,128)S(1)}, s32[1,1,4]{2,1,0:T(1,128)}, u32[]{:S(2)}) copy-start(s32[1,1,4]{2,1,0:T(1,128)} %widths.13) | copy-start | bytes 52
  1.3 1.6 %copy-start = (bf16[1,1,4,512,512]{4,3,2,1,0:T(8,128)(2,1)S(1)}, bf16[1,1,4,512,512]{4,3,2,1,0:T(8,128)(2,1)}, u32[]{:S(2)}) copy-start(bf16[1,1,4,512,512]{4,3,2,1,0:T(8,128)(2,1)} %inverse.13) | copy-start | bytes 6291460
  2.9 1.1 %copy-start.7 = (bf16[1,1,3,256,512]{4,3,2,1,0:T(8,128)(2,1)S(1)}, bf16[1,1,3,256,512]{4,3,2,1,0:T(8,128)(2,1)}, u32[]{:S(2)}) copy-start(bf16[1,1,3,256,512]{4,3,2,1,0:T(8,128)(2,1)} %coupling.11) | copy-start | bytes 2359300
  4.0 0.8 copy-start.9
  4.8 0.7 copy-start.11
  5.5 9.5 %copy-start.8 = (bf16[1,1,3,256,512]{4,3,2,1,0:T(8,128)(2,1)S(1)}, bf16[1,1,3,256,512]{4,3,2,1,0:T(8,128)(2,1)}, u32[]{:S(2)}) copy-start(bf16[1,1,3,256,512]{4,3,2,1,0:T(8,128)(2,1)} %coupling.11) | copy-start | bytes 2359300
  7.6 15.5 %copy-start.13 = (bf16[512,128]{1,0:T(8,128)(2,1)}, bf16[512,128]{1,0:T(8,128)(2,1)S(1)}, u32[]{:S(2)}) copy-start(bf16[512,128]{1,0:T(8,128)(2,1)S(1)} %get-tuple-element.68.state) | copy-start | bytes 393220
  7.6 15.5 %all-to-all-start = ((bf16[32,16,128]{2,1,0:T(8,128)(2,1)}), bf16[32,16,128]{2,1,0:T(8,128)(2,1)S(1)}, u32[]{:S(2)}, u32[]{:S(2)}) async-start(bf16[32,16,128]{2,1,0:T(8,128)(2,1)} %bitcast.2), calls=%async_computation | async-start | bytes 262144 | tf_op jit(solution)/shard_map/all_to_all | solution.py:281
  14.9 1.6 %copy-start.1 = (bf16[1,1,4,512,512]{4,3,2,1,0:T(8,128)(2,1)S(1)}, bf16[1,1,4,512,512]{4,3,2,1,0:T(8,128)(2,1)}, u32[]{:S(2)}) copy-start(bf16[1,1,4,512,512]{4,3,2,1,0:T(8,128)(2,1)} %inverse.13) | copy-start | bytes 6291460
  24.9 10.8 %all-to-all-start.1 = ((bf16[32,16,128]{2,1,0:T(8,128)(2,1)}), bf16[32,16,128]{2,1,0:T(8,128)(2,1)S(1)}, u32[]{:S(2)}, u32[]{:S(2)}) async-start(bf16[32,16,128]{2,1,0:T(8,128)(2,1)} %bitcast.4), calls=%async_computation.1 | async-start | bytes 262144 | tf_op jit(solution)/shard_map/all_to_all | solution.py:281
  27.4 1.6 %copy-start.2 = (bf16[1,1,4,512,512]{4,3,2,1,0:T(8,128)(2,1)S(1)}, bf16[1,1,4,512,512]{4,3,2,1,0:T(8,128)(2,1)}, u32[]{:S(2)}) copy-start(bf16[1,1,4,512,512]{4,3,2,1,0:T(8,128)(2,1)} %inverse.13) | copy-start | bytes 6291460
  29.0 10.9 %copy-start.10 = (s32[3,2,16,64]{3,2,1,0:T(8,128)S(1)}, s32[3,2,16,64]{3,2,1,0:T(8,128)}, u32[]{:S(2)}) copy-start(s32[3,2,16,64]{3,2,1,0:T(8,128)} %targets.13) | copy-start | bytes 73732
  37.4 10.8 %all-to-all-start.2 = ((bf16[32,16,128]{2,1,0:T(8,128)(2,1)}), bf16[32,16,128]{2,1,0:T(8,128)(2,1)S(1)}, u32[]{:S(2)}, u32[]{:S(2)}) async-start(bf16[32,16,128]{2,1,0:T(8,128)(2,1)} %bitcast.6), calls=%async_computation.2 | async-start | bytes 262144 | tf_op jit(solution)/shard_map/all_to_all | solution.py:281
  40.0 1.6 %copy-start.3 = (bf16[1,1,4,512,512]{4,3,2,1,0:T(8,128)(2,1)S(1)}, bf16[1,1,4,512,512]{4,3,2,1,0:T(8,128)(2,1)}, u32[]{:S(2)}) copy-start(bf16[1,1,4,512,512]{4,3,2,1,0:T(8,128)(2,1)} %inverse.13) | copy-start | bytes 6291460
  49.9 10.8 %all-to-all-start.3 = ((bf16[32,16,128]{2,1,0:T(8,128)(2,1)}), bf16[32,16,128]{2,1,0:T(8,128)(2,1)S(1)}, u32[]{:S(2)}, u32[]{:S(2)}) async-start(bf16[32,16,128]{2,1,0:T(8,128)(2,1)} %bitcast.8), calls=%async_computation.3 | async-start | bytes 262144 | tf_op jit(solution)/shard_map/all_to_all | solution.py:281
  52.5 1.6 %copy-start.4 = (bf16[1,1,4,512,512]{4,3,2,1,0:T(8,128)(2,1)S(1)}, bf16[1,1,4,512,512]{4,3,2,1,0:T(8,128)(2,1)}, u32[]{:S(2)}) copy-start(bf16[1,1,4,512,512]{4,3,2,1,0:T(8,128)(2,1)} %inverse.13) | copy-start | bytes 6291460
  62.3 10.8 %all-to-all-start.4 = ((bf16[32,16,128]{2,1,0:T(8,128)(2,1)}), bf16[32,16,128]{2,1,0:T(8,128)(2,1)S(1)}, u32[]{:S(2)}, u32[]{:S(2)}) async-start(bf16[32,16,128]{2,1,0:T(8,128)(2,1)} %bitcast.10), calls=%async_computation.4 | async-start | bytes 262144 | tf_op jit(solution)/shard_map/all_to_all | solution.py:281
  64.9 1.6 %copy-start.5 = (bf16[1,1,4,512,512]{4,3,2,1,0:T(8,128)(2,1)S(1)}, bf16[1,1,4,512,512]{4,3,2,1,0:T(8,128)(2,1)}, u32[]{:S(2)}) copy-start(bf16[1,1,4,512,512]{4,3,2,1,0:T(8,128)(2,1)} %inverse.13) | copy-start | bytes 6291460
  66.5 10.8 %copy-start.14 = (bf16[512,128]{1,0:T(8,128)(2,1)S(1)}, bf16[512,128]{1,0:T(8,128)(2,1)}, u32[]{:S(2)}) copy-start(bf16[512,128]{1,0:T(8,128)(2,1)} %copy-done.13) | copy-start | bytes 393220
  74.6 10.8 %all-to-all-start.5 = ((bf16[32,16,128]{2,1,0:T(8,128)(2,1)}), bf16[32,16,128]{2,1,0:T(8,128)(2,1)S(1)}, u32[]{:S(2)}, u32[]{:S(2)}) async-start(bf16[32,16,128]{2,1,0:T(8,128)(2,1)} %bitcast.12), calls=%async_computation.5 | async-start | bytes 262144 | tf_op jit(solution)/shard_map/all_to_all | solution.py:281
  77.2 1.6 %copy-start.6 = (bf16[1,1,4,512,512]{4,3,2,1,0:T(8,128)(2,1)S(1)}, bf16[1,1,4,512,512]{4,3,2,1,0:T(8,128)(2,1)}, u32[]{:S(2)}) copy-start(bf16[1,1,4,512,512]{4,3,2,1,0:T(8,128)(2,1)} %inverse.13) | copy-start | bytes 6291460

commit v2 on v1

v2 whole, which is shorter than its diff:
```python
import functools

import jax
import jax.numpy as jnp
from jax import lax
from jax.experimental import pallas as pl
from jax.experimental.pallas import tpu as pltpu
from jax.sharding import Mesh, PartitionSpec as P

BLOCK = 128
LANES = 128
F32 = jnp.float32
BF16 = jnp.bfloat16


def iota(shape, axis):
    return lax.broadcasted_iota(jnp.int32, shape, axis)


def ones_where(condition):
    return jnp.where(condition, 1.0, 0.0).astype(BF16)


def dot(left, right):
    return jnp.dot(left, right, preferred_element_type=F32)


def trans_dot(left, right):
    return lax.dot_general(left, right, (((0,), (0,)), ((), ())), preferred_element_type=F32)


class Sizes:
    def __init__(self, right_sides, couplings, targets, leaf_axes):
        self.leaf_axes = leaf_axes
        self.owners = lax.axis_size("blk")
        self.levels, self.columns, self.width = right_sides.shape[-3:]
        self.rows = couplings.shape[-2]
        self.pieces = targets.shape[-1]
        self.leaf_bits = len(leaf_axes)
        self.sub = self.rows // self.pieces
        self.places = self.width // self.sub
        self.cap = max(3, (2 * self.pieces + self.owners - 1) // self.owners + 1)
        self.message = self.cap + self.cap % 2
        self.slots = 2 * self.owners * self.message


def live(widths, level, shape, axis):
    return iota(shape, axis) < widths[level] * BLOCK


def own_lanes(sizes, rows):
    shape = (rows, LANES)
    return iota(shape, 1) // sizes.columns == iota(shape, 0) % sizes.sub


def keep_own(sizes, value):
    return jnp.where(own_lanes(sizes, value.shape[0]), value, jnp.zeros_like(value))


def spread(sizes, value):
    value = keep_own(sizes, value)
    step = sizes.columns
    while step < LANES:
        value = value + pltpu.roll(value, step, 1)
        step *= 2
    return value


def repeat_columns(sizes, value):
    return jnp.concatenate([value] * (LANES // sizes.columns), axis=0).T


def position(sizes, level):
    group = 0
    for axis in sizes.leaf_axes:
        group = group * 2 + lax.axis_index(axis)
    return group, lax.axis_index("blk"), level % sizes.leaf_bits


def send_slots(sizes, level, targets):
    group, owner, bit = position(sizes, level)
    count = sizes.pieces
    table = targets[level, group]
    mine = jnp.sum(jnp.where(iota(table.shape, 0) == owner, table, 0), axis=0, keepdims=True)
    key_row = mine // sizes.places
    square = (count, count)
    diagonal = iota(square, 0) == iota(square, 1)
    keys_down = jnp.broadcast_to(key_row, square)
    key_col = jnp.sum(jnp.where(diagonal, keys_down, 0).astype(F32), axis=1, keepdims=True).astype(jnp.int32)
    same = keys_down == key_col
    rank_row = jnp.sum(jnp.where(same & (iota(square, 0) < iota(square, 1)), 1.0, 0.0), axis=0, keepdims=True)
    rank_col = jnp.sum(jnp.where(same & (iota(square, 1) < iota(square, 0)), 1.0, 0.0), axis=1, keepdims=True)

    def slot(key, rank):
        side, dest = key // sizes.owners, key % sizes.owners
        half = jnp.bitwise_xor(side, lax.shift_right_logical(group, bit) & 1)
        return (half * sizes.owners + dest) * sizes.message + rank.astype(jnp.int32)

    return slot(key_row, rank_row), slot(key_col, rank_col)


def send_rows(sizes, level, targets):
    _, slot_col = send_slots(sizes, level, targets)
    shape = (sizes.pieces, sizes.rows)
    chosen = iota(shape, 1) // sizes.sub == iota(shape, 0)
    wide = jnp.sum(jnp.where(chosen, slot_col, 0).astype(F32), axis=0, keepdims=True).astype(jnp.int32)
    return ones_where(iota((sizes.slots, sizes.rows), 0) == wide)


def send_columns(sizes, level, targets):
    slot_row, _ = send_slots(sizes, level, targets)
    shape = (sizes.rows, sizes.pieces)
    chosen = iota(shape, 0) // sizes.sub == iota(shape, 1)
    wide = jnp.sum(jnp.where(chosen, slot_row, 0).astype(F32), axis=1, keepdims=True).astype(jnp.int32)
    return ones_where(iota((sizes.rows, sizes.slots), 1) == wide)


def take_table(sizes, level, targets):
    group, owner, bit = position(sizes, level)
    own_half = lax.shift_right_logical(group, bit) & 1
    first = group - own_half * 2**bit
    tables = []
    for half in range(2):
        codes = targets[level, first + half * 2**bit]
        wanted = jnp.bitwise_xor(own_half, half) * sizes.owners + owner
        tables.append(jnp.where(codes // sizes.places == wanted, codes % sizes.places + 1, 0))
    place = jnp.concatenate(tables, axis=0).astype(F32)
    square = (sizes.pieces, sizes.pieces)
    earlier = ones_where(iota(square, 0) < iota(square, 1))
    rank = dot(ones_where(place > 0), earlier)
    return place, rank


def take_rows(sizes, level, targets):
    place, rank = take_table(sizes, level, targets)
    shape = (2 * sizes.owners, sizes.slots)
    offset = iota(shape, 1) - iota(shape, 0) * sizes.message
    spot = jnp.zeros(shape, F32)
    for each in range(sizes.cap):
        held = jnp.sum(jnp.where(rank == each, place, 0.0), axis=1, keepdims=True)
        spot = jnp.where(offset == each, held, spot)
    spot = jnp.sum(spot, axis=0, keepdims=True).astype(jnp.int32)
    return ones_where(iota((sizes.width, sizes.slots), 0) // sizes.sub + 1 == spot)


def take_columns(sizes, level, targets):
    place, rank = take_table(sizes, level, targets)
    shape = (sizes.slots, 2 * sizes.owners)
    source = ones_where(iota(shape, 0) // sizes.message == iota(shape, 1))
    places = dot(source, place.astype(BF16))
    ranks = dot(source, rank.astype(BF16))
    wanted = (iota(places.shape, 0) % sizes.message).astype(F32)
    spot = jnp.sum(jnp.where(ranks == wanted, places, 0.0), axis=1, keepdims=True).astype(jnp.int32)
    return ones_where(iota((sizes.slots, sizes.width), 1) // sizes.sub + 1 == spot)


def coupled_inverse(sizes, level, widths, inverse, coupling):
    kept = jnp.where(live(widths, level, coupling.shape, 1), coupling, jnp.zeros_like(coupling))
    return dot(kept, inverse).astype(BF16)


def solve_forward(sizes, level, widths, inverse, residual):
    product = dot(inverse, residual)
    return jnp.where(live(widths, level, product.shape, 0), product, 0.0).astype(BF16)


def solve_backward(sizes, level, widths, inverse, side):
    product = trans_dot(inverse, side)
    return jnp.where(live(widths, level, product.shape, 0), product, 0.0)


def fetch(source, target, semaphore):
    copy = pltpu.make_async_copy(source, target, semaphore)
    copy.start()
    return copy


def start_kernel(sizes, right, inverse, coupling, widths, targets, buffer, forward, *scratch):
    right_in, inverse_in, coupling_in, widths_in, targets_in, done = scratch
    copies = [
        fetch(targets.at[pl.ds(0, 1)], targets_in, done.at[0]),
        fetch(right.at[0, 0, 0], right_in, done.at[1]),
        fetch(widths.at[0, 0], widths_in, done.at[2]),
        fetch(inverse.at[0, 0, 0], inverse_in, done.at[3]),
        fetch(coupling.at[0, 0, 0], coupling_in, done.at[4]),
    ]
    copies[0].wait()
    sender = send_rows(sizes, 0, targets_in)
    copies[1].wait()
    residual = repeat_columns(sizes, right_in[...])
    copies[2].wait()
    copies[3].wait()
    solved = solve_forward(sizes, 0, widths_in, inverse_in[...], residual)
    forward[...] = solved
    copies[4].wait()
    pieces = keep_own(sizes, dot(coupling_in[...], solved).astype(BF16))
    buffer[...] = dot(sender, pieces).astype(BF16)


def up_plan_kernel(sizes, right, inverse, coupling, widths, targets, after, *refs):
    top = sizes.levels - 1
    right_in, inverse_in, coupling_in, widths_in, targets_in, done = refs[-6:]
    outs = refs[:-6]
    copies = [
        fetch(targets, targets_in, done.at[0]),
        fetch(right.at[0, 0], right_in, done.at[1]),
        fetch(widths.at[0, 0], widths_in, done.at[2]),
        fetch(inverse.at[0, 0, pl.ds(1, top)], inverse_in, done.at[3]),
        fetch(coupling.at[0, 0, pl.ds(1, top - 1)], coupling_in, done.at[4]),
    ]
    copies[0].wait()
    for level in range(1, top):
        _, _, sender, taker = outs[4 * level - 4 : 4 * level]
        sender[...] = send_rows(sizes, level, targets_in)
        taker[...] = take_rows(sizes, level - 1, targets_in)
    _, _, taker, returner = outs[-4:]
    taker[...] = take_rows(sizes, top - 1, targets_in)
    returner[...] = take_columns(sizes, top - 1, targets_in)
    copies[1].wait()
    for level in range(1, top + 1):
        outs[4 * level - 4][...] = repeat_columns(sizes, right_in[level])
    copies[2].wait()
    copies[3].wait()
    copies[4].wait()
    for level in range(1, top):
        product = coupled_inverse(sizes, level, widths_in, inverse_in[level - 1], coupling_in[level - 1])
        outs[4 * level - 3][...] = product
    block = inverse_in[top - 1]
    kept = jnp.where(live(widths_in, top, block.shape, 0), block, jnp.zeros_like(block))
    full = trans_dot(block, kept)
    outs[-3][...] = jnp.where(live(widths_in, top, full.shape, 0), full, 0.0).astype(BF16)


def up_kernel(sizes, arrived, side, product, sender, taker, buffer, residual):
    incoming = spread(sizes, dot(taker[...], arrived[...]))
    left = (side[...].astype(F32) - incoming).astype(BF16)
    residual[...] = left
    pieces = keep_own(sizes, dot(product[...], left).astype(BF16))
    buffer[...] = dot(sender[...], pieces).astype(BF16)


def top_kernel(sizes, arrived, side, product, taker, returner, buffer, solved):
    incoming = spread(sizes, dot(taker[...], arrived[...]))
    left = (side[...].astype(F32) - incoming).astype(BF16)
    value = dot(product[...], left).astype(BF16)
    buffer[...] = dot(returner[...], keep_own(sizes, value)).astype(BF16)
    solved[...] = value


def down_plan_kernel(sizes, inverse, coupling, widths, targets, after, *refs):
    top = sizes.levels - 1
    inverse_in, coupling_in, widths_in, targets_in, done = refs[-5:]
    states, products, outs = refs[:top], refs[top : 2 * top - 1], refs[2 * top - 1 : -5]
    copies = [
        fetch(targets, targets_in, done.at[0]),
        fetch(widths.at[0, 0], widths_in, done.at[1]),
        fetch(inverse.at[0, 0, pl.ds(0, top)], inverse_in, done.at[2]),
        fetch(coupling.at[0, 0, 0], coupling_in, done.at[3]),
    ]
    copies[0].wait()
    for level in range(top):
        outs[4 * level + 2][...] = send_columns(sizes, level, targets_in)
        if level > 0:
            outs[4 * level + 3 - 4][...] = take_columns(sizes, level - 1, targets_in)
    for copy in copies[1:]:
        copy.wait()
    for level in range(top):
        block = inverse_in[level]
        forward = states[level][...]
        if level > 0:
            forward = solve_forward(sizes, level, widths_in, block, forward)
            full = products[level - 1][...].T
        else:
            full = coupled_inverse(sizes, level, widths_in, block, coupling_in[...]).T
        outs[4 * level][...] = solve_backward(sizes, level, widths_in, block, forward)
        outs[4 * level + 1][...] = jnp.where(live(widths_in, level, full.shape, 0), full, jnp.zeros_like(full))


def down_kernel(sizes, arrived, side, product, picker, returner, buffer, solved):
    gathered = spread(sizes, dot(picker[...], arrived[...])).astype(BF16)
    value = (side[...] - dot(product[...], gathered)).astype(BF16)
    buffer[...] = dot(returner[...], keep_own(sizes, value)).astype(BF16)
    solved[...] = value


def last_kernel(sizes, arrived, side, product, picker, *refs):
    above, out, held, done = refs[:-3], refs[-3], refs[-2], refs[-1]
    count = len(above)
    for level in range(count):
        held[level + 1] = above[level][...].T[: sizes.columns]
    early = fetch(held.at[pl.ds(1, count)], out.at[0, 0, pl.ds(1, count)], done.at[0])
    gathered = spread(sizes, dot(picker[...], arrived[...])).astype(BF16)
    value = (side[...] - dot(product[...], gathered)).astype(BF16)
    held[0] = value.T[: sizes.columns]
    late = fetch(held.at[0], out.at[0, 0, 0], done.at[1])
    early.wait()
    late.wait()


VMEM = pl.BlockSpec(memory_space=pltpu.VMEM)
HBM = pl.BlockSpec(memory_space=pltpu.HBM)


def call(kernel, name, operands, far, outs, cost, scratch=(), out_spec=VMEM):
    held = [pltpu.with_memory_space_constraint(one, pltpu.HBM) for one in operands[:far]]
    operands = (*held, *operands[far:])
    return pl.pallas_call(
        kernel,
        in_specs=[HBM] * far + [VMEM] * (len(operands) - far),
        out_specs=[out_spec] * len(outs),
        out_shape=[jax.ShapeDtypeStruct(shape, kind) for shape, kind in outs],
        scratch_shapes=scratch,
        compiler_params=pltpu.CompilerParams(vmem_limit_bytes=24 * 2**20),
        cost_estimate=pl.CostEstimate(flops=cost, bytes_accessed=2**20, transcendentals=0),
        name=name,
    )(*operands)


def shards(leaf_axes, right_sides, inverses, couplings, widths, targets):
    right_sides = jnp.swapaxes(right_sides, 3, 4)
    sizes = Sizes(right_sides, couplings, targets, leaf_axes)
    width, slots, rows, columns, levels = sizes.width, sizes.slots, sizes.rows, sizes.columns, sizes.levels
    top = levels - 1
    vector = ((width, LANES), BF16)
    message = ((slots, LANES), BF16)
    side = ((width, LANES), F32)
    codes = targets.shape[1:]
    small, large = 10**6, 10**9

    def exchange(buffer, level):
        pair = leaf_axes[len(leaf_axes) - 1 - level % sizes.leaf_bits]
        blocks = buffer.reshape(slots // 2, 2, LANES)
        moved = lax.all_to_all(blocks, (pair, "blk"), split_axis=0, concat_axis=0, tiled=True)
        return moved.reshape(slots, LANES)

    buffer, state = call(
        functools.partial(start_kernel, sizes),
        "start",
        (right_sides, inverses, couplings, widths, targets),
        5,
        (message, vector),
        large,
        (
            pltpu.VMEM((columns, width), BF16),
            pltpu.VMEM((width, width), BF16),
            pltpu.VMEM((rows, width), BF16),
            pltpu.SMEM((levels,), jnp.int32),
            pltpu.VMEM((1, *codes), jnp.int32),
            pltpu.SemaphoreType.DMA((5,)),
        ),
    )
    up_shapes = (vector, ((rows, width), BF16), ((slots, rows), BF16), ((width, slots), BF16))
    top_shapes = (vector, ((width, width), BF16), ((width, slots), BF16), ((slots, width), BF16))
    plan = call(
        functools.partial(up_plan_kernel, sizes),
        "up_plan",
        (right_sides, inverses, couplings, widths, targets, buffer),
        5,
        up_shapes * (top - 1) + top_shapes,
        large,
        (
            pltpu.VMEM((levels, columns, width), BF16),
            pltpu.VMEM((top, width, width), BF16),
            pltpu.VMEM((top - 1, rows, width), BF16),
            pltpu.SMEM((levels,), jnp.int32),
            pltpu.VMEM(targets.shape, jnp.int32),
            pltpu.SemaphoreType.DMA((5,)),
        ),
    )
    states, products = [state], []
    for level in range(1, top):
        arrived = exchange(buffer, level - 1)
        mine = plan[4 * level - 4 : 4 * level]
        buffer, state = call(
            functools.partial(up_kernel, sizes), f"up_{level}", (arrived, *mine), 0, (message, vector), small
        )
        states.append(state)
        products.append(mine[1])
    arrived = exchange(buffer, top - 1)
    buffer, solved = call(
        functools.partial(top_kernel, sizes), "top", (arrived, *plan[-4:]), 0, (message, vector), small
    )
    down_shapes = (side, ((width, rows), BF16), ((rows, slots), BF16))
    plan = call(
        functools.partial(down_plan_kernel, sizes),
        "down_plan",
        (inverses, couplings, widths, targets, buffer, *states, *products),
        4,
        (*down_shapes, ((slots, width), BF16)) * (top - 1) + down_shapes,
        large,
        (
            pltpu.VMEM((top, width, width), BF16),
            pltpu.VMEM((rows, width), BF16),
            pltpu.SMEM((levels,), jnp.int32),
            pltpu.VMEM(targets.shape, jnp.int32),
            pltpu.SemaphoreType.DMA((4,)),
        ),
    )
    above = [solved]
    for level in reversed(range(1, top)):
        arrived = exchange(buffer, level)
        mine = plan[4 * level : 4 * level + 3]
        buffer, solved = call(
            functools.partial(down_kernel, sizes),
            f"down_{level}",
            (arrived, *mine, plan[4 * level - 1]),
            0,
            (message, vector),
            small,
        )
        above.insert(0, solved)
    arrived = exchange(buffer, 0)
    (out,) = call(
        functools.partial(last_kernel, sizes),
        "last",
        (arrived, *plan[:3], *above),
        0,
        ((right_sides.shape, BF16),),
        small,
        (pltpu.VMEM((levels, columns, width), BF16), pltpu.SemaphoreType.DMA((2,))),
        HBM,
    )
    return jnp.swapaxes(out, 3, 4)


def solution(mesh):
    groups, owners = mesh.devices.shape
    bits = groups.bit_length() - 1
    leaf_axes = tuple(f"leaf{bit}" for bit in reversed(range(bits)))
    split = Mesh(mesh.devices.reshape((2,) * bits + (owners,)), leaf_axes + ("blk",))
    return jax.shard_map(
        functools.partial(shards, leaf_axes),
        mesh=split,
        in_specs=(
            P(leaf_axes, "blk", None, None, None),
            P(leaf_axes, "blk", None, None, None),
            P(leaf_axes, "blk", None, None, None),
            P(leaf_axes, "blk", None),
            P(),
        ),
        out_specs=P(leaf_axes, "blk", None, None, None),
        check_vma=False,
    )
```

time: 87.6 us -> 75.3 us (0.86)
  blocking collectives: 0 us -> 40 us
  waiting for transfers between devices: 31.3 us -> 5.06 us
  local copies, waits for them, and re-layouts: 15.7 us -> 3.38 us
  starting transfers between devices: 20.2 us -> 9.88 us
  Pallas kernels: 19.4 us -> 16.4 us
    all_to_all x0 -> x4, blocking collectives: none -> 40 us  [exchange(): lax.all_to_all(blocks, (pair, 'blk'), split_axis=0, concat_axis=0, tiled=...]
    all_to_all x6 -> x2, waiting for transfers between devices: 31.3 us -> 5.06 us  [exchange(): lax.all_to_all(blocks, (pair, 'blk'), split_axis=0, concat_axis=0, tiled=...]
    unnamed x31 -> x16, local copies, waits for them, and re-layouts: 14.9 us -> 3.38 us
    all_to_all x6 -> x2, starting transfers between devices: 20.2 us -> 9.88 us  [exchange(): lax.all_to_all(blocks, (pair, 'blk'), split_axis=0, concat_axis=0, tiled=...]
    pallas_call x13 -> x9, Pallas kernels: 19.4 us -> 16.4 us  [call(): pl.pallas_call(kernel, in_specs=[HBM] * far + [VMEM] * (len(operands) - f...]
  transfers between devices with their start and end apart: 6 -> 2, of which waited for: 6 -> 2; matrix products, arithmetic and copies ran while one was open for 0% -> 0% of each run, Pallas kernels for 10% -> 10%
where the time goes in v2:
time: 75.3 us; the launch traced here: 74.9 us
  blocking collectives  40 us (53%)
  Pallas kernels  16.4 us (22%)
  starting transfers between devices  9.88 us (13%)
  waiting for transfers between devices  5.06 us (7%)
  local copies, waits for them, and re-layouts  3.38 us (4%)
    all_to_all x4, blocking collectives, exchange(): lax.all_to_all(blocks, (pair, 'blk'), split_axis=0, concat_axis=0, tiled=...  40 us
    pallas_call x9, Pallas kernels, call(): pl.pallas_call(kernel, in_specs=[HBM] * far + [VMEM] * (len(operands) - f...  16.4 us
    all_to_all x2, starting transfers between devices, exchange(): lax.all_to_all(blocks, (pair, 'blk'), split_axis=0, concat_axis=0, tiled=...  9.88 us
    all_to_all x2, waiting for transfers between devices, exchange(): lax.all_to_all(blocks, (pair, 'blk'), split_axis=0, concat_axis=0, tiled=...  5.06 us
    unnamed x16, local copies, waits for them, and re-layouts  3.38 us
  transfers between devices with their start and end apart: 2, of which 2 were waited for; matrix products, arithmetic and copies ran while one was open for 0% of the time, Pallas kernels for 10%

profile of v2, /device:TPU:0, one launch (start us, length us, event | category | flops | bytes accessed | tf_op | source)
XLA Modules:
  0.0 74.9 jit_solution(265536878399881522)
XLA Ops:
  0.0 2.6 %start.1 = (bf16[320,128]{1,0:T(8,128)(2,1)}, bf16[512,128]{1,0:T(8,128)(2,1)S(1)}) custom-call(bf16[1,1,4,32,512]{4,3,2,1,0:T(8,128)(2,1)} %bitcast.24, bf16[1,1,4,512,512]{4,3,2,1,0:T(8,128)(2,1)} %inverse.5, bf16[1,1,3,256,512]{4,3,2,1,0:T(8,128)(2,1)} %coupling.5, s32[1,1,4]{2,1,0:T(1,128)} %widths.5, s32[3,2,16,64]{3,2,1,0:T(8,128)} %targets.5), custom_call_target="tpu_custom_call" | custom-call | flops 1000000000 | bytes 1048576 | tf_op jit(solution)/shard_map/start/pallas_call | solution.py:307
  2.6 7.3 %all-to-all-start = ((bf16[160,2,128]{2,1,0:T(2,128)(2,1)}), bf16[160,2,128]{2,1,0:T(2,128)(2,1)S(1)}, u32[]{:S(2)}, u32[]{:S(2)}) async-start(bf16[160,2,128]{2,1,0:T(2,128)(2,1)} %bitcast.1), calls=%async_computation | async-start | bytes 163840 | tf_op jit(solution)/shard_map/all_to_all | solution.py:333
  9.9 3.9 %up_plan.1 = (bf16[512,128]{1,0:T(8,128)(2,1)S(1)}, bf16[256,512]{1,0:T(8,128)(2,1)S(1)}, bf16[320,256]{1,0:T(8,128)(2,1)S(1)}, bf16[512,320]{1,0:T(8,128)(2,1)S...) custom-call(bf16[1,1,4,32,512]{4,3,2,1,0:T(8,128)(2,1)} %bitcast.25,, ...), custom_call_target="tpu_custom_call" | custom-call | flops 1000000000 | bytes 1048576 | tf_op jit(solution)/shard_map/up_plan/pallas_call | solution.py:307
  13.8 0.0 copy-start.6
  13.8 0.6 copy-done.6
  14.5 3.1 %all-to-all-done = bf16[160,2,128]{2,1,0:T(2,128)(2,1)S(1)} async-done(((bf16[160,2,128]{2,1,0:T(2,128)(2,1)}), bf16[160,2,128]{2,1,0:T(2,128)(2,1)S(1)}, u32[]{:S(2)}, u32[]{:S(2)}) %all-to-all-start) | async-done | bytes 81952 | tf_op jit(solution)/shard_map/all_to_all | solution.py:333
  17.5 0.0 copy-start.7
  17.5 0.9 %copy-done.7 = bf16[512,128]{1,0:T(8,128)(2,1)S(1)} copy-done((bf16[512,128]{1,0:T(8,128)(2,1)S(1)}, bf16[512,128]{1,0:T(8,128)(2,1)}, u32[]{:S(2)}) %copy-start.7) | copy-done | bytes 131096
  18.4 0.9 %up_1.1 = (bf16[320,128]{1,0:T(8,128)(2,1)S(1)}, bf16[512,128]{1,0:T(8,128)(2,1)S(1)}) custom-call(bf16[320,128]{1,0:T(8,128)(2,1)S(1)} %bitcast.15, bf16[512,128]{1,0:T(8,128)(2,1)S(1)} %copy-done.7, bf16[256,512]{1,0:T(8,128)(2,1)S(1)} %get-tuple-element.42.product.refs_3_, bf16[320,256]{1,0:T(8,128)(2,1)S(1)} %get-tuple-element.43.sender, ...), custom_call_target="tpu_custom_call" | custom-call | flops 1000000 | bytes 1048576 | tf_op jit(solution)/shard_map/up_1/pallas_call | solution.py:307
  19.3 0.0 copy-start
  19.3 10.2 %all_to_all.30 = bf16[160,2,128]{2,1,0:T(2,128)(2,1)S(1)} all-to-all(bf16[160,2,128]{2,1,0:T(2,128)(2,1)S(1)} %bitcast.22), channel_id=1, replica_groups=mesh['leaf'=2,'blk'=16] {'leaf','blk'}, dimensions={0} | all-to-all | bytes 163840 | tf_op jit(solution)/shard_map/all_to_all | solution.py:333
  29.5 0.9 %up_2.1 = (bf16[320,128]{1,0:T(8,128)(2,1)S(1)}, bf16[512,128]{1,0:T(8,128)(2,1)S(1)}) custom-call(bf16[320,128]{1,0:T(8,128)(2,1)S(1)} %bitcast.18, bf16[512,128]{1,0:T(8,128)(2,1)S(1)} %get-tuple-element.46.side, bf16[256,512]{1,0:T(8,128)(2,1)S(1)} %get-tuple-element.47.product.refs_4_, bf16[320,256]{1,0:T(8,128)(2,1)S(1)} %get-tuple-element.48.sender, ...), custom_call_target="tpu_custom_call" | custom-call | flops 1000000 | bytes 1048576 | tf_op jit(solution)/shard_map/up_2/pallas_call | solution.py:307
  30.4 0.0 copy-start.2
  30.4 9.3 %all_to_all.31 = bf16[160,2,128]{2,1,0:T(2,128)(2,1)S(1)} all-to-all(bf16[160,2,128]{2,1,0:T(2,128)(2,1)S(1)} %bitcast.23), channel_id=1, replica_groups=mesh['leaf'=2,'blk'=16] {'leaf','blk'}, dimensions={0} | all-to-all | bytes 163840 | tf_op jit(solution)/shard_map/all_to_all | solution.py:333
  39.7 1.6 %top.1 = (bf16[320,128]{1,0:T(8,128)(2,1)}, bf16[512,128]{1,0:T(8,128)(2,1)S(1)}) custom-call(bf16[320,128]{1,0:T(8,128)(2,1)S(1)} %bitcast.16, bf16[512,128]{1,0:T(8,128)(2,1)S(1)} %get-tuple-element.51.side, bf16[512,512]{1,0:T(8,128)(2,1)S(1)} %get-tuple-element.52.product, bf16[512,320]{1,0:T(8,128)(2,1)S(1)} %get-tuple-element.53.taker, ...), custom_call_target="tpu_custom_call" | custom-call | flops 1000000 | bytes 1048576 | tf_op jit(solution)/shard_map/top/pallas_call | solution.py:307
  41.3 0.0 copy-start.4
  41.3 2.6 %all-to-all-start.3 = ((bf16[160,2,128]{2,1,0:T(2,128)(2,1)}), bf16[160,2,128]{2,1,0:T(2,128)(2,1)S(1)}, u32[]{:S(2)}, u32[]{:S(2)}) async-start(bf16[160,2,128]{2,1,0:T(2,128)(2,1)} %bitcast.7), calls=%async_computation.3 | async-start | bytes 163840 | tf_op jit(solution)/shard_map/all_to_all | solution.py:333
  43.9 0.0 copy-done
  43.9 0.0 copy-done.2
  43.9 0.0 copy-done.4
  43.9 0.0 copy-start.1
  43.9 0.9 %copy-done.1 = bf16[512,128]{1,0:T(8,128)(2,1)S(1)} copy-done((bf16[512,128]{1,0:T(8,128)(2,1)S(1)}, bf16[512,128]{1,0:T(8,128)(2,1)}, u32[]{:S(2)}) %copy-start.1) | copy-done | bytes 131096
  44.8 0.0 copy-start.3
  44.8 0.9 %copy-done.3 = bf16[512,128]{1,0:T(8,128)(2,1)S(1)} copy-done((bf16[512,128]{1,0:T(8,128)(2,1)S(1)}, bf16[512,128]{1,0:T(8,128)(2,1)}, u32[]{:S(2)}) %copy-start.3) | copy-done | bytes 131096
  45.7 3.7 %down_plan.1 = (f32[512,128]{1,0:T(8,128)S(1)}, bf16[512,256]{1,0:T(8,128)(2,1)S(1)}, bf16[256,320]{1,0:T(8,128)(2,1)S(1)}, bf16[320,512]{1,0:T(8,128)(2,1)S(1)}...) custom-call(bf16[1,1,4,512,512]{4,3,2,1,0:T(8,128)(2,1)} %inverse.5,, ...), custom_call_target="tpu_custom_call" | custom-call | flops 1000000000 | bytes 1048576 | tf_op jit(solution)/shard_map/down_plan/pallas_call | solution.py:307
  49.4 0.0 copy-start.5
  49.5 2.0 %all-to-all-done.3 = bf16[160,2,128]{2,1,0:T(2,128)(2,1)S(1)} async-done(((bf16[160,2,128]{2,1,0:T(2,128)(2,1)}), bf16[160,2,128]{2,1,0:T(2,128)(2,1)S(1)}, u32[]{:S(2)}, u32[]{:S(2)}) %all-to-all-start.3) | async-done | bytes 81952 | tf_op jit(solution)/shard_map/all_to_all | solution.py:333
  51.5 0.8 %down_2.1 = (bf16[320,128]{1,0:T(8,128)(2,1)S(1)}, bf16[512,128]{1,0:T(8,128)(2,1)S(1)}) custom-call(bf16[320,128]{1,0:T(8,128)(2,1)S(1)} %bitcast.14, f32[512,128]{1,0:T(8,128)S(1)} %get-tuple-element.59.side, bf16[512,256]{1,0:T(8,128)(2,1)S(1)} %get-tuple-element.60.product, bf16[256,320]{1,0:T(8,128)(2,1)S(1)} %get-tuple-element.61.picker, ...), custom_call_target="tpu_custom_call" | custom-call | flops 1000000 | bytes 1048576 | tf_op jit(solution)/shard_map/down_2/pallas_call | solution.py:307
  52.3 11.2 %all_to_all.32 = bf16[160,2,128]{2,1,0:T(2,128)(2,1)S(1)} all-to-all(bf16[160,2,128]{2,1,0:T(2,128)(2,1)S(1)} %bitcast.20), channel_id=1, replica_groups=mesh['leaf'=2,'blk'=16] {'leaf','blk'}, dimensions={0} | all-to-all | bytes 163840 | tf_op jit(solution)/shard_map/all_to_all | solution.py:333
  63.5 0.8 %down_1.1 = (bf16[320,128]{1,0:T(8,128)(2,1)S(1)}, bf16[512,128]{1,0:T(8,128)(2,1)S(1)}) custom-call(bf16[320,128]{1,0:T(8,128)(2,1)S(1)} %bitcast.17, f32[512,128]{1,0:T(8,128)S(1)} %get-tuple-element.64.side, bf16[512,256]{1,0:T(8,128)(2,1)S(1)} %get-tuple-element.65.product, bf16[256,320]{1,0:T(8,128)(2,1)S(1)} %get-tuple-element.66.picker, ...), custom_call_target="tpu_custom_call" | custom-call | flops 1000000 | bytes 1048576 | tf_op jit(solution)/shard_map/down_1/pallas_call | solution.py:307
  64.3 9.3 %all_to_all.33 = bf16[160,2,128]{2,1,0:T(2,128)(2,1)S(1)} all-to-all(bf16[160,2,128]{2,1,0:T(2,128)(2,1)S(1)} %bitcast.21), channel_id=1, replica_groups=mesh['leaf'=2,'blk'=16] {'leaf','blk'}, dimensions={0} | all-to-all | bytes 163840 | tf_op jit(solution)/shard_map/all_to_all | solution.py:333
  73.6 0.0 copy-done.5
  73.6 1.2 %last.1 = bf16[1,1,4,32,512]{4,3,2,1,0:T(8,128)(2,1)} custom-call(bf16[320,128]{1,0:T(8,128)(2,1)S(1)} %bitcast.19, f32[512,128]{1,0:T(8,128)S(1)} %get-tuple-element.69.side, bf16[512,256]{1,0:T(8,128)(2,1)S(1)} %get-tuple-element.70.product, bf16[256,320]{1,0:T(8,128)(2,1)S(1)} %get-tuple-element.71.picker, ...), custom_call_target="tpu_custom_call" | custom-call | flops 1000000 | bytes 1048576 | tf_op jit(solution)/shard_map/last/pallas_call | solution.py:307
Async XLA Ops:
  2.6 14.9 %all-to-all-start = ((bf16[160,2,128]{2,1,0:T(2,128)(2,1)}), bf16[160,2,128]{2,1,0:T(2,128)(2,1)S(1)}, u32[]{:S(2)}, u32[]{:S(2)}) async-start(bf16[160,2,128]{2,1,0:T(2,128)(2,1)} %bitcast.1), calls=%async_computation | async-start | bytes 163840 | tf_op jit(solution)/shard_map/all_to_all | solution.py:333
  13.8 0.7 copy-start.6
  17.5 0.9 %copy-start.7 = (bf16[512,128]{1,0:T(8,128)(2,1)S(1)}, bf16[512,128]{1,0:T(8,128)(2,1)}, u32[]{:S(2)}) copy-start(bf16[512,128]{1,0:T(8,128)(2,1)} %copy-done.6) | copy-start | bytes 393220
  19.3 24.6 %copy-start = (bf16[512,128]{1,0:T(8,128)(2,1)}, bf16[512,128]{1,0:T(8,128)(2,1)S(1)}, u32[]{:S(2)}) copy-start(bf16[512,128]{1,0:T(8,128)(2,1)S(1)} %get-tuple-element.57.refs_1_) | copy-start | bytes 393220
  30.4 13.5 %copy-start.2 = (bf16[512,128]{1,0:T(8,128)(2,1)}, bf16[512,128]{1,0:T(8,128)(2,1)S(1)}, u32[]{:S(2)}) copy-start(bf16[512,128]{1,0:T(8,128)(2,1)S(1)} %get-tuple-element.58.refs_2_) | copy-start | bytes 393220
  41.3 2.6 %copy-start.4 = (bf16[512,128]{1,0:T(8,128)(2,1)}, bf16[512,128]{1,0:T(8,128)(2,1)S(1)}, u32[]{:S(2)}) copy-start(bf16[512,128]{1,0:T(8,128)(2,1)S(1)} %get-tuple-element.74.refs_2_) | copy-start | bytes 393220
  41.3 10.2 %all-to-all-start.3 = ((bf16[160,2,128]{2,1,0:T(2,128)(2,1)}), bf16[160,2,128]{2,1,0:T(2,128)(2,1)S(1)}, u32[]{:S(2)}, u32[]{:S(2)}) async-start(bf16[160,2,128]{2,1,0:T(2,128)(2,1)} %bitcast.7), calls=%async_computation.3 | async-start | bytes 163840 | tf_op jit(solution)/shard_map/all_to_all | solution.py:333
  43.9 0.9 %copy-start.1 = (bf16[512,128]{1,0:T(8,128)(2,1)S(1)}, bf16[512,128]{1,0:T(8,128)(2,1)}, u32[]{:S(2)}) copy-start(bf16[512,128]{1,0:T(8,128)(2,1)} %copy-done) | copy-start | bytes 393220
  44.8 0.9 %copy-start.3 = (bf16[512,128]{1,0:T(8,128)(2,1)S(1)}, bf16[512,128]{1,0:T(8,128)(2,1)}, u32[]{:S(2)}) copy-start(bf16[512,128]{1,0:T(8,128)(2,1)} %copy-done.2) | copy-start | bytes 393220
  49.4 24.2 %copy-start.5 = (bf16[512,128]{1,0:T(8,128)(2,1)S(1)}, bf16[512,128]{1,0:T(8,128)(2,1)}, u32[]{:S(2)}) copy-start(bf16[512,128]{1,0:T(8,128)(2,1)} %copy-done.4) | copy-start | bytes 393220

commit v3 on v2

v3 whole, which is shorter than its diff:
```python
import functools

import jax
import jax.numpy as jnp
from jax import lax
from jax.experimental import pallas as pl
from jax.experimental.pallas import tpu as pltpu
from jax.sharding import Mesh, PartitionSpec as P

BLOCK = 128
LANES = 128
F32 = jnp.float32
BF16 = jnp.bfloat16


def iota(shape, axis):
    return lax.broadcasted_iota(jnp.int32, shape, axis)


def ones_where(condition):
    return jnp.where(condition, 1.0, 0.0).astype(BF16)


def dot(left, right):
    return jnp.dot(left, right, preferred_element_type=F32)


def trans_dot(left, right):
    return lax.dot_general(left, right, (((0,), (0,)), ((), ())), preferred_element_type=F32)


def over(value, size):
    if size & (size - 1):
        return value // size
    return lax.shift_right_logical(value, size.bit_length() - 1)


def within(value, size):
    if size & (size - 1):
        return value % size
    return jnp.bitwise_and(value, size - 1)


class Sizes:
    def __init__(self, right_sides, couplings, targets, leaf_axes):
        self.leaf_axes = leaf_axes
        self.owners = lax.axis_size("blk")
        self.levels, self.columns, self.width = right_sides.shape[-3:]
        self.rows = couplings.shape[-2]
        self.pieces = targets.shape[-1]
        self.leaf_bits = len(leaf_axes)
        self.sub = self.rows // self.pieces
        self.places = self.width // self.sub
        self.cap = max(3, (2 * self.pieces + self.owners - 1) // self.owners + 1)
        self.message = self.cap + self.cap % 2
        self.slots = 2 * self.owners * self.message


def live(widths, level, shape, axis):
    return iota(shape, axis) < widths[level] * BLOCK


def own_lanes(sizes, rows):
    shape = (rows, LANES)
    return over(iota(shape, 1), sizes.columns) == within(iota(shape, 0), sizes.sub)


def keep_own(sizes, value):
    return jnp.where(own_lanes(sizes, value.shape[0]), value, jnp.zeros_like(value))


def spread(sizes, value):
    value = keep_own(sizes, value)
    step = sizes.columns
    while step < LANES:
        value = value + pltpu.roll(value, step, 1)
        step *= 2
    return value


def repeat_columns(sizes, value):
    return jnp.concatenate([value] * (LANES // sizes.columns), axis=0).T


def position(sizes, level):
    group = 0
    for axis in sizes.leaf_axes:
        group = group * 2 + lax.axis_index(axis)
    return group, lax.axis_index("blk"), level % sizes.leaf_bits


def send_slots(sizes, level, targets):
    group, owner, bit = position(sizes, level)
    count = sizes.pieces
    table = targets[level, group]
    mine = jnp.sum(jnp.where(iota(table.shape, 0) == owner, table, 0), axis=0, keepdims=True)
    square = (count, count)
    keys_down = jnp.broadcast_to(over(mine, sizes.places), square)
    key_col = jnp.sum(jnp.where(iota(square, 0) == iota(square, 1), keys_down, 0).astype(F32), axis=1, keepdims=True)
    key_col = key_col.astype(jnp.int32)
    earlier = (keys_down == key_col) & (iota(square, 1) < iota(square, 0))
    rank = jnp.sum(jnp.where(earlier, 1.0, 0.0), axis=1, keepdims=True).astype(jnp.int32)
    side, dest = over(key_col, sizes.owners), within(key_col, sizes.owners)
    half = jnp.bitwise_xor(side, lax.shift_right_logical(group, bit) & 1)
    slot = (half * sizes.owners + dest) * sizes.message + rank
    shape = (count, sizes.rows)
    chosen = over(iota(shape, 1), sizes.sub) == iota(shape, 0)
    return jnp.sum(jnp.where(chosen, slot, 0).astype(F32), axis=0, keepdims=True).astype(jnp.int32)


def send_matrix(sizes, slots):
    return ones_where(iota((sizes.slots, sizes.rows), 0) == slots)


def take_places(sizes, level, targets):
    group, owner, bit = position(sizes, level)
    own_half = lax.shift_right_logical(group, bit) & 1
    first = group - own_half * 2**bit
    tables = []
    for half in range(2):
        codes = targets[level, first + half * 2**bit]
        wanted = jnp.bitwise_xor(own_half, half) * sizes.owners + owner
        tables.append(jnp.where(over(codes, sizes.places) == wanted, within(codes, sizes.places) + 1, 0))
    place = jnp.concatenate(tables, axis=0).astype(F32)
    square = (sizes.pieces, sizes.pieces)
    earlier = ones_where(iota(square, 0) < iota(square, 1))
    rank = dot(ones_where(place > 0), earlier)
    shape = (2 * sizes.owners, sizes.slots)
    offset = iota(shape, 1) - iota(shape, 0) * sizes.message
    spot = jnp.zeros(shape, F32)
    for each in range(sizes.cap):
        held = jnp.sum(jnp.where(rank == each, place, 0.0), axis=1, keepdims=True)
        spot = jnp.where(offset == each, held, spot)
    return jnp.sum(spot, axis=0, keepdims=True).astype(jnp.int32) - 1


def take_matrix(sizes, places):
    return ones_where(over(iota((sizes.width, sizes.slots), 0), sizes.sub) == places)


def coupled_inverse(sizes, level, widths, inverse, coupling):
    kept = jnp.where(live(widths, level, coupling.shape, 1), coupling, jnp.zeros_like(coupling))
    return dot(kept, inverse).astype(BF16)


def solve_forward(sizes, level, widths, inverse, residual):
    product = dot(inverse, residual)
    return jnp.where(live(widths, level, product.shape, 0), product, 0.0).astype(BF16)


def solve_backward(sizes, level, widths, inverse, side):
    product = trans_dot(inverse, side)
    return jnp.where(live(widths, level, product.shape, 0), product, 0.0)


def fetch(source, target, semaphore):
    copy = pltpu.make_async_copy(source, target, semaphore)
    copy.start()
    return copy


def squared_inverse(sizes, level, widths, inverse):
    kept = jnp.where(live(widths, level, inverse.shape, 0), inverse, jnp.zeros_like(inverse))
    product = trans_dot(inverse, kept)
    return jnp.where(live(widths, level, product.shape, 0), product, 0.0).astype(BF16)


def start_kernel(sizes, right, inverse, coupling, widths, targets, buffer, forward, *scratch):
    right_in, inverse_in, coupling_in, widths_in, targets_in, done = scratch
    copies = [
        fetch(targets.at[pl.ds(0, 1)], targets_in, done.at[0]),
        fetch(right.at[0, 0, 0], right_in, done.at[1]),
        fetch(widths.at[0, 0], widths_in, done.at[2]),
        fetch(inverse.at[0, 0, 0], inverse_in, done.at[3]),
        fetch(coupling.at[0, 0, 0], coupling_in, done.at[4]),
    ]
    copies[0].wait()
    sender = send_matrix(sizes, send_slots(sizes, 0, targets_in))
    copies[1].wait()
    residual = repeat_columns(sizes, right_in[...])
    copies[2].wait()
    copies[3].wait()
    solved = solve_forward(sizes, 0, widths_in, inverse_in[...], residual)
    forward[...] = solved
    copies[4].wait()
    pieces = keep_own(sizes, dot(coupling_in[...], solved).astype(BF16))
    buffer[...] = dot(sender, pieces).astype(BF16)


def plan_kernel(sizes, right, inverse, coupling, widths, targets, forward, *refs):
    top = sizes.levels - 1
    right_in, inverse_in, coupling_in, widths_in, targets_in, done = refs[-6:]
    sends, takes, limits, start = refs[:4]
    sides, squares = refs[4 : 4 + top], refs[4 + top : 4 + 2 * top]
    products = refs[4 + 2 * top : -6]
    copies = [
        fetch(targets, targets_in, done.at[0]),
        fetch(right.at[0, 0], right_in, done.at[1]),
        fetch(widths.at[0, 0], widths_in, done.at[2]),
        fetch(inverse.at[0, 0], inverse_in, done.at[3]),
        fetch(coupling.at[0, 0], coupling_in, done.at[4]),
    ]
    copies[0].wait()
    for level in range(top):
        sends[level] = send_slots(sizes, level, targets_in)
        takes[level] = take_places(sizes, level, targets_in)
    for copy in copies[1:]:
        copy.wait()
    for level in range(sizes.levels):
        limits[level] = jnp.full((1, LANES), widths_in[level] * BLOCK, jnp.int32)
    for level in range(1, top + 1):
        sides[level - 1][...] = repeat_columns(sizes, right_in[level])
        squares[level - 1][...] = squared_inverse(sizes, level, widths_in, inverse_in[level])
    for level in range(top):
        products[level][...] = coupled_inverse(sizes, level, widths_in, inverse_in[level], coupling_in[level])
    start[...] = solve_backward(sizes, 0, widths_in, inverse_in[0], forward[...]).astype(BF16)


def residual_of(sizes, level, arrived, side, takes):
    incoming = spread(sizes, dot(take_matrix(sizes, takes[level - 1]), arrived[...]))
    return (side[...].astype(F32) - incoming).astype(BF16)


def up_kernel(sizes, level, arrived, side, square, product, sends, takes, buffer, start):
    residual = residual_of(sizes, level, arrived, side, takes)
    pieces = keep_own(sizes, dot(product[...], residual).astype(BF16))
    buffer[...] = dot(send_matrix(sizes, sends[level]), pieces).astype(BF16)
    start[...] = dot(square[...], residual).astype(BF16)


def reply(sizes, level, value, takes):
    return trans_dot(take_matrix(sizes, takes[level - 1]), keep_own(sizes, value)).astype(BF16)


def top_kernel(sizes, level, arrived, side, square, takes, buffer, solved):
    residual = residual_of(sizes, level, arrived, side, takes)
    value = dot(square[...], residual).astype(BF16)
    buffer[...] = reply(sizes, level, value, takes)
    solved[...] = value


def solution_of(sizes, level, arrived, start, product, sends, limits):
    gathered = spread(sizes, trans_dot(send_matrix(sizes, sends[level]), arrived[...])).astype(BF16)
    update = trans_dot(product[...], gathered)
    update = jnp.where(iota(update.shape, 0) < limits[level], update, 0.0)
    return (start[...].astype(F32) - update).astype(BF16)


def down_kernel(sizes, level, arrived, start, product, sends, limits, takes, buffer, solved):
    value = solution_of(sizes, level, arrived, start, product, sends, limits)
    buffer[...] = reply(sizes, level, value, takes)
    solved[...] = value


def last_kernel(sizes, arrived, start, product, sends, limits, *refs):
    above, out, held, done = refs[:-3], refs[-3], refs[-2], refs[-1]
    count = len(above)
    for level in range(count):
        held[level + 1] = above[level][...].T[: sizes.columns]
    early = fetch(held.at[pl.ds(1, count)], out.at[0, 0, pl.ds(1, count)], done.at[0])
    held[0] = solution_of(sizes, 0, arrived, start, product, sends, limits).T[: sizes.columns]
    late = fetch(held.at[0], out.at[0, 0, 0], done.at[1])
    early.wait()
    late.wait()


VMEM = pl.BlockSpec(memory_space=pltpu.VMEM)
HBM = pl.BlockSpec(memory_space=pltpu.HBM)


def call(kernel, name, operands, far, outs, cost, scratch=(), out_spec=VMEM):
    held = [pltpu.with_memory_space_constraint(one, pltpu.HBM) for one in operands[:far]]
    operands = (*held, *operands[far:])
    return pl.pallas_call(
        kernel,
        in_specs=[HBM] * far + [VMEM] * (len(operands) - far),
        out_specs=[out_spec] * len(outs),
        out_shape=[jax.ShapeDtypeStruct(shape, kind) for shape, kind in outs],
        scratch_shapes=scratch,
        compiler_params=pltpu.CompilerParams(vmem_limit_bytes=24 * 2**20),
        cost_estimate=pl.CostEstimate(flops=cost, bytes_accessed=2**20, transcendentals=0),
        name=name,
    )(*operands)


def shards(leaf_axes, right_sides, inverses, couplings, widths, targets):
    right_sides = jnp.swapaxes(right_sides, 3, 4)
    sizes = Sizes(right_sides, couplings, targets, leaf_axes)
    width, slots, rows, columns, levels = sizes.width, sizes.slots, sizes.rows, sizes.columns, sizes.levels
    top = levels - 1
    vector = ((width, LANES), BF16)
    message = ((slots, LANES), BF16)
    matrix = ((width, width), BF16)
    coupled = ((rows, width), BF16)
    small, large = 10**6, 10**9

    def exchange(buffer, level):
        pair = leaf_axes[len(leaf_axes) - 1 - level % sizes.leaf_bits]
        blocks = buffer.reshape(slots // 2, 2, LANES)
        moved = lax.all_to_all(blocks, (pair, "blk"), split_axis=0, concat_axis=0, tiled=True)
        return moved.reshape(slots, LANES)

    inputs = (right_sides, inverses, couplings, widths, targets)
    buffer, forward = call(
        functools.partial(start_kernel, sizes),
        "start",
        inputs,
        5,
        (message, vector),
        large,
        (
            pltpu.VMEM((columns, width), BF16),
            pltpu.VMEM((width, width), BF16),
            pltpu.VMEM((rows, width), BF16),
            pltpu.SMEM((levels,), jnp.int32),
            pltpu.VMEM((1, *targets.shape[1:]), jnp.int32),
            pltpu.SemaphoreType.DMA((5,)),
        ),
    )
    sends, takes, limits, start, *planned = call(
        functools.partial(plan_kernel, sizes),
        "plan",
        (*inputs, forward),
        5,
        (
            ((top, 1, rows), jnp.int32),
            ((top, 1, slots), jnp.int32),
            ((levels, 1, LANES), jnp.int32),
            vector,
            *(vector,) * top,
            *(matrix,) * top,
            *(coupled,) * top,
        ),
        large,
        (
            pltpu.VMEM((levels, columns, width), BF16),
            pltpu.VMEM((levels, width, width), BF16),
            pltpu.VMEM((top, rows, width), BF16),
            pltpu.SMEM((levels,), jnp.int32),
            pltpu.VMEM(targets.shape, jnp.int32),
            pltpu.SemaphoreType.DMA((5,)),
        ),
    )
    sides, squares, products = planned[:top], planned[top : 2 * top], planned[2 * top :]
    starts = [start]
    for level in range(1, top):
        arrived = exchange(buffer, level - 1)
        buffer, start = call(
            functools.partial(up_kernel, sizes, level),
            f"up_{level}",
            (arrived, sides[level - 1], squares[level - 1], products[level], sends, takes),
            0,
            (message, vector),
            small,
        )
        starts.append(start)
    arrived = exchange(buffer, top - 1)
    buffer, solved = call(
        functools.partial(top_kernel, sizes, top),
        "top",
        (arrived, sides[-1], squares[-1], takes),
        0,
        (message, vector),
        small,
    )
    above = [solved]
    for level in reversed(range(1, top)):
        arrived = exchange(buffer, level)
        buffer, solved = call(
            functools.partial(down_kernel, sizes, level),
            f"down_{level}",
            (arrived, starts[level], products[level], sends, limits, takes),
            0,
            (message, vector),
            small,
        )
        above.insert(0, solved)
    arrived = exchange(buffer, 0)
    (out,) = call(
        functools.partial(last_kernel, sizes),
        "last",
        (arrived, starts[0], products[0], sends, limits, *above),
        0,
        ((right_sides.shape, BF16),),
        small,
        (pltpu.VMEM((levels, columns, width), BF16), pltpu.SemaphoreType.DMA((2,))),
        HBM,
    )
    return jnp.swapaxes(out, 3, 4)


def solution(mesh):
    groups, owners = mesh.devices.shape
    bits = groups.bit_length() - 1
    leaf_axes = tuple(f"leaf{bit}" for bit in reversed(range(bits)))
    split = Mesh(mesh.devices.reshape((2,) * bits + (owners,)), leaf_axes + ("blk",))
    return jax.shard_map(
        functools.partial(shards, leaf_axes),
        mesh=split,
        in_specs=(
            P(leaf_axes, "blk", None, None, None),
            P(leaf_axes, "blk", None, None, None),
            P(leaf_axes, "blk", None, None, None),
            P(leaf_axes, "blk", None),
            P(),
        ),
        out_specs=P(leaf_axes, "blk", None, None, None),
        check_vma=False,
    )
```

time: 75.3 us -> 70.4 us (0.935)
  blocking collectives: 40 us -> 46.5 us
  Pallas kernels: 16.4 us -> 12.1 us
  local copies, waits for them, and re-layouts: 3.38 us -> 0 us
  starting transfers between devices: 9.88 us -> 7.3 us
  waiting for transfers between devices: 5.06 us -> 4.11 us
    all_to_all x4 -> x5, blocking collectives: 40 us -> 46.5 us  [exchange(): lax.all_to_all(blocks, (pair, 'blk'), split_axis=0, concat_axis=0, tiled=...]
    pallas_call x9 -> x8, Pallas kernels: 16.4 us -> 12.1 us  [call(): pl.pallas_call(kernel, in_specs=[HBM] * far + [VMEM] * (len(operands) - f...]
    unnamed x16 -> x0, local copies, waits for them, and re-layouts: 3.38 us -> none
    all_to_all x2 -> x1, starting transfers between devices: 9.88 us -> 7.3 us  [exchange(): lax.all_to_all(blocks, (pair, 'blk'), split_axis=0, concat_axis=0, tiled=...]
    all_to_all x2 -> x1, waiting for transfers between devices: 5.06 us -> 4.11 us  [exchange(): lax.all_to_all(blocks, (pair, 'blk'), split_axis=0, concat_axis=0, tiled=...]
  transfers between devices with their start and end apart: 2 -> 1, of which waited for: 2 -> 1; matrix products, arithmetic and copies ran while one was open for 0% -> 0% of each run, Pallas kernels for 10% -> 5%
where the time goes in v3:
time: 70.4 us; the launch traced here: 70 us
  blocking collectives  46.5 us (66%)
  Pallas kernels  12.1 us (17%)
  starting transfers between devices  7.3 us (10%)
  waiting for transfers between devices  4.11 us (6%)
    all_to_all x5, blocking collectives, exchange(): lax.all_to_all(blocks, (pair, 'blk'), split_axis=0, concat_axis=0, tiled=...  46.5 us
    pallas_call x8, Pallas kernels, call(): pl.pallas_call(kernel, in_specs=[HBM] * far + [VMEM] * (len(operands) - f...  12.1 us
    all_to_all x1, starting transfers between devices, exchange(): lax.all_to_all(blocks, (pair, 'blk'), split_axis=0, concat_axis=0, tiled=...  7.3 us
    all_to_all x1, waiting for transfers between devices, exchange(): lax.all_to_all(blocks, (pair, 'blk'), split_axis=0, concat_axis=0, tiled=...  4.11 us
  transfers between devices with their start and end apart: 1, of which 1 were waited for; matrix products, arithmetic and copies ran while one was open for 0% of the time, Pallas kernels for 5%

profile of v3, /device:TPU:0, one launch (start us, length us, event | category | flops | bytes accessed | tf_op | source)
XLA Modules:
  0.0 70.0 jit_solution(712901375324778621)
XLA Ops:
  0.0 2.6 %start.1 = (bf16[320,128]{1,0:T(8,128)(2,1)}, bf16[512,128]{1,0:T(8,128)(2,1)S(1)}) custom-call(bf16[1,1,4,32,512]{4,3,2,1,0:T(8,128)(2,1)} %bitcast.25, bf16[1,1,4,512,512]{4,3,2,1,0:T(8,128)(2,1)} %inverse.3, bf16[1,1,3,256,512]{4,3,2,1,0:T(8,128)(2,1)} %coupling.3, s32[1,1,4]{2,1,0:T(1,128)} %widths.3, s32[3,2,16,64]{3,2,1,0:T(8,128)} %targets.3), custom_call_target="tpu_custom_call" | custom-call | flops 1000000000 | bytes 1048576 | tf_op jit(solution)/shard_map/start/pallas_call | solution.py:274
  2.6 7.3 %all-to-all-start = ((bf16[160,2,128]{2,1,0:T(2,128)(2,1)}), bf16[160,2,128]{2,1,0:T(2,128)(2,1)S(1)}, u32[]{:S(2)}, u32[]{:S(2)}) async-start(bf16[160,2,128]{2,1,0:T(2,128)(2,1)} %bitcast.1), calls=%async_computation | async-start | bytes 163840 | tf_op jit(solution)/shard_map/all_to_all | solution.py:300
  9.9 3.5 %plan.1 = (s32[3,1,256]{2,1,0:T(1,128)S(1)}, s32[3,1,320]{2,1,0:T(1,128)S(1)}, s32[4,1,128]{2,1,0:T(1,128)S(1)}, bf16[512,128]{1,0:T(8,128)(2,1)S(1)}, bf16[512,...) custom-call(bf16[1,1,4,32,512]{4,3,2,1,0:T(8,128)(2,1)} %bitcast.26,, ...), custom_call_target="tpu_custom_call" | custom-call | flops 1000000000 | bytes 1048576 | tf_op jit(solution)/shard_map/plan/pallas_call | solution.py:274
  13.4 4.1 %all-to-all-done = bf16[160,2,128]{2,1,0:T(2,128)(2,1)S(1)} async-done(((bf16[160,2,128]{2,1,0:T(2,128)(2,1)}), bf16[160,2,128]{2,1,0:T(2,128)(2,1)S(1)}, u32[]{:S(2)}, u32[]{:S(2)}) %all-to-all-start) | async-done | bytes 81952 | tf_op jit(solution)/shard_map/all_to_all | solution.py:300
  17.5 1.0 %up_1.1 = (bf16[320,128]{1,0:T(8,128)(2,1)S(1)}, bf16[512,128]{1,0:T(8,128)(2,1)S(1)}) custom-call(bf16[320,128]{1,0:T(8,128)(2,1)S(1)} %bitcast.14, bf16[512,128]{1,0:T(8,128)(2,1)S(1)} %get-tuple-element.32.side, bf16[512,512]{1,0:T(8,128)(2,1)S(1)} %get-tuple-element.33.square, bf16[256,512]{1,0:T(8,128)(2,1)S(1)} %get-tuple-element.34.product, ...), custom_call_target="tpu_custom_call" | custom-call | flops 1000000 | bytes 1048576 | tf_op jit(solution)/shard_map/up_1/pallas_call | solution.py:274
  18.5 9.3 %all_to_all.30 = bf16[160,2,128]{2,1,0:T(2,128)(2,1)S(1)} all-to-all(bf16[160,2,128]{2,1,0:T(2,128)(2,1)S(1)} %bitcast.21), channel_id=1, replica_groups=mesh['leaf'=2,'blk'=16] {'leaf','blk'}, dimensions={0} | all-to-all | bytes 163840 | tf_op jit(solution)/shard_map/all_to_all | solution.py:300
  27.8 1.0 %up_2.1 = (bf16[320,128]{1,0:T(8,128)(2,1)S(1)}, bf16[512,128]{1,0:T(8,128)(2,1)S(1)}) custom-call(bf16[320,128]{1,0:T(8,128)(2,1)S(1)} %bitcast.16, bf16[512,128]{1,0:T(8,128)(2,1)S(1)} %get-tuple-element.38.side, bf16[512,512]{1,0:T(8,128)(2,1)S(1)} %get-tuple-element.39.square, bf16[256,512]{1,0:T(8,128)(2,1)S(1)} %get-tuple-element.40.product, ...), custom_call_target="tpu_custom_call" | custom-call | flops 1000000 | bytes 1048576 | tf_op jit(solution)/shard_map/up_2/pallas_call | solution.py:274
  28.9 9.3 %all_to_all.31 = bf16[160,2,128]{2,1,0:T(2,128)(2,1)S(1)} all-to-all(bf16[160,2,128]{2,1,0:T(2,128)(2,1)S(1)} %bitcast.22), channel_id=1, replica_groups=mesh['leaf'=2,'blk'=16] {'leaf','blk'}, dimensions={0} | all-to-all | bytes 163840 | tf_op jit(solution)/shard_map/all_to_all | solution.py:300
  38.2 1.0 %top.1 = (bf16[320,128]{1,0:T(8,128)(2,1)S(1)}, bf16[512,128]{1,0:T(8,128)(2,1)S(1)}) custom-call(bf16[320,128]{1,0:T(8,128)(2,1)S(1)} %bitcast.17, bf16[512,128]{1,0:T(8,128)(2,1)S(1)} %get-tuple-element.42.side, bf16[512,512]{1,0:T(8,128)(2,1)S(1)} %get-tuple-element.43.square, s32[3,1,320]{2,1,0:T(1,128)S(1)} %get-tuple-element.36.takes), custom_call_target="tpu_custom_call" | custom-call | flops 1000000 | bytes 1048576 | tf_op jit(solution)/shard_map/top/pallas_call | solution.py:274
  39.1 9.3 %all_to_all.32 = bf16[160,2,128]{2,1,0:T(2,128)(2,1)S(1)} all-to-all(bf16[160,2,128]{2,1,0:T(2,128)(2,1)S(1)} %bitcast.23), channel_id=1, replica_groups=mesh['leaf'=2,'blk'=16] {'leaf','blk'}, dimensions={0} | all-to-all | bytes 163840 | tf_op jit(solution)/shard_map/all_to_all | solution.py:300
  48.4 0.9 %down_2.1 = (bf16[320,128]{1,0:T(8,128)(2,1)S(1)}, bf16[512,128]{1,0:T(8,128)(2,1)S(1)}) custom-call(bf16[320,128]{1,0:T(8,128)(2,1)S(1)} %bitcast.19, bf16[512,128]{1,0:T(8,128)(2,1)S(1)} %get-tuple-element.45.start, bf16[256,512]{1,0:T(8,128)(2,1)S(1)} %get-tuple-element.40.product, s32[3,1,256]{2,1,0:T(1,128)S(1)} %get-tuple-element.35.sends, ...), custom_call_target="tpu_custom_call" | custom-call | flops 1000000 | bytes 1048576 | tf_op jit(solution)/shard_map/down_2/pallas_call | solution.py:274
  49.3 9.3 %all_to_all.33 = bf16[160,2,128]{2,1,0:T(2,128)(2,1)S(1)} all-to-all(bf16[160,2,128]{2,1,0:T(2,128)(2,1)S(1)} %bitcast.24), channel_id=1, replica_groups=mesh['leaf'=2,'blk'=16] {'leaf','blk'}, dimensions={0} | all-to-all | bytes 163840 | tf_op jit(solution)/shard_map/all_to_all | solution.py:300
  58.6 0.9 %down_1.1 = (bf16[320,128]{1,0:T(8,128)(2,1)S(1)}, bf16[512,128]{1,0:T(8,128)(2,1)S(1)}) custom-call(bf16[320,128]{1,0:T(8,128)(2,1)S(1)} %bitcast.18, bf16[512,128]{1,0:T(8,128)(2,1)S(1)} %get-tuple-element.48.start, bf16[256,512]{1,0:T(8,128)(2,1)S(1)} %get-tuple-element.34.product, s32[3,1,256]{2,1,0:T(1,128)S(1)} %get-tuple-element.35.sends, ...), custom_call_target="tpu_custom_call" | custom-call | flops 1000000 | bytes 1048576 | tf_op jit(solution)/shard_map/down_1/pallas_call | solution.py:274
  59.4 9.3 %all_to_all.34 = bf16[160,2,128]{2,1,0:T(2,128)(2,1)S(1)} all-to-all(bf16[160,2,128]{2,1,0:T(2,128)(2,1)S(1)} %bitcast.20), channel_id=1, replica_groups=mesh['leaf'=2,'blk'=16] {'leaf','blk'}, dimensions={0} | all-to-all | bytes 163840 | tf_op jit(solution)/shard_map/all_to_all | solution.py:300
  68.7 1.3 %last.1 = bf16[1,1,4,32,512]{4,3,2,1,0:T(8,128)(2,1)} custom-call(bf16[320,128]{1,0:T(8,128)(2,1)S(1)} %bitcast.15, bf16[512,128]{1,0:T(8,128)(2,1)S(1)} %get-tuple-element.50.start, bf16[256,512]{1,0:T(8,128)(2,1)S(1)} %get-tuple-element.51.product, s32[3,1,256]{2,1,0:T(1,128)S(1)} %get-tuple-element.35.sends, s32[4,1,128]{2,1,0:T(1,128)S(1)} %get-tuple-element.46.limits, ...), custom_call_target="tpu_custom_call" | custom-call | flops 1000000 | bytes 1048576 | tf_op jit(solution)/shard_map/last/pallas_call | solution.py:274
Async XLA Ops:
  2.6 14.9 %all-to-all-start = ((bf16[160,2,128]{2,1,0:T(2,128)(2,1)}), bf16[160,2,128]{2,1,0:T(2,128)(2,1)S(1)}, u32[]{:S(2)}, u32[]{:S(2)}) async-start(bf16[160,2,128]{2,1,0:T(2,128)(2,1)} %bitcast.1), calls=%async_computation | async-start | bytes 163840 | tf_op jit(solution)/shard_map/all_to_all | solution.py:300

commit v4 on v3

v4 whole, which is shorter than its diff:
```python
import functools

import jax
import jax.numpy as jnp
from jax import lax
from jax.experimental import pallas as pl
from jax.experimental.pallas import tpu as pltpu
from jax.sharding import Mesh, PartitionSpec as P

BLOCK = 128
LANES = 128
F32 = jnp.float32
BF16 = jnp.bfloat16


def iota(shape, axis):
    return lax.broadcasted_iota(jnp.int32, shape, axis)


def ones_where(condition):
    return jnp.where(condition, 1.0, 0.0).astype(BF16)


def dot(left, right):
    return jnp.dot(left, right, preferred_element_type=F32)


def trans_dot(left, right):
    return lax.dot_general(left, right, (((0,), (0,)), ((), ())), preferred_element_type=F32)


def over(value, size):
    if size & (size - 1):
        return value // size
    return lax.shift_right_logical(value, size.bit_length() - 1)


def within(value, size):
    if size & (size - 1):
        return value % size
    return jnp.bitwise_and(value, size - 1)


class Sizes:
    def __init__(self, right_sides, couplings, targets, leaf_axes):
        self.leaf_axes = leaf_axes
        self.near, self.far = lax.axis_size("near"), lax.axis_size("far")
        self.owners = self.near * self.far
        self.levels, self.columns, self.width = right_sides.shape[-3:]
        self.rows = couplings.shape[-2]
        self.pieces = targets.shape[-1]
        self.leaf_bits = len(leaf_axes)
        self.sub = self.rows // self.pieces
        self.places = self.width // self.sub
        self.cap = max(3, (2 * self.pieces + self.owners - 1) // self.owners + 1)
        self.message = self.cap + self.cap % 2
        self.slots = 2 * self.owners * self.message


def live(limits, level, shape, axis):
    return iota(shape, axis) < limits[level][:, :1]


def own_lanes(sizes, rows):
    shape = (rows, LANES)
    return over(iota(shape, 1), sizes.columns) == within(iota(shape, 0), sizes.sub)


def keep_own(sizes, value):
    return jnp.where(own_lanes(sizes, value.shape[0]), value, jnp.zeros_like(value))


def spread(sizes, value):
    value = keep_own(sizes, value)
    step = sizes.columns
    while step < LANES:
        value = value + pltpu.roll(value, step, 1)
        step *= 2
    return value


def repeat_columns(sizes, value):
    return jnp.concatenate([value] * (LANES // sizes.columns), axis=0).T


def position(sizes, level):
    group = 0
    for axis in sizes.leaf_axes:
        group = group * 2 + lax.axis_index(axis)
    owner = lax.axis_index("far") * sizes.near + lax.axis_index("near")
    return group, owner, level % sizes.leaf_bits


def turn(sizes, half, owner):
    return (within(owner, sizes.near) * 2 + half) * sizes.far + over(owner, sizes.near)


def send_slots(sizes, level, targets):
    group, owner, bit = position(sizes, level)
    count = sizes.pieces
    table = targets[level, group]
    mine = jnp.sum(jnp.where(iota(table.shape, 0) == owner, table, 0), axis=0, keepdims=True)
    square = (count, count)
    keys_down = jnp.broadcast_to(over(mine, sizes.places), square)
    key_col = jnp.sum(jnp.where(iota(square, 0) == iota(square, 1), keys_down, 0).astype(F32), axis=1, keepdims=True)
    key_col = key_col.astype(jnp.int32)
    earlier = (keys_down == key_col) & (iota(square, 1) < iota(square, 0))
    rank = jnp.sum(jnp.where(earlier, 1.0, 0.0), axis=1, keepdims=True).astype(jnp.int32)
    side, dest = over(key_col, sizes.owners), within(key_col, sizes.owners)
    half = jnp.bitwise_xor(side, lax.shift_right_logical(group, bit) & 1)
    slot = turn(sizes, half, dest) * sizes.message + rank
    shape = (count, sizes.rows)
    chosen = over(iota(shape, 1), sizes.sub) == iota(shape, 0)
    return jnp.sum(jnp.where(chosen, slot, 0).astype(F32), axis=0, keepdims=True).astype(jnp.int32)


def send_matrix(sizes, slots):
    return ones_where(iota((sizes.slots, sizes.rows), 0) == slots)


def take_places(sizes, level, targets):
    group, owner, bit = position(sizes, level)
    own_half = lax.shift_right_logical(group, bit) & 1
    first = group - own_half * 2**bit
    tables = []
    for half in range(2):
        codes = targets[level, first + half * 2**bit]
        wanted = jnp.bitwise_xor(own_half, half) * sizes.owners + owner
        tables.append(jnp.where(over(codes, sizes.places) == wanted, within(codes, sizes.places) + 1, 0))
    place = jnp.concatenate(tables, axis=0).astype(F32)
    square = (sizes.pieces, sizes.pieces)
    earlier = ones_where(iota(square, 0) < iota(square, 1))
    rank = dot(ones_where(place > 0), earlier)
    shape = (2 * sizes.owners, sizes.slots)
    source = iota(shape, 0)
    source = turn(sizes, over(source, sizes.owners), within(source, sizes.owners))
    offset = iota(shape, 1) - source * sizes.message
    spot = jnp.zeros(shape, F32)
    for each in range(sizes.cap):
        held = jnp.sum(jnp.where(rank == each, place, 0.0), axis=1, keepdims=True)
        spot = jnp.where(offset == each, held, spot)
    return jnp.sum(spot, axis=0, keepdims=True).astype(jnp.int32) - 1


def take_matrix(sizes, places):
    return ones_where(over(iota((sizes.width, sizes.slots), 0), sizes.sub) == places)


def coupled_inverse(sizes, level, limits, inverse, coupling):
    kept = jnp.where(live(limits, level, coupling.shape, 1), coupling, jnp.zeros_like(coupling))
    return dot(kept, inverse).astype(BF16)


def solve_forward(sizes, level, limits, inverse, residual):
    product = dot(inverse, residual)
    return jnp.where(live(limits, level, product.shape, 0), product, 0.0).astype(BF16)


def solve_backward(sizes, level, limits, inverse, side):
    product = trans_dot(inverse, side)
    return jnp.where(live(limits, level, product.shape, 0), product, 0.0)


def fetch(source, target, semaphore):
    copy = pltpu.make_async_copy(source, target, semaphore)
    copy.start()
    return copy


def squared_inverse(sizes, level, limits, inverse):
    kept = jnp.where(live(limits, level, inverse.shape, 0), inverse, jnp.zeros_like(inverse))
    product = trans_dot(inverse, kept)
    return jnp.where(live(limits, level, product.shape, 0), product, 0.0).astype(BF16)


def start_kernel(sizes, right, inverse, coupling, widths, targets, buffer, forward, limits, *refs):
    right_in, inverse_in, coupling_in, targets_in, widths_in, done = refs
    top = sizes.levels - 1
    first, others = pl.ds(0, 1), pl.ds(1, top)
    copies = [
        fetch(targets, targets_in, done.at[0]),
        fetch(right.at[0, 0], right_in, done.at[1]),
        fetch(widths.at[0, 0], widths_in, done.at[2]),
        fetch(inverse.at[0, 0, first], inverse_in.at[first], done.at[3]),
        fetch(coupling.at[0, 0, first], coupling_in.at[first], done.at[4]),
        fetch(inverse.at[0, 0, others], inverse_in.at[others], done.at[5]),
        fetch(coupling.at[0, 0, pl.ds(1, top - 1)], coupling_in.at[pl.ds(1, top - 1)], done.at[6]),
    ]
    copies[0].wait()
    sender = send_matrix(sizes, send_slots(sizes, 0, targets_in))
    copies[1].wait()
    residual = repeat_columns(sizes, right_in[0])
    copies[2].wait()
    for level in range(sizes.levels):
        limits[level] = jnp.full((1, LANES), widths_in[level] * BLOCK, jnp.int32)
    copies[3].wait()
    solved = solve_forward(sizes, 0, limits, inverse_in[0], residual)
    forward[...] = solved
    copies[4].wait()
    pieces = keep_own(sizes, dot(coupling_in[0], solved).astype(BF16))
    buffer[...] = dot(sender, pieces).astype(BF16)
    copies[5].wait()
    copies[6].wait()


def plan_kernel(sizes, forward, limits, right, inverse, coupling, targets, *refs):
    top = sizes.levels - 1
    sends, takes, start, first, last = refs[:5]
    sides, stacks = refs[5 : 5 + top], refs[5 + top :]
    for level in range(1, top + 1):
        sides[level - 1][...] = repeat_columns(sizes, right[level])
    for level in range(top):
        product = coupled_inverse(sizes, level, limits, inverse[level], coupling[level])
        if level == 0:
            first[...] = product
        else:
            stacks[level - 1][pl.ds(0, sizes.rows)] = product
            stacks[level - 1][pl.ds(sizes.rows, sizes.width)] = squared_inverse(sizes, level, limits, inverse[level])
    last[...] = squared_inverse(sizes, top, limits, inverse[top])
    start[...] = solve_backward(sizes, 0, limits, inverse[0], forward[...]).astype(BF16)
    for level in range(top):
        sends[level] = send_slots(sizes, level, targets)
        takes[level] = take_places(sizes, level, targets)


def residual_of(sizes, level, arrived, side, takes):
    incoming = spread(sizes, dot(take_matrix(sizes, takes[level - 1]), arrived[...]))
    return (side[...].astype(F32) - incoming).astype(BF16)


def up_kernel(sizes, level, arrived, side, stack, sends, takes, buffer, start):
    residual = residual_of(sizes, level, arrived, side, takes)
    both = dot(stack[...], residual)
    pieces = keep_own(sizes, both[: sizes.rows].astype(BF16))
    buffer[...] = dot(send_matrix(sizes, sends[level]), pieces).astype(BF16)
    start[...] = both[sizes.rows :].astype(BF16)


def reply(sizes, level, value, takes):
    return trans_dot(take_matrix(sizes, takes[level - 1]), keep_own(sizes, value)).astype(BF16)


def top_kernel(sizes, level, arrived, side, square, takes, buffer, solved):
    residual = residual_of(sizes, level, arrived, side, takes)
    value = dot(square[...], residual).astype(BF16)
    buffer[...] = reply(sizes, level, value, takes)
    solved[...] = value


def solution_of(sizes, level, arrived, start, product, sends, limits):
    gathered = spread(sizes, trans_dot(send_matrix(sizes, sends[level]), arrived[...])).astype(BF16)
    update = trans_dot(product, gathered)
    update = jnp.where(live(limits, level, update.shape, 0), update, 0.0)
    return (start[...].astype(F32) - update).astype(BF16)


def down_kernel(sizes, level, arrived, start, product, sends, limits, takes, buffer, solved):
    value = solution_of(sizes, level, arrived, start, product[: sizes.rows], sends, limits)
    buffer[...] = reply(sizes, level, value, takes)
    solved[...] = value


def last_kernel(sizes, arrived, start, product, sends, limits, *refs):
    above, out, held, done = refs[:-3], refs[-3], refs[-2], refs[-1]
    count = len(above)
    for level in range(count):
        held[level + 1] = above[level][...].T[: sizes.columns]
    early = fetch(held.at[pl.ds(1, count)], out.at[0, 0, pl.ds(1, count)], done.at[0])
    held[0] = solution_of(sizes, 0, arrived, start, product[...], sends, limits).T[: sizes.columns]
    late = fetch(held.at[0], out.at[0, 0, 0], done.at[1])
    early.wait()
    late.wait()


VMEM = pl.BlockSpec(memory_space=pltpu.VMEM)
HBM = pl.BlockSpec(memory_space=pltpu.HBM)


def call(kernel, name, operands, far, outs, cost, scratch=(), out_spec=VMEM):
    held = [pltpu.with_memory_space_constraint(one, pltpu.HBM) for one in operands[:far]]
    operands = (*held, *operands[far:])
    return pl.pallas_call(
        kernel,
        in_specs=[HBM] * far + [VMEM] * (len(operands) - far),
        out_specs=[out_spec] * len(outs),
        out_shape=[jax.ShapeDtypeStruct(shape, kind) for shape, kind in outs],
        scratch_shapes=scratch,
        compiler_params=pltpu.CompilerParams(vmem_limit_bytes=24 * 2**20),
        cost_estimate=pl.CostEstimate(flops=cost, bytes_accessed=2**20, transcendentals=0),
        name=name,
    )(*operands)


def shards(leaf_axes, right_sides, inverses, couplings, widths, targets):
    right_sides = jnp.swapaxes(right_sides, 3, 4)
    sizes = Sizes(right_sides, couplings, targets, leaf_axes)
    width, slots, rows, columns, levels = sizes.width, sizes.slots, sizes.rows, sizes.columns, sizes.levels
    top = levels - 1
    vector = ((width, LANES), BF16)
    message = ((slots, LANES), BF16)
    matrix = ((width, width), BF16)
    stacked = ((rows + width, width), BF16)
    small, large = 10**6, 10**9

    def exchange(buffer, level):
        pair = leaf_axes[len(leaf_axes) - 1 - level % sizes.leaf_bits]
        blocks = buffer.reshape(slots // 2, 2, LANES)
        moved = lax.all_to_all(blocks, ("near", pair, "far"), split_axis=0, concat_axis=0, tiled=True)
        return moved.reshape(slots, LANES)

    inputs = (right_sides, inverses, couplings, widths, targets)
    buffer, *held = call(
        functools.partial(start_kernel, sizes),
        "start",
        inputs,
        5,
        (
            message,
            vector,
            ((levels, 1, LANES), jnp.int32),
            ((levels, columns, width), BF16),
            ((levels, width, width), BF16),
            ((top, rows, width), BF16),
            (targets.shape, jnp.int32),
        ),
        large,
        (pltpu.SMEM((levels,), jnp.int32), pltpu.SemaphoreType.DMA((7,))),
    )
    limits = held[1]
    sends, takes, start, first, last, *planned = call(
        functools.partial(plan_kernel, sizes),
        "plan",
        held,
        0,
        (
            ((top, 1, rows), jnp.int32),
            ((top, 1, slots), jnp.int32),
            vector,
            ((rows, width), BF16),
            matrix,
            *(vector,) * top,
            *(stacked,) * (top - 1),
        ),
        large,
    )
    sides, stacks = planned[:top], planned[top:]
    starts = [start]
    for level in range(1, top):
        arrived = exchange(buffer, level - 1)
        buffer, start = call(
            functools.partial(up_kernel, sizes, level),
            f"up_{level}",
            (arrived, sides[level - 1], stacks[level - 1], sends, takes),
            0,
            (message, vector),
            small,
        )
        starts.append(start)
    arrived = exchange(buffer, top - 1)
    buffer, solved = call(
        functools.partial(top_kernel, sizes, top),
        "top",
        (arrived, sides[-1], last, takes),
        0,
        (message, vector),
        small,
    )
    above = [solved]
    for level in reversed(range(1, top)):
        arrived = exchange(buffer, level)
        buffer, solved = call(
            functools.partial(down_kernel, sizes, level),
            f"down_{level}",
            (arrived, starts[level], stacks[level - 1], sends, limits, takes),
            0,
            (message, vector),
            small,
        )
        above.insert(0, solved)
    arrived = exchange(buffer, 0)
    (out,) = call(
        functools.partial(last_kernel, sizes),
        "last",
        (arrived, starts[0], first, sends, limits, *above),
        0,
        ((right_sides.shape, BF16),),
        small,
        (pltpu.VMEM((levels, columns, width), BF16), pltpu.SemaphoreType.DMA((2,))),
        HBM,
    )
    return jnp.swapaxes(out, 3, 4)


def solution(mesh):
    groups, owners = mesh.devices.shape
    bits = groups.bit_length() - 1
    near = 1 if owners % 4 else 4
    leaf_axes = tuple(f"leaf{bit}" for bit in reversed(range(bits)))
    split = Mesh(mesh.devices.reshape((2,) * bits + (owners // near, near)), leaf_axes + ("far", "near"))
    blk = ("far", "near")
    return jax.shard_map(
        functools.partial(shards, leaf_axes),
        mesh=split,
        in_specs=(
            P(leaf_axes, blk, None, None, None),
            P(leaf_axes, blk, None, None, None),
            P(leaf_axes, blk, None, None, None),
            P(leaf_axes, blk, None),
            P(),
        ),
        out_specs=P(leaf_axes, blk, None, None, None),
        check_vma=False,
    )
```

time: 70.4 us -> 72.5 us (1.030)
  local copies, waits for them, and re-layouts: 0 us -> 4.93 us
  Pallas kernels: 12.1 us -> 10.2 us
  waiting for transfers between devices: 4.11 us -> 2.86 us
    unnamed x0 -> x8, local copies, waits for them, and re-layouts: none -> 4.93 us
    pallas_call x8, Pallas kernels: 12.1 us -> 10.2 us  [call(): pl.pallas_call(kernel, in_specs=[HBM] * far + [VMEM] * (len(operands) - f...]
    all_to_all x1, waiting for transfers between devices: 4.11 us -> 2.86 us  [exchange(): lax.all_to_all(blocks, ('near', pair, 'far'), split_axis=0, concat_axis=0...]
  transfers between devices with their start and end apart: 1 -> 1, of which waited for: 1 -> 1; matrix products, arithmetic and copies ran while one was open for 0% -> 0% of each run, Pallas kernels for 5% -> 3%
where the time goes in v4:
time: 72.5 us; the launch traced here: 72.1 us
  blocking collectives  46.8 us (65%)
  Pallas kernels  10.2 us (14%)
  starting transfers between devices  7.29 us (10%)
  local copies, waits for them, and re-layouts  4.93 us (7%)
  waiting for transfers between devices  2.86 us (4%)
    all_to_all x5, blocking collectives, exchange(): lax.all_to_all(blocks, ('near', pair, 'far'), split_axis=0, concat_axis=0...  46.8 us
    pallas_call x8, Pallas kernels, call(): pl.pallas_call(kernel, in_specs=[HBM] * far + [VMEM] * (len(operands) - f...  10.2 us
    all_to_all x1, starting transfers between devices, exchange(): lax.all_to_all(blocks, ('near', pair, 'far'), split_axis=0, concat_axis=0...  7.29 us
    unnamed x8, local copies, waits for them, and re-layouts  4.93 us
    all_to_all x1, waiting for transfers between devices, exchange(): lax.all_to_all(blocks, ('near', pair, 'far'), split_axis=0, concat_axis=0...  2.86 us
  transfers between devices with their start and end apart: 1, of which 1 were waited for; matrix products, arithmetic and copies ran while one was open for 0% of the time, Pallas kernels for 3%

profile of v4, /device:TPU:0, one launch (start us, length us, event | category | flops | bytes accessed | tf_op | source)
XLA Modules:
  0.0 72.1 jit_solution(5499646011278691214)
XLA Ops:
  0.0 2.7 %start.1 = (bf16[320,128]{1,0:T(8,128)(2,1)}, bf16[512,128]{1,0:T(8,128)(2,1)S(1)}, s32[4,1,128]{2,1,0:T(1,128)S(1)}, bf16[4,32,512]{2,1,0:T(8,128)(2,1)S(1)}, b...) custom-call(bf16[1,1,4,32,512]{4,3,2,1,0:T(8,128)(2,1)} %bitcast.25, ...), custom_call_target="tpu_custom_call" | custom-call | flops 1000000000 | bytes 1048576 | tf_op jit(solution)/shard_map/start/pallas_call | solution.py:282
  2.7 0.0 copy-start
  2.7 1.3 %copy-done = bf16[4,512,512]{2,1,0:T(8,128)(2,1)} copy-done((bf16[4,512,512]{2,1,0:T(8,128)(2,1)}, bf16[4,512,512]{2,1,0:T(8,128)(2,1)S(1)}, u32[]{:S(2)}) %copy-start) | copy-done | bytes 2097176
  4.0 0.0 copy-start.2
  4.0 0.9 %copy-done.2 = bf16[3,256,512]{2,1,0:T(8,128)(2,1)} copy-done((bf16[3,256,512]{2,1,0:T(8,128)(2,1)}, bf16[3,256,512]{2,1,0:T(8,128)(2,1)S(1)}, u32[]{:S(2)}) %copy-start.2) | copy-done | bytes 786456
  4.9 7.3 %all-to-all-start = ((bf16[160,2,128]{2,1,0:T(2,128)(2,1)}), bf16[160,2,128]{2,1,0:T(2,128)(2,1)S(1)}, u32[]{:S(2)}, u32[]{:S(2)}) async-start(bf16[160,2,128]{2,1,0:T(2,128)(2,1)} %bitcast.1), calls=%async_computation | async-start | bytes 163840 | tf_op jit(solution)/shard_map/all_to_all | solution.py:308
  12.2 0.0 copy-start.1
  12.2 1.6 %copy-done.1 = bf16[4,512,512]{2,1,0:T(8,128)(2,1)S(1)} copy-done((bf16[4,512,512]{2,1,0:T(8,128)(2,1)S(1)}, bf16[4,512,512]{2,1,0:T(8,128)(2,1)}, u32[]{:S(2)}) %copy-start.1) | copy-done | bytes 2097176
  13.8 0.0 copy-start.3
  13.8 1.1 %copy-done.3 = bf16[3,256,512]{2,1,0:T(8,128)(2,1)S(1)} copy-done((bf16[3,256,512]{2,1,0:T(8,128)(2,1)S(1)}, bf16[3,256,512]{2,1,0:T(8,128)(2,1)}, u32[]{:S(2)}) %copy-start.3) | copy-done | bytes 786456
  15.0 1.8 %plan.1 = (s32[3,1,256]{2,1,0:T(1,128)S(1)}, s32[3,1,320]{2,1,0:T(1,128)S(1)}, bf16[512,128]{1,0:T(8,128)(2,1)S(1)}, bf16[256,512]{1,0:T(8,128)(2,1)S(1)}, bf16[...) custom-call(bf16[512,128]{1,0:T(8,128)(2,1)S(1)} %get-tuple-element., ...), custom_call_target="tpu_custom_call" | custom-call | flops 1000000000 | bytes 1048576 | tf_op jit(solution)/shard_map/plan/pallas_call | solution.py:282
  16.8 2.9 %all-to-all-done = bf16[160,2,128]{2,1,0:T(2,128)(2,1)S(1)} async-done(((bf16[160,2,128]{2,1,0:T(2,128)(2,1)}), bf16[160,2,128]{2,1,0:T(2,128)(2,1)S(1)}, u32[]{:S(2)}, u32[]{:S(2)}) %all-to-all-start) | async-done | bytes 81952 | tf_op jit(solution)/shard_map/all_to_all | solution.py:308
  19.7 0.9 %up_1.1 = (bf16[320,128]{1,0:T(8,128)(2,1)S(1)}, bf16[512,128]{1,0:T(8,128)(2,1)S(1)}) custom-call(bf16[320,128]{1,0:T(8,128)(2,1)S(1)} %bitcast.14, bf16[512,128]{1,0:T(8,128)(2,1)S(1)} %get-tuple-element.39.side, bf16[768,512]{1,0:T(8,128)(2,1)S(1)} %get-tuple-element.40.stack.product, s32[3,1,256]{2,1,0:T(1,128)S(1)} %get-tuple-element.41.sends, ...), custom_call_target="tpu_custom_call" | custom-call | flops 1000000 | bytes 1048576 | tf_op jit(solution)/shard_map/up_1/pallas_call | solution.py:282
  20.5 10.2 %all_to_all.30 = bf16[160,2,128]{2,1,0:T(2,128)(2,1)S(1)} all-to-all(bf16[160,2,128]{2,1,0:T(2,128)(2,1)S(1)} %bitcast.23), channel_id=1, replica_groups=mesh['leaf0'=2,'far'=4,'near'=4] {'near','leaf0','far'}, dimensions={0} | all-to-all | bytes 163840 | tf_op jit(solution)/shard_map/all_to_all | solution.py:308
  30.8 0.9 %up_2.1 = (bf16[320,128]{1,0:T(8,128)(2,1)S(1)}, bf16[512,128]{1,0:T(8,128)(2,1)S(1)}) custom-call(bf16[320,128]{1,0:T(8,128)(2,1)S(1)} %bitcast.18, bf16[512,128]{1,0:T(8,128)(2,1)S(1)} %get-tuple-element.44.side, bf16[768,512]{1,0:T(8,128)(2,1)S(1)} %get-tuple-element.45.stack.product, s32[3,1,256]{2,1,0:T(1,128)S(1)} %get-tuple-element.41.sends, ...), custom_call_target="tpu_custom_call" | custom-call | flops 1000000 | bytes 1048576 | tf_op jit(solution)/shard_map/up_2/pallas_call | solution.py:282
  31.6 9.1 %all_to_all.31 = bf16[160,2,128]{2,1,0:T(2,128)(2,1)S(1)} all-to-all(bf16[160,2,128]{2,1,0:T(2,128)(2,1)S(1)} %bitcast.24), channel_id=1, replica_groups=mesh['leaf0'=2,'far'=4,'near'=4] {'near','leaf0','far'}, dimensions={0} | all-to-all | bytes 163840 | tf_op jit(solution)/shard_map/all_to_all | solution.py:308
  40.7 1.0 %top.1 = (bf16[320,128]{1,0:T(8,128)(2,1)S(1)}, bf16[512,128]{1,0:T(8,128)(2,1)S(1)}) custom-call(bf16[320,128]{1,0:T(8,128)(2,1)S(1)} %bitcast.19, bf16[512,128]{1,0:T(8,128)(2,1)S(1)} %get-tuple-element.47.side, bf16[512,512]{1,0:T(8,128)(2,1)S(1)} %get-tuple-element.48.square, s32[3,1,320]{2,1,0:T(1,128)S(1)} %get-tuple-element.42.takes), custom_call_target="tpu_custom_call" | custom-call | flops 1000000 | bytes 1048576 | tf_op jit(solution)/shard_map/top/pallas_call | solution.py:282
  41.7 9.1 %all_to_all.32 = bf16[160,2,128]{2,1,0:T(2,128)(2,1)S(1)} all-to-all(bf16[160,2,128]{2,1,0:T(2,128)(2,1)S(1)} %bitcast.21), channel_id=1, replica_groups=mesh['leaf0'=2,'far'=4,'near'=4] {'near','leaf0','far'}, dimensions={0} | all-to-all | bytes 163840 | tf_op jit(solution)/shard_map/all_to_all | solution.py:308
  50.8 0.9 %down_2.1 = (bf16[320,128]{1,0:T(8,128)(2,1)S(1)}, bf16[512,128]{1,0:T(8,128)(2,1)S(1)}) custom-call(bf16[320,128]{1,0:T(8,128)(2,1)S(1)} %bitcast.17, bf16[512,128]{1,0:T(8,128)(2,1)S(1)} %get-tuple-element.50.start, bf16[768,512]{1,0:T(8,128)(2,1)S(1)} %get-tuple-element.45.stack.product, s32[3,1,256]{2,1,0:T(1,128)S(1)} %get-tuple-element.41.sends, ...), custom_call_target="tpu_custom_call" | custom-call | flops 1000000 | bytes 1048576 | tf_op jit(solution)/shard_map/down_2/pallas_call | solution.py:282
  51.7 9.1 %all_to_all.33 = bf16[160,2,128]{2,1,0:T(2,128)(2,1)S(1)} all-to-all(bf16[160,2,128]{2,1,0:T(2,128)(2,1)S(1)} %bitcast.22), channel_id=1, replica_groups=mesh['leaf0'=2,'far'=4,'near'=4] {'near','leaf0','far'}, dimensions={0} | all-to-all | bytes 163840 | tf_op jit(solution)/shard_map/all_to_all | solution.py:308
  60.8 0.9 %down_1.1 = (bf16[320,128]{1,0:T(8,128)(2,1)S(1)}, bf16[512,128]{1,0:T(8,128)(2,1)S(1)}) custom-call(bf16[320,128]{1,0:T(8,128)(2,1)S(1)} %bitcast.16, bf16[512,128]{1,0:T(8,128)(2,1)S(1)} %get-tuple-element.52.start, bf16[768,512]{1,0:T(8,128)(2,1)S(1)} %get-tuple-element.40.stack.product, s32[3,1,256]{2,1,0:T(1,128)S(1)} %get-tuple-element.41.sends, ...), custom_call_target="tpu_custom_call" | custom-call | flops 1000000 | bytes 1048576 | tf_op jit(solution)/shard_map/down_1/pallas_call | solution.py:282
  61.7 9.1 %all_to_all.34 = bf16[160,2,128]{2,1,0:T(2,128)(2,1)S(1)} all-to-all(bf16[160,2,128]{2,1,0:T(2,128)(2,1)S(1)} %bitcast.20), channel_id=1, replica_groups=mesh['leaf0'=2,'far'=4,'near'=4] {'near','leaf0','far'}, dimensions={0} | all-to-all | bytes 163840 | tf_op jit(solution)/shard_map/all_to_all | solution.py:308
  70.8 1.3 %last.1 = bf16[1,1,4,32,512]{4,3,2,1,0:T(8,128)(2,1)} custom-call(bf16[320,128]{1,0:T(8,128)(2,1)S(1)} %bitcast.15, bf16[512,128]{1,0:T(8,128)(2,1)S(1)} %get-tuple-element.54.start, bf16[256,512]{1,0:T(8,128)(2,1)S(1)} %get-tuple-element.55.product, s32[3,1,256]{2,1,0:T(1,128)S(1)} %get-tuple-element.41.sends, s32[4,1,128]{2,1,0:T(1,128)S(1)} %get-tuple-element.34.limits, ...), custom_call_target="tpu_custom_call" | custom-call | flops 1000000 | bytes 1048576 | tf_op jit(solution)/shard_map/last/pallas_call | solution.py:282
Async XLA Ops:
  2.7 1.3 %copy-start = (bf16[4,512,512]{2,1,0:T(8,128)(2,1)}, bf16[4,512,512]{2,1,0:T(8,128)(2,1)S(1)}, u32[]{:S(2)}) copy-start(bf16[4,512,512]{2,1,0:T(8,128)(2,1)S(1)} %get-tuple-element.36.inverse) | copy-start | bytes 6291460
  4.0 0.9 %copy-start.2 = (bf16[3,256,512]{2,1,0:T(8,128)(2,1)}, bf16[3,256,512]{2,1,0:T(8,128)(2,1)S(1)}, u32[]{:S(2)}) copy-start(bf16[3,256,512]{2,1,0:T(8,128)(2,1)S(1)} %get-tuple-element.37.coupling) | copy-start | bytes 2359300
  4.9 14.7 %all-to-all-start = ((bf16[160,2,128]{2,1,0:T(2,128)(2,1)}), bf16[160,2,128]{2,1,0:T(2,128)(2,1)S(1)}, u32[]{:S(2)}, u32[]{:S(2)}) async-start(bf16[160,2,128]{2,1,0:T(2,128)(2,1)} %bitcast.1), calls=%async_computation | async-start | bytes 163840 | tf_op jit(solution)/shard_map/all_to_all | solution.py:308
  12.2 1.6 %copy-start.1 = (bf16[4,512,512]{2,1,0:T(8,128)(2,1)S(1)}, bf16[4,512,512]{2,1,0:T(8,128)(2,1)}, u32[]{:S(2)}) copy-start(bf16[4,512,512]{2,1,0:T(8,128)(2,1)} %copy-done) | copy-start | bytes 6291460
  13.8 1.1 %copy-start.3 = (bf16[3,256,512]{2,1,0:T(8,128)(2,1)S(1)}, bf16[3,256,512]{2,1,0:T(8,128)(2,1)}, u32[]{:S(2)}) copy-start(bf16[3,256,512]{2,1,0:T(8,128)(2,1)} %copy-done.2) | copy-start | bytes 2359300

commit v5 on v4

--- a/solution.py
+++ b/solution.py
@@ -174,17 +174,13 @@
 
 
 def start_kernel(sizes, right, inverse, coupling, widths, targets, buffer, forward, limits, *refs):
-    right_in, inverse_in, coupling_in, targets_in, widths_in, done = refs
-    top = sizes.levels - 1
-    first, others = pl.ds(0, 1), pl.ds(1, top)
+    right_in, targets_in, inverse_in, coupling_in, widths_in, done = refs
     copies = [
         fetch(targets, targets_in, done.at[0]),
         fetch(right.at[0, 0], right_in, done.at[1]),
         fetch(widths.at[0, 0], widths_in, done.at[2]),
-        fetch(inverse.at[0, 0, first], inverse_in.at[first], done.at[3]),
-        fetch(coupling.at[0, 0, first], coupling_in.at[first], done.at[4]),
-        fetch(inverse.at[0, 0, others], inverse_in.at[others], done.at[5]),
-        fetch(coupling.at[0, 0, pl.ds(1, top - 1)], coupling_in.at[pl.ds(1, top - 1)], done.at[6]),
+        fetch(inverse.at[0, 0, 0], inverse_in, done.at[3]),
+        fetch(coupling.at[0, 0, 0], coupling_in, done.at[4]),
     ]
     copies[0].wait()
     sender = send_matrix(sizes, send_slots(sizes, 0, targets_in))
@@ -194,33 +190,44 @@
     for level in range(sizes.levels):
         limits[level] = jnp.full((1, LANES), widths_in[level] * BLOCK, jnp.int32)
     copies[3].wait()
-    solved = solve_forward(sizes, 0, limits, inverse_in[0], residual)
+    solved = solve_forward(sizes, 0, limits, inverse_in[...], residual)
     forward[...] = solved
     copies[4].wait()
-    pieces = keep_own(sizes, dot(coupling_in[0], solved).astype(BF16))
+    pieces = keep_own(sizes, dot(coupling_in[...], solved).astype(BF16))
     buffer[...] = dot(sender, pieces).astype(BF16)
-    copies[5].wait()
-    copies[6].wait()
-
-
-def plan_kernel(sizes, forward, limits, right, inverse, coupling, targets, *refs):
+
+
+def plan_kernel(sizes, inverse, coupling, forward, limits, right, targets, *refs):
     top = sizes.levels - 1
     sends, takes, start, first, last = refs[:5]
-    sides, stacks = refs[5 : 5 + top], refs[5 + top :]
-    for level in range(1, top + 1):
-        sides[level - 1][...] = repeat_columns(sizes, right[level])
-    for level in range(top):
-        product = coupled_inverse(sizes, level, limits, inverse[level], coupling[level])
-        if level == 0:
-            first[...] = product
-        else:
-            stacks[level - 1][pl.ds(0, sizes.rows)] = product
-            stacks[level - 1][pl.ds(sizes.rows, sizes.width)] = squared_inverse(sizes, level, limits, inverse[level])
-    last[...] = squared_inverse(sizes, top, limits, inverse[top])
-    start[...] = solve_backward(sizes, 0, limits, inverse[0], forward[...]).astype(BF16)
+    sides, stacks = refs[5 : 5 + top], refs[5 + top : -3]
+    inverse_in, coupling_in, done = refs[-3:]
+    copies = []
+    for level in (*range(1, top + 1), 0):
+        at = 2 * len(copies)
+        pair = [fetch(inverse.at[0, 0, level], inverse_in.at[level], done.at[at])]
+        if level < top:
+            pair.append(fetch(coupling.at[0, 0, level], coupling_in.at[level], done.at[at + 1]))
+        copies.append(pair)
     for level in range(top):
         sends[level] = send_slots(sizes, level, targets)
         takes[level] = take_places(sizes, level, targets)
+    for level in range(1, top + 1):
+        sides[level - 1][...] = repeat_columns(sizes, right[level])
+    for level in (*range(1, top + 1), 0):
+        for copy in copies.pop(0):
+            copy.wait()
+        block = inverse_in[level]
+        if level == top:
+            last[...] = squared_inverse(sizes, top, limits, block)
+            continue
+        product = coupled_inverse(sizes, level, limits, block, coupling_in[level])
+        if level == 0:
+            first[...] = product
+            start[...] = solve_backward(sizes, 0, limits, block, forward[...]).astype(BF16)
+        else:
+            stacks[level - 1][pl.ds(0, sizes.rows)] = product
+            stacks[level - 1][pl.ds(sizes.rows, sizes.width)] = squared_inverse(sizes, level, limits, block)
 
 
 def residual_of(sizes, level, arrived, side, takes):
@@ -299,6 +306,7 @@
     vector = ((width, LANES), BF16)
     message = ((slots, LANES), BF16)
     matrix = ((width, width), BF16)
+    coupled = ((rows, width), BF16)
     stacked = ((rows + width, width), BF16)
     small, large = 10**6, 10**9
 
@@ -319,29 +327,37 @@
             vector,
             ((levels, 1, LANES), jnp.int32),
             ((levels, columns, width), BF16),
-            ((levels, width, width), BF16),
-            ((top, rows, width), BF16),
             (targets.shape, jnp.int32),
         ),
         large,
-        (pltpu.SMEM((levels,), jnp.int32), pltpu.SemaphoreType.DMA((7,))),
+        (
+            pltpu.VMEM(*matrix),
+            pltpu.VMEM(*coupled),
+            pltpu.SMEM((levels,), jnp.int32),
+            pltpu.SemaphoreType.DMA((5,)),
+        ),
     )
     limits = held[1]
     sends, takes, start, first, last, *planned = call(
         functools.partial(plan_kernel, sizes),
         "plan",
-        held,
-        0,
+        (inverses, couplings, *held),
+        2,
         (
             ((top, 1, rows), jnp.int32),
             ((top, 1, slots), jnp.int32),
             vector,
-            ((rows, width), BF16),
+            coupled,
             matrix,
             *(vector,) * top,
             *(stacked,) * (top - 1),
         ),
         large,
+        (
+            pltpu.VMEM((levels, width, width), BF16),
+            pltpu.VMEM((top, rows, width), BF16),
+            pltpu.SemaphoreType.DMA((2 * levels,)),
+        ),
     )
     sides, stacks = planned[:top], planned[top:]
     starts = [start]

time: 72.5 us -> 69.1 us (0.953)
  local copies, waits for them, and re-layouts: 4.93 us -> 0 us
  Pallas kernels: 10.2 us -> 11.8 us
  blocking collectives: 46.8 us -> 45.7 us
  waiting for transfers between devices: 2.86 us -> 3.95 us
    unnamed x8 -> x0, local copies, waits for them, and re-layouts: 4.93 us -> none
    pallas_call x8, Pallas kernels: 10.2 us -> 11.8 us  [call(): pl.pallas_call(kernel, in_specs=[HBM] * far + [VMEM] * (len(operands) - f...]
    all_to_all x1, waiting for transfers between devices: 2.86 us -> 3.95 us  [exchange(): lax.all_to_all(blocks, ('near', pair, 'far'), split_axis=0, concat_axis=0...]
    all_to_all x5, blocking collectives: 46.8 us -> 45.7 us  [exchange(): lax.all_to_all(blocks, ('near', pair, 'far'), split_axis=0, concat_axis=0...]
  transfers between devices with their start and end apart: 1 -> 1, of which waited for: 1 -> 1; matrix products, arithmetic and copies ran while one was open for 0% -> 0% of each run, Pallas kernels for 3% -> 5%
where the time goes in v5:
time: 69.1 us; the launch traced here: 68.8 us
  blocking collectives  45.7 us (66%)
  Pallas kernels  11.8 us (17%)
  starting transfers between devices  7.3 us (11%)
  waiting for transfers between devices  3.95 us (6%)
    all_to_all x5, blocking collectives, exchange(): lax.all_to_all(blocks, ('near', pair, 'far'), split_axis=0, concat_axis=0...  45.7 us
    pallas_call x8, Pallas kernels, call(): pl.pallas_call(kernel, in_specs=[HBM] * far + [VMEM] * (len(operands) - f...  11.8 us
    all_to_all x1, starting transfers between devices, exchange(): lax.all_to_all(blocks, ('near', pair, 'far'), split_axis=0, concat_axis=0...  7.3 us
    all_to_all x1, waiting for transfers between devices, exchange(): lax.all_to_all(blocks, ('near', pair, 'far'), split_axis=0, concat_axis=0...  3.95 us
  transfers between devices with their start and end apart: 1, of which 1 were waited for; matrix products, arithmetic and copies ran while one was open for 0% of the time, Pallas kernels for 5%

profile of v5, /device:TPU:0, one launch (start us, length us, event | category | flops | bytes accessed | tf_op | source)
XLA Modules:
  0.0 68.8 jit_solution(16424265853502936853)
XLA Ops:
  0.0 2.7 %start.1 = (bf16[320,128]{1,0:T(8,128)(2,1)}, bf16[512,128]{1,0:T(8,128)(2,1)S(1)}, s32[4,1,128]{2,1,0:T(1,128)S(1)}, bf16[4,32,512]{2,1,0:T(8,128)(2,1)S(1)}, s32[3,2,16,64]{3,2,1,0:T(8,128)S(1)}) custom-call(bf16[1,1,4,32,512]{4,3,2,1,0:T(8,128)(2,1)} %bitcast.25, bf16[1,1,4,512,512]{4,3,2,1,0:T(8,128)(2,1)} %inverse.3, ...), custom_call_target="tpu_custom_call" | custom-call | flops 1000000000 | bytes 1048576 | tf_op jit(solution)/shard_map/start/pallas_call | solution.py:289
  2.7 7.3 %all-to-all-start = ((bf16[160,2,128]{2,1,0:T(2,128)(2,1)}), bf16[160,2,128]{2,1,0:T(2,128)(2,1)S(1)}, u32[]{:S(2)}, u32[]{:S(2)}) async-start(bf16[160,2,128]{2,1,0:T(2,128)(2,1)} %bitcast.1), calls=%async_computation | async-start | bytes 163840 | tf_op jit(solution)/shard_map/all_to_all | solution.py:316
  10.0 3.5 %plan.1 = (s32[3,1,256]{2,1,0:T(1,128)S(1)}, s32[3,1,320]{2,1,0:T(1,128)S(1)}, bf16[512,128]{1,0:T(8,128)(2,1)S(1)}, bf16[256,512]{1,0:T(8,128)(2,1)S(1)}, bf16[...) custom-call(bf16[1,1,4,512,512]{4,3,2,1,0:T(8,128)(2,1)} %inverse.3,, ...), custom_call_target="tpu_custom_call" | custom-call | flops 1000000000 | bytes 1048576 | tf_op jit(solution)/shard_map/plan/pallas_call | solution.py:289
  13.5 3.9 %all-to-all-done = bf16[160,2,128]{2,1,0:T(2,128)(2,1)S(1)} async-done(((bf16[160,2,128]{2,1,0:T(2,128)(2,1)}), bf16[160,2,128]{2,1,0:T(2,128)(2,1)S(1)}, u32[]{:S(2)}, u32[]{:S(2)}) %all-to-all-start) | async-done | bytes 81952 | tf_op jit(solution)/shard_map/all_to_all | solution.py:316
  17.4 0.8 %up_1.1 = (bf16[320,128]{1,0:T(8,128)(2,1)S(1)}, bf16[512,128]{1,0:T(8,128)(2,1)S(1)}) custom-call(bf16[320,128]{1,0:T(8,128)(2,1)S(1)} %bitcast.14, bf16[512,128]{1,0:T(8,128)(2,1)S(1)} %get-tuple-element.35.side, bf16[768,512]{1,0:T(8,128)(2,1)S(1)} %get-tuple-element.36.stack.product, s32[3,1,256]{2,1,0:T(1,128)S(1)} %get-tuple-element.37.sends, ...), custom_call_target="tpu_custom_call" | custom-call | flops 1000000 | bytes 1048576 | tf_op jit(solution)/shard_map/up_1/pallas_call | solution.py:289
  18.3 9.1 %all_to_all.30 = bf16[160,2,128]{2,1,0:T(2,128)(2,1)S(1)} all-to-all(bf16[160,2,128]{2,1,0:T(2,128)(2,1)S(1)} %bitcast.23), channel_id=1, replica_groups=mesh['leaf0'=2,'far'=4,'near'=4] {'near','leaf0','far'}, dimensions={0} | all-to-all | bytes 163840 | tf_op jit(solution)/shard_map/all_to_all | solution.py:316
  27.4 0.8 %up_2.1 = (bf16[320,128]{1,0:T(8,128)(2,1)S(1)}, bf16[512,128]{1,0:T(8,128)(2,1)S(1)}) custom-call(bf16[320,128]{1,0:T(8,128)(2,1)S(1)} %bitcast.18, bf16[512,128]{1,0:T(8,128)(2,1)S(1)} %get-tuple-element.40.side, bf16[768,512]{1,0:T(8,128)(2,1)S(1)} %get-tuple-element.41.stack.product, s32[3,1,256]{2,1,0:T(1,128)S(1)} %get-tuple-element.37.sends, ...), custom_call_target="tpu_custom_call" | custom-call | flops 1000000 | bytes 1048576 | tf_op jit(solution)/shard_map/up_2/pallas_call | solution.py:289
  28.3 9.1 %all_to_all.31 = bf16[160,2,128]{2,1,0:T(2,128)(2,1)S(1)} all-to-all(bf16[160,2,128]{2,1,0:T(2,128)(2,1)S(1)} %bitcast.24), channel_id=1, replica_groups=mesh['leaf0'=2,'far'=4,'near'=4] {'near','leaf0','far'}, dimensions={0} | all-to-all | bytes 163840 | tf_op jit(solution)/shard_map/all_to_all | solution.py:316
  37.4 1.0 %top.1 = (bf16[320,128]{1,0:T(8,128)(2,1)S(1)}, bf16[512,128]{1,0:T(8,128)(2,1)S(1)}) custom-call(bf16[320,128]{1,0:T(8,128)(2,1)S(1)} %bitcast.19, bf16[512,128]{1,0:T(8,128)(2,1)S(1)} %get-tuple-element.43.side, bf16[512,512]{1,0:T(8,128)(2,1)S(1)} %get-tuple-element.44.square, s32[3,1,320]{2,1,0:T(1,128)S(1)} %get-tuple-element.38.takes), custom_call_target="tpu_custom_call" | custom-call | flops 1000000 | bytes 1048576 | tf_op jit(solution)/shard_map/top/pallas_call | solution.py:289
  38.4 9.1 %all_to_all.32 = bf16[160,2,128]{2,1,0:T(2,128)(2,1)S(1)} all-to-all(bf16[160,2,128]{2,1,0:T(2,128)(2,1)S(1)} %bitcast.21), channel_id=1, replica_groups=mesh['leaf0'=2,'far'=4,'near'=4] {'near','leaf0','far'}, dimensions={0} | all-to-all | bytes 163840 | tf_op jit(solution)/shard_map/all_to_all | solution.py:316
  47.5 0.9 %down_2.1 = (bf16[320,128]{1,0:T(8,128)(2,1)S(1)}, bf16[512,128]{1,0:T(8,128)(2,1)S(1)}) custom-call(bf16[320,128]{1,0:T(8,128)(2,1)S(1)} %bitcast.17, bf16[512,128]{1,0:T(8,128)(2,1)S(1)} %get-tuple-element.46.start, bf16[768,512]{1,0:T(8,128)(2,1)S(1)} %get-tuple-element.41.stack.product, s32[3,1,256]{2,1,0:T(1,128)S(1)} %get-tuple-element.37.sends, ...), custom_call_target="tpu_custom_call" | custom-call | flops 1000000 | bytes 1048576 | tf_op jit(solution)/shard_map/down_2/pallas_call | solution.py:289
  48.4 9.1 %all_to_all.33 = bf16[160,2,128]{2,1,0:T(2,128)(2,1)S(1)} all-to-all(bf16[160,2,128]{2,1,0:T(2,128)(2,1)S(1)} %bitcast.22), channel_id=1, replica_groups=mesh['leaf0'=2,'far'=4,'near'=4] {'near','leaf0','far'}, dimensions={0} | all-to-all | bytes 163840 | tf_op jit(solution)/shard_map/all_to_all | solution.py:316
  57.5 0.9 %down_1.1 = (bf16[320,128]{1,0:T(8,128)(2,1)S(1)}, bf16[512,128]{1,0:T(8,128)(2,1)S(1)}) custom-call(bf16[320,128]{1,0:T(8,128)(2,1)S(1)} %bitcast.16, bf16[512,128]{1,0:T(8,128)(2,1)S(1)} %get-tuple-element.48.start, bf16[768,512]{1,0:T(8,128)(2,1)S(1)} %get-tuple-element.36.stack.product, s32[3,1,256]{2,1,0:T(1,128)S(1)} %get-tuple-element.37.sends, ...), custom_call_target="tpu_custom_call" | custom-call | flops 1000000 | bytes 1048576 | tf_op jit(solution)/shard_map/down_1/pallas_call | solution.py:289
  58.4 9.1 %all_to_all.34 = bf16[160,2,128]{2,1,0:T(2,128)(2,1)S(1)} all-to-all(bf16[160,2,128]{2,1,0:T(2,128)(2,1)S(1)} %bitcast.20), channel_id=1, replica_groups=mesh['leaf0'=2,'far'=4,'near'=4] {'near','leaf0','far'}, dimensions={0} | all-to-all | bytes 163840 | tf_op jit(solution)/shard_map/all_to_all | solution.py:316
  67.5 1.3 %last.1 = bf16[1,1,4,32,512]{4,3,2,1,0:T(8,128)(2,1)} custom-call(bf16[320,128]{1,0:T(8,128)(2,1)S(1)} %bitcast.15, bf16[512,128]{1,0:T(8,128)(2,1)S(1)} %get-tuple-element.50.start, bf16[256,512]{1,0:T(8,128)(2,1)S(1)} %get-tuple-element.51.product, s32[3,1,256]{2,1,0:T(1,128)S(1)} %get-tuple-element.37.sends, s32[4,1,128]{2,1,0:T(1,128)S(1)} %get-tuple-element.32.limits, ...), custom_call_target="tpu_custom_call" | custom-call | flops 1000000 | bytes 1048576 | tf_op jit(solution)/shard_map/last/pallas_call | solution.py:289
Async XLA Ops:
  2.7 14.7 %all-to-all-start = ((bf16[160,2,128]{2,1,0:T(2,128)(2,1)}), bf16[160,2,128]{2,1,0:T(2,128)(2,1)S(1)}, u32[]{:S(2)}, u32[]{:S(2)}) async-start(bf16[160,2,128]{2,1,0:T(2,128)(2,1)} %bitcast.1), calls=%async_computation | async-start | bytes 163840 | tf_op jit(solution)/shard_map/all_to_all | solution.py:316

commit v6 on v5

--- a/solution.py
+++ b/solution.py
@@ -27,6 +27,14 @@
 
 def trans_dot(left, right):
     return lax.dot_general(left, right, (((0,), (0,)), ((), ())), preferred_element_type=F32)
+
+
+def dot_trans(left, right):
+    return lax.dot_general(left, right, (((1,), (1,)), ((), ())), preferred_element_type=F32)
+
+
+def cross_dot(left, right):
+    return lax.dot_general(left, right, (((0,), (1,)), ((), ())), preferred_element_type=F32)
 
 
 def over(value, size):
@@ -57,30 +65,25 @@
         self.slots = 2 * self.owners * self.message
 
 
-def live(limits, level, shape, axis):
-    return iota(shape, axis) < limits[level][:, :1]
-
-
-def own_lanes(sizes, rows):
-    shape = (rows, LANES)
-    return over(iota(shape, 1), sizes.columns) == within(iota(shape, 0), sizes.sub)
+def keep_live(limits, level, value, axis):
+    return jnp.where(iota(value.shape, axis) < limits[level][:, :1], value, jnp.zeros_like(value))
 
 
 def keep_own(sizes, value):
-    return jnp.where(own_lanes(sizes, value.shape[0]), value, jnp.zeros_like(value))
-
-
-def spread(sizes, value):
+    own = within(iota(value.shape, 1), sizes.sub) == over(iota(value.shape, 0), sizes.columns)
+    return jnp.where(own, value, jnp.zeros_like(value))
+
+
+def to_rows(sizes, value):
     value = keep_own(sizes, value)
-    step = sizes.columns
-    while step < LANES:
-        value = value + pltpu.roll(value, step, 1)
-        step *= 2
-    return value
-
-
-def repeat_columns(sizes, value):
-    return jnp.concatenate([value] * (LANES // sizes.columns), axis=0).T
+    parts = [value[at * sizes.columns : (at + 1) * sizes.columns] for at in range(sizes.sub)]
+    while len(parts) > 1:
+        parts = [sum(parts[at : at + 2]) for at in range(0, len(parts), 2)]
+    return parts[0]
+
+
+def to_flat(sizes, value):
+    return keep_own(sizes, jnp.concatenate([value] * sizes.sub, axis=0))
 
 
 def position(sizes, level):
@@ -147,18 +150,12 @@
 
 
 def coupled_inverse(sizes, level, limits, inverse, coupling):
-    kept = jnp.where(live(limits, level, coupling.shape, 1), coupling, jnp.zeros_like(coupling))
-    return dot(kept, inverse).astype(BF16)
-
-
-def solve_forward(sizes, level, limits, inverse, residual):
-    product = dot(inverse, residual)
-    return jnp.where(live(limits, level, product.shape, 0), product, 0.0).astype(BF16)
-
-
-def solve_backward(sizes, level, limits, inverse, side):
-    product = trans_dot(inverse, side)
-    return jnp.where(live(limits, level, product.shape, 0), product, 0.0)
+    return dot(keep_live(limits, level, coupling, 1), inverse).astype(BF16)
+
+
+def squared_inverse(sizes, level, limits, inverse):
+    product = trans_dot(inverse, keep_live(limits, level, inverse, 0))
+    return keep_live(limits, level, product, 1).astype(BF16)
 
 
 def fetch(source, target, semaphore):
@@ -167,40 +164,41 @@
     return copy
 
 
-def squared_inverse(sizes, level, limits, inverse):
-    kept = jnp.where(live(limits, level, inverse.shape, 0), inverse, jnp.zeros_like(inverse))
-    product = trans_dot(inverse, kept)
-    return jnp.where(live(limits, level, product.shape, 0), product, 0.0).astype(BF16)
+def send_pieces(sizes, sender, pieces):
+    return dot_trans(sender, to_flat(sizes, pieces.astype(BF16))).astype(BF16)
 
 
 def start_kernel(sizes, right, inverse, coupling, widths, targets, buffer, forward, limits, *refs):
     right_in, targets_in, inverse_in, coupling_in, widths_in, done = refs
+    first, others = pl.ds(0, 1), pl.ds(1, sizes.levels - 1)
     copies = [
-        fetch(targets, targets_in, done.at[0]),
-        fetch(right.at[0, 0], right_in, done.at[1]),
+        fetch(targets.at[first], targets_in.at[first], done.at[0]),
+        fetch(right.at[0, 0, first], right_in.at[first], done.at[1]),
         fetch(widths.at[0, 0], widths_in, done.at[2]),
         fetch(inverse.at[0, 0, 0], inverse_in, done.at[3]),
         fetch(coupling.at[0, 0, 0], coupling_in, done.at[4]),
+        fetch(right.at[0, 0, others], right_in.at[others], done.at[5]),
+        fetch(targets.at[pl.ds(1, sizes.levels - 2)], targets_in.at[pl.ds(1, sizes.levels - 2)], done.at[6]),
     ]
     copies[0].wait()
     sender = send_matrix(sizes, send_slots(sizes, 0, targets_in))
     copies[1].wait()
-    residual = repeat_columns(sizes, right_in[0])
     copies[2].wait()
     for level in range(sizes.levels):
         limits[level] = jnp.full((1, LANES), widths_in[level] * BLOCK, jnp.int32)
     copies[3].wait()
-    solved = solve_forward(sizes, 0, limits, inverse_in[...], residual)
+    solved = keep_live(limits, 0, dot_trans(right_in[0], inverse_in[...]), 1).astype(BF16)
     forward[...] = solved
     copies[4].wait()
-    pieces = keep_own(sizes, dot(coupling_in[...], solved).astype(BF16))
-    buffer[...] = dot(sender, pieces).astype(BF16)
-
-
-def plan_kernel(sizes, inverse, coupling, forward, limits, right, targets, *refs):
+    buffer[...] = send_pieces(sizes, sender, dot_trans(solved, coupling_in[...]))
+    copies[5].wait()
+    copies[6].wait()
+
+
+def plan_kernel(sizes, inverse, coupling, forward, limits, targets, *refs):
     top = sizes.levels - 1
-    sends, takes, start, first, last = refs[:5]
-    sides, stacks = refs[5 : 5 + top], refs[5 + top : -3]
+    sends, takes, start = refs[:3]
+    products, squares = refs[3 : 3 + top], refs[3 + top : 3 + 2 * top]
     inverse_in, coupling_in, done = refs[-3:]
     copies = []
     for level in (*range(1, top + 1), 0):
@@ -212,71 +210,57 @@
     for level in range(top):
         sends[level] = send_slots(sizes, level, targets)
         takes[level] = take_places(sizes, level, targets)
-    for level in range(1, top + 1):
-        sides[level - 1][...] = repeat_columns(sizes, right[level])
     for level in (*range(1, top + 1), 0):
         for copy in copies.pop(0):
             copy.wait()
         block = inverse_in[level]
-        if level == top:
-            last[...] = squared_inverse(sizes, top, limits, block)
-            continue
-        product = coupled_inverse(sizes, level, limits, block, coupling_in[level])
-        if level == 0:
-            first[...] = product
-            start[...] = solve_backward(sizes, 0, limits, block, forward[...]).astype(BF16)
+        if level < top:
+            products[level][...] = coupled_inverse(sizes, level, limits, block, coupling_in[level])
+        if level > 0:
+            squares[level - 1][...] = squared_inverse(sizes, level, limits, block)
         else:
-            stacks[level - 1][pl.ds(0, sizes.rows)] = product
-            stacks[level - 1][pl.ds(sizes.rows, sizes.width)] = squared_inverse(sizes, level, limits, block)
-
-
-def residual_of(sizes, level, arrived, side, takes):
-    incoming = spread(sizes, dot(take_matrix(sizes, takes[level - 1]), arrived[...]))
-    return (side[...].astype(F32) - incoming).astype(BF16)
-
-
-def up_kernel(sizes, level, arrived, side, stack, sends, takes, buffer, start):
-    residual = residual_of(sizes, level, arrived, side, takes)
-    both = dot(stack[...], residual)
-    pieces = keep_own(sizes, both[: sizes.rows].astype(BF16))
-    buffer[...] = dot(send_matrix(sizes, sends[level]), pieces).astype(BF16)
-    start[...] = both[sizes.rows :].astype(BF16)
-
-
-def reply(sizes, level, value, takes):
-    return trans_dot(take_matrix(sizes, takes[level - 1]), keep_own(sizes, value)).astype(BF16)
-
-
-def top_kernel(sizes, level, arrived, side, square, takes, buffer, solved):
-    residual = residual_of(sizes, level, arrived, side, takes)
-    value = dot(square[...], residual).astype(BF16)
-    buffer[...] = reply(sizes, level, value, takes)
+            start[...] = keep_live(limits, 0, dot(forward[...], block), 1).astype(BF16)
+
+
+def residual_of(sizes, level, arrived, right, taker):
+    incoming = to_rows(sizes, dot_trans(arrived[...].T, taker))
+    return (right[level].astype(F32) - incoming).astype(BF16)
+
+
+def up_kernel(sizes, level, arrived, right, product, square, sends, takes, buffer, start):
+    residual = residual_of(sizes, level, arrived, right, take_matrix(sizes, takes[level - 1]))
+    pieces = dot_trans(residual, product[...])
+    start[...] = dot(residual, square[...]).astype(BF16)
+    buffer[...] = send_pieces(sizes, send_matrix(sizes, sends[level]), pieces)
+
+
+def top_kernel(sizes, level, arrived, right, square, takes, buffer, solved):
+    taker = take_matrix(sizes, takes[level - 1])
+    value = dot(residual_of(sizes, level, arrived, right, taker), square[...]).astype(BF16)
+    buffer[...] = cross_dot(taker, to_flat(sizes, value)).astype(BF16)
     solved[...] = value
 
 
 def solution_of(sizes, level, arrived, start, product, sends, limits):
-    gathered = spread(sizes, trans_dot(send_matrix(sizes, sends[level]), arrived[...])).astype(BF16)
-    update = trans_dot(product, gathered)
-    update = jnp.where(live(limits, level, update.shape, 0), update, 0.0)
+    gathered = to_rows(sizes, dot(arrived[...].T, send_matrix(sizes, sends[level]))).astype(BF16)
+    update = keep_live(limits, level, dot(gathered, product[...]), 1)
     return (start[...].astype(F32) - update).astype(BF16)
 
 
 def down_kernel(sizes, level, arrived, start, product, sends, limits, takes, buffer, solved):
-    value = solution_of(sizes, level, arrived, start, product[: sizes.rows], sends, limits)
-    buffer[...] = reply(sizes, level, value, takes)
+    value = solution_of(sizes, level, arrived, start, product, sends, limits)
+    taker = take_matrix(sizes, takes[level - 1])
+    buffer[...] = dot(to_flat(sizes, value), taker).astype(BF16).T
     solved[...] = value
 
 
 def last_kernel(sizes, arrived, start, product, sends, limits, *refs):
     above, out, held, done = refs[:-3], refs[-3], refs[-2], refs[-1]
-    count = len(above)
-    for level in range(count):
-        held[level + 1] = above[level][...].T[: sizes.columns]
-    early = fetch(held.at[pl.ds(1, count)], out.at[0, 0, pl.ds(1, count)], done.at[0])
-    held[0] = solution_of(sizes, 0, arrived, start, product[...], sends, limits).T[: sizes.columns]
-    late = fetch(held.at[0], out.at[0, 0, 0], done.at[1])
-    early.wait()
-    late.wait()
+    copies = [fetch(solved, out.at[0, 0, at + 1], done.at[at + 1]) for at, solved in enumerate(above)]
+    held[...] = solution_of(sizes, 0, arrived, start, product, sends, limits)
+    copies.append(fetch(held, out.at[0, 0, 0], done.at[0]))
+    for copy in copies:
+        copy.wait()
 
 
 VMEM = pl.BlockSpec(memory_space=pltpu.VMEM)
@@ -303,18 +287,17 @@
     sizes = Sizes(right_sides, couplings, targets, leaf_axes)
     width, slots, rows, columns, levels = sizes.width, sizes.slots, sizes.rows, sizes.columns, sizes.levels
     top = levels - 1
-    vector = ((width, LANES), BF16)
-    message = ((slots, LANES), BF16)
+    vector = ((columns, width), BF16)
+    message = ((slots, sizes.sub * columns), BF16)
     matrix = ((width, width), BF16)
     coupled = ((rows, width), BF16)
-    stacked = ((rows + width, width), BF16)
     small, large = 10**6, 10**9
 
     def exchange(buffer, level):
         pair = leaf_axes[len(leaf_axes) - 1 - level % sizes.leaf_bits]
-        blocks = buffer.reshape(slots // 2, 2, LANES)
+        blocks = buffer.reshape(slots // 2, 2, buffer.shape[1])
         moved = lax.all_to_all(blocks, ("near", pair, "far"), split_axis=0, concat_axis=0, tiled=True)
-        return moved.reshape(slots, LANES)
+        return moved.reshape(buffer.shape)
 
     inputs = (right_sides, inverses, couplings, widths, targets)
     buffer, *held = call(
@@ -334,24 +317,16 @@
             pltpu.VMEM(*matrix),
             pltpu.VMEM(*coupled),
             pltpu.SMEM((levels,), jnp.int32),
-            pltpu.SemaphoreType.DMA((5,)),
+            pltpu.SemaphoreType.DMA((7,)),
         ),
     )
-    limits = held[1]
-    sends, takes, start, first, last, *planned = call(
+    forward, limits, right, codes = held
+    sends, takes, start, *planned = call(
         functools.partial(plan_kernel, sizes),
         "plan",
-        (inverses, couplings, *held),
+        (inverses, couplings, forward, limits, codes),
         2,
-        (
-            ((top, 1, rows), jnp.int32),
-            ((top, 1, slots), jnp.int32),
-            vector,
-            coupled,
-            matrix,
-            *(vector,) * top,
-            *(stacked,) * (top - 1),
-        ),
+        (((top, 1, rows), jnp.int32), ((top, 1, slots), jnp.int32), vector, *(coupled,) * top, *(matrix,) * top),
         large,
         (
             pltpu.VMEM((levels, width, width), BF16),
@@ -359,14 +334,14 @@
             pltpu.SemaphoreType.DMA((2 * levels,)),
         ),
     )
-    sides, stacks = planned[:top], planned[top:]
+    products, squares = planned[:top], planned[top:]
     starts = [start]
     for level in range(1, top):
         arrived = exchange(buffer, level - 1)
         buffer, start = call(
             functools.partial(up_kernel, sizes, level),
             f"up_{level}",
-            (arrived, sides[level - 1], stacks[level - 1], sends, takes),
+            (arrived, right, products[level], squares[level - 1], sends, takes),
             0,
             (message, vector),
             small,
@@ -376,7 +351,7 @@
     buffer, solved = call(
         functools.partial(top_kernel, sizes, top),
         "top",
-        (arrived, sides[-1], last, takes),
+        (arrived, right, squares[-1], takes),
         0,
         (message, vector),
         small,
@@ -387,7 +362,7 @@
         buffer, solved = call(
             functools.partial(down_kernel, sizes, level),
             f"down_{level}",
-            (arrived, starts[level], stacks[level - 1], sends, limits, takes),
+            (arrived, starts[level], products[level], sends, limits, takes),
             0,
             (message, vector),
             small,
@@ -397,11 +372,11 @@
     (out,) = call(
         functools.partial(last_kernel, sizes),
         "last",
-        (arrived, starts[0], first, sends, limits, *above),
+        (arrived, starts[0], products[0], sends, limits, *above),
         0,
         ((right_sides.shape, BF16),),
         small,
-        (pltpu.VMEM((levels, columns, width), BF16), pltpu.SemaphoreType.DMA((2,))),
+        (pltpu.VMEM(*vector), pltpu.SemaphoreType.DMA((levels,))),
         HBM,
     )
     return jnp.swapaxes(out, 3, 4)

time: 69.1 us -> 67.6 us (0.978)
  Pallas kernels: 11.8 us -> 10.2 us
    pallas_call x8, Pallas kernels: 11.8 us -> 10.2 us  [call(): pl.pallas_call(kernel, in_specs=[HBM] * far + [VMEM] * (len(operands) - f...]
where the time goes in v6:
time: 67.6 us; the launch traced here: 67.3 us
  blocking collectives  45.7 us (68%)
  Pallas kernels  10.2 us (15%)
  starting transfers between devices  7.3 us (11%)
  waiting for transfers between devices  4.05 us (6%)
    all_to_all x5, blocking collectives, exchange(): lax.all_to_all(blocks, ('near', pair, 'far'), split_axis=0, concat_axis=0...  45.7 us
    pallas_call x8, Pallas kernels, call(): pl.pallas_call(kernel, in_specs=[HBM] * far + [VMEM] * (len(operands) - f...  10.2 us
    all_to_all x1, starting transfers between devices, exchange(): lax.all_to_all(blocks, ('near', pair, 'far'), split_axis=0, concat_axis=0...  7.3 us
    all_to_all x1, waiting for transfers between devices, exchange(): lax.all_to_all(blocks, ('near', pair, 'far'), split_axis=0, concat_axis=0...  4.05 us
  transfers between devices with their start and end apart: 1, of which 1 were waited for; matrix products, arithmetic and copies ran while one was open for 0% of the time, Pallas kernels for 5%

profile of v6, /device:TPU:0, one launch (start us, length us, event | category | flops | bytes accessed | tf_op | source)
XLA Modules:
  0.0 67.3 jit_solution(13088873807205749774)
XLA Ops:
  0.0 2.5 %start.1 = (bf16[320,128]{1,0:T(8,128)(2,1)}, bf16[32,512]{1,0:T(8,128)(2,1)S(1)}, s32[4,1,128]{2,1,0:T(1,128)S(1)}, bf16[4,32,512]{2,1,0:T(8,128)(2,1)S(1)}, s32[3,2,16,64]{3,2,1,0:T(8,128)S(1)}) custom-call(bf16[1,1,4,32,512]{4,3,2,1,0:T(8,128)(2,1)} %bitcast.25, bf16[1,1,4,512,512]{4,3,2,1,0:T(8,128)(2,1)} %inverse.3, ...), custom_call_target="tpu_custom_call" | custom-call | flops 1000000000 | bytes 1048576 | tf_op jit(solution)/shard_map/start/pallas_call | solution.py:273
  2.5 7.3 %all-to-all-start = ((bf16[160,2,128]{2,1,0:T(2,128)(2,1)}), bf16[160,2,128]{2,1,0:T(2,128)(2,1)S(1)}, u32[]{:S(2)}, u32[]{:S(2)}) async-start(bf16[160,2,128]{2,1,0:T(2,128)(2,1)} %bitcast.1), calls=%async_computation | async-start | bytes 163840 | tf_op jit(solution)/shard_map/all_to_all | solution.py:299
  9.8 3.4 %plan.1 = (s32[3,1,256]{2,1,0:T(1,128)S(1)}, s32[3,1,320]{2,1,0:T(1,128)S(1)}, bf16[32,512]{1,0:T(8,128)(2,1)S(1)}, bf16[256,512]{1,0:T(8,128)(2,1)S(1)}, bf16[2...) custom-call(bf16[1,1,4,512,512]{4,3,2,1,0:T(8,128)(2,1)} %inverse.3,, ...), custom_call_target="tpu_custom_call" | custom-call | flops 1000000000 | bytes 1048576 | tf_op jit(solution)/shard_map/plan/pallas_call | solution.py:273
  13.2 4.0 %all-to-all-done = bf16[160,2,128]{2,1,0:T(2,128)(2,1)S(1)} async-done(((bf16[160,2,128]{2,1,0:T(2,128)(2,1)}), bf16[160,2,128]{2,1,0:T(2,128)(2,1)S(1)}, u32[]{:S(2)}, u32[]{:S(2)}) %all-to-all-start) | async-done | bytes 81952 | tf_op jit(solution)/shard_map/all_to_all | solution.py:299
  17.3 0.7 %up_1.1 = (bf16[320,128]{1,0:T(8,128)(2,1)S(1)}, bf16[32,512]{1,0:T(8,128)(2,1)S(1)}) custom-call(bf16[320,128]{1,0:T(8,128)(2,1)S(1)} %bitcast.14, bf16[4,32,512]{2,1,0:T(8,128)(2,1)S(1)} %get-tuple-element.30.right, bf16[256,512]{1,0:T(8,128)(2,1)S(1)} %get-tuple-element.34.product, bf16[512,512]{1,0:T(8,128)(2,1)S(1)} %get-tuple-element.35.square, ...), custom_call_target="tpu_custom_call" | custom-call | flops 1000000 | bytes 1048576 | tf_op jit(solution)/shard_map/up_1/pallas_call | solution.py:273
  18.0 9.1 %all_to_all.30 = bf16[160,2,128]{2,1,0:T(2,128)(2,1)S(1)} all-to-all(bf16[160,2,128]{2,1,0:T(2,128)(2,1)S(1)} %bitcast.23), channel_id=1, replica_groups=mesh['leaf0'=2,'far'=4,'near'=4] {'near','leaf0','far'}, dimensions={0} | all-to-all | bytes 163840 | tf_op jit(solution)/shard_map/all_to_all | solution.py:299
  27.1 0.7 %up_2.1 = (bf16[320,128]{1,0:T(8,128)(2,1)S(1)}, bf16[32,512]{1,0:T(8,128)(2,1)S(1)}) custom-call(bf16[320,128]{1,0:T(8,128)(2,1)S(1)} %bitcast.15, bf16[4,32,512]{2,1,0:T(8,128)(2,1)S(1)} %get-tuple-element.30.right, bf16[256,512]{1,0:T(8,128)(2,1)S(1)} %get-tuple-element.39.product, bf16[512,512]{1,0:T(8,128)(2,1)S(1)} %get-tuple-element.40.square, ...), custom_call_target="tpu_custom_call" | custom-call | flops 1000000 | bytes 1048576 | tf_op jit(solution)/shard_map/up_2/pallas_call | solution.py:273
  27.8 9.1 %all_to_all.31 = bf16[160,2,128]{2,1,0:T(2,128)(2,1)S(1)} all-to-all(bf16[160,2,128]{2,1,0:T(2,128)(2,1)S(1)} %bitcast.24), channel_id=1, replica_groups=mesh['leaf0'=2,'far'=4,'near'=4] {'near','leaf0','far'}, dimensions={0} | all-to-all | bytes 163840 | tf_op jit(solution)/shard_map/all_to_all | solution.py:299
  36.9 0.7 %top.1 = (bf16[320,128]{1,0:T(8,128)(2,1)S(1)}, bf16[32,512]{1,0:T(8,128)(2,1)S(1)}) custom-call(bf16[320,128]{1,0:T(8,128)(2,1)S(1)} %bitcast.17, bf16[4,32,512]{2,1,0:T(8,128)(2,1)S(1)} %get-tuple-element.30.right, bf16[512,512]{1,0:T(8,128)(2,1)S(1)} %get-tuple-element.42.square, s32[3,1,320]{2,1,0:T(1,128)S(1)} %get-tuple-element.37.takes), custom_call_target="tpu_custom_call" | custom-call | flops 1000000 | bytes 1048576 | tf_op jit(solution)/shard_map/top/pallas_call | solution.py:273
  37.6 9.1 %all_to_all.32 = bf16[160,2,128]{2,1,0:T(2,128)(2,1)S(1)} all-to-all(bf16[160,2,128]{2,1,0:T(2,128)(2,1)S(1)} %bitcast.21), channel_id=1, replica_groups=mesh['leaf0'=2,'far'=4,'near'=4] {'near','leaf0','far'}, dimensions={0} | all-to-all | bytes 163840 | tf_op jit(solution)/shard_map/all_to_all | solution.py:299
  46.8 0.6 down_2.1
  47.4 9.1 %all_to_all.33 = bf16[160,2,128]{2,1,0:T(2,128)(2,1)S(1)} all-to-all(bf16[160,2,128]{2,1,0:T(2,128)(2,1)S(1)} %bitcast.22), channel_id=1, replica_groups=mesh['leaf0'=2,'far'=4,'near'=4] {'near','leaf0','far'}, dimensions={0} | all-to-all | bytes 163840 | tf_op jit(solution)/shard_map/all_to_all | solution.py:299
  56.5 0.6 down_1.1
  57.1 9.1 %all_to_all.34 = bf16[160,2,128]{2,1,0:T(2,128)(2,1)S(1)} all-to-all(bf16[160,2,128]{2,1,0:T(2,128)(2,1)S(1)} %bitcast.20), channel_id=1, replica_groups=mesh['leaf0'=2,'far'=4,'near'=4] {'near','leaf0','far'}, dimensions={0} | all-to-all | bytes 163840 | tf_op jit(solution)/shard_map/all_to_all | solution.py:299
  66.3 1.0 %last.1 = bf16[1,1,4,32,512]{4,3,2,1,0:T(8,128)(2,1)} custom-call(bf16[320,128]{1,0:T(8,128)(2,1)S(1)} %bitcast.16, bf16[32,512]{1,0:T(8,128)(2,1)S(1)} %get-tuple-element.48.start, bf16[256,512]{1,0:T(8,128)(2,1)S(1)} %get-tuple-element.49.product, s32[3,1,256]{2,1,0:T(1,128)S(1)} %get-tuple-element.36.sends, s32[4,1,128]{2,1,0:T(1,128)S(1)} %get-tuple-element.32.limits, ...), custom_call_target="tpu_custom_call" | custom-call | flops 1000000 | bytes 1048576 | tf_op jit(solution)/shard_map/last/pallas_call | solution.py:273
Async XLA Ops:
  2.5 14.8 %all-to-all-start = ((bf16[160,2,128]{2,1,0:T(2,128)(2,1)}), bf16[160,2,128]{2,1,0:T(2,128)(2,1)S(1)}, u32[]{:S(2)}, u32[]{:S(2)}) async-start(bf16[160,2,128]{2,1,0:T(2,128)(2,1)} %bitcast.1), calls=%async_computation | async-start | bytes 163840 | tf_op jit(solution)/shard_map/all_to_all | solution.py:299

commit v7 on v6

--- a/solution.py
+++ b/solution.py
@@ -158,6 +158,14 @@
     return keep_live(limits, level, product, 1).astype(BF16)
 
 
+def solve_forward(sizes, level, limits, residual, inverse):
+    return keep_live(limits, level, dot_trans(residual, inverse[...]), 1).astype(BF16)
+
+
+def solve_back(sizes, level, limits, solved, inverse):
+    return keep_live(limits, level, dot(solved, inverse[...]), 1).astype(BF16)
+
+
 def fetch(source, target, semaphore):
     copy = pltpu.make_async_copy(source, target, semaphore)
     copy.start()
@@ -187,7 +195,7 @@
     for level in range(sizes.levels):
         limits[level] = jnp.full((1, LANES), widths_in[level] * BLOCK, jnp.int32)
     copies[3].wait()
-    solved = keep_live(limits, 0, dot_trans(right_in[0], inverse_in[...]), 1).astype(BF16)
+    solved = solve_forward(sizes, 0, limits, right_in[0], inverse_in)
     forward[...] = solved
     copies[4].wait()
     buffer[...] = send_pieces(sizes, sender, dot_trans(solved, coupling_in[...]))
@@ -198,12 +206,13 @@
 def plan_kernel(sizes, inverse, coupling, forward, limits, targets, *refs):
     top = sizes.levels - 1
     sends, takes, start = refs[:3]
-    products, squares = refs[3 : 3 + top], refs[3 + top : 3 + 2 * top]
-    inverse_in, coupling_in, done = refs[-3:]
+    products, blocks, square = refs[3 : 3 + top], refs[3 + top : 2 + 2 * top], refs[2 + 2 * top]
+    first_in, top_in, coupling_in, done = refs[-4:]
+    held = (first_in, *blocks, top_in)
     copies = []
     for level in (*range(1, top + 1), 0):
         at = 2 * len(copies)
-        pair = [fetch(inverse.at[0, 0, level], inverse_in.at[level], done.at[at])]
+        pair = [fetch(inverse.at[0, 0, level], held[level], done.at[at])]
         if level < top:
             pair.append(fetch(coupling.at[0, 0, level], coupling_in.at[level], done.at[at + 1]))
         copies.append(pair)
@@ -213,13 +222,12 @@
     for level in (*range(1, top + 1), 0):
         for copy in copies.pop(0):
             copy.wait()
-        block = inverse_in[level]
+        block = held[level][...]
         if level < top:
             products[level][...] = coupled_inverse(sizes, level, limits, block, coupling_in[level])
-        if level > 0:
-            squares[level - 1][...] = squared_inverse(sizes, level, limits, block)
         else:
-            start[...] = keep_live(limits, 0, dot(forward[...], block), 1).astype(BF16)
+            square[...] = squared_inverse(sizes, level, limits, block)
+    start[...] = solve_back(sizes, 0, limits, forward[...], first_in)
 
 
 def residual_of(sizes, level, arrived, right, taker):
@@ -227,11 +235,12 @@
     return (right[level].astype(F32) - incoming).astype(BF16)
 
 
-def up_kernel(sizes, level, arrived, right, product, square, sends, takes, buffer, start):
+def up_kernel(sizes, level, arrived, right, product, inverse, sends, limits, takes, buffer, start):
     residual = residual_of(sizes, level, arrived, right, take_matrix(sizes, takes[level - 1]))
     pieces = dot_trans(residual, product[...])
-    start[...] = dot(residual, square[...]).astype(BF16)
+    solved = solve_forward(sizes, level, limits, residual, inverse)
     buffer[...] = send_pieces(sizes, send_matrix(sizes, sends[level]), pieces)
+    start[...] = solve_back(sizes, level, limits, solved, inverse)
 
 
 def top_kernel(sizes, level, arrived, right, square, takes, buffer, solved):
@@ -329,19 +338,20 @@
         (((top, 1, rows), jnp.int32), ((top, 1, slots), jnp.int32), vector, *(coupled,) * top, *(matrix,) * top),
         large,
         (
-            pltpu.VMEM((levels, width, width), BF16),
+            pltpu.VMEM(*matrix),
+            pltpu.VMEM(*matrix),
             pltpu.VMEM((top, rows, width), BF16),
             pltpu.SemaphoreType.DMA((2 * levels,)),
         ),
     )
-    products, squares = planned[:top], planned[top:]
+    products, blocks = planned[:top], planned[top:]
     starts = [start]
     for level in range(1, top):
         arrived = exchange(buffer, level - 1)
         buffer, start = call(
             functools.partial(up_kernel, sizes, level),
             f"up_{level}",
-            (arrived, right, products[level], squares[level - 1], sends, takes),
+            (arrived, right, products[level], blocks[level - 1], sends, limits, takes),
             0,
             (message, vector),
             small,
@@ -351,7 +361,7 @@
     buffer, solved = call(
         functools.partial(top_kernel, sizes, top),
         "top",
-        (arrived, right, squares[-1], takes),
+        (arrived, right, blocks[-1], takes),
         0,
         (message, vector),
         small,

time: 67.6 us -> 67.6 us (level)
  transfers between devices with their start and end apart: 1 -> 1, of which waited for: 1 -> 1; matrix products, arithmetic and copies ran while one was open for 0% -> 0% of each run, Pallas kernels for 5% -> 4%
where the time goes in v7:
time: 67.6 us; the launch traced here: 67.3 us
  blocking collectives  45.7 us (68%)
  Pallas kernels  9.65 us (14%)
  starting transfers between devices  7.3 us (11%)
  waiting for transfers between devices  4.64 us (7%)
    all_to_all x5, blocking collectives, exchange(): lax.all_to_all(blocks, ('near', pair, 'far'), split_axis=0, concat_axis=0...  45.7 us
    pallas_call x8, Pallas kernels, call(): pl.pallas_call(kernel, in_specs=[HBM] * far + [VMEM] * (len(operands) - f...  9.65 us
    all_to_all x1, starting transfers between devices, exchange(): lax.all_to_all(blocks, ('near', pair, 'far'), split_axis=0, concat_axis=0...  7.3 us
    all_to_all x1, waiting for transfers between devices, exchange(): lax.all_to_all(blocks, ('near', pair, 'far'), split_axis=0, concat_axis=0...  4.64 us
  transfers between devices with their start and end apart: 1, of which 1 were waited for; matrix products, arithmetic and copies ran while one was open for 0% of the time, Pallas kernels for 4%

profile of v7, /device:TPU:0, one launch (start us, length us, event | category | flops | bytes accessed | tf_op | source)
XLA Modules:
  0.0 67.3 jit_solution(1779932058537636992)
XLA Ops:
  0.0 2.5 %start.1 = (bf16[320,128]{1,0:T(8,128)(2,1)}, bf16[32,512]{1,0:T(8,128)(2,1)S(1)}, s32[4,1,128]{2,1,0:T(1,128)S(1)}, bf16[4,32,512]{2,1,0:T(8,128)(2,1)S(1)}, s32[3,2,16,64]{3,2,1,0:T(8,128)S(1)}) custom-call(bf16[1,1,4,32,512]{4,3,2,1,0:T(8,128)(2,1)} %bitcast.25, bf16[1,1,4,512,512]{4,3,2,1,0:T(8,128)(2,1)} %inverse.3, ...), custom_call_target="tpu_custom_call" | custom-call | flops 1000000000 | bytes 1048576 | tf_op jit(solution)/shard_map/start/pallas_call | solution.py:282
  2.5 7.3 %all-to-all-start = ((bf16[160,2,128]{2,1,0:T(2,128)(2,1)}), bf16[160,2,128]{2,1,0:T(2,128)(2,1)S(1)}, u32[]{:S(2)}, u32[]{:S(2)}) async-start(bf16[160,2,128]{2,1,0:T(2,128)(2,1)} %bitcast.1), calls=%async_computation | async-start | bytes 163840 | tf_op jit(solution)/shard_map/all_to_all | solution.py:308
  9.8 2.8 %plan.1 = (s32[3,1,256]{2,1,0:T(1,128)S(1)}, s32[3,1,320]{2,1,0:T(1,128)S(1)}, bf16[32,512]{1,0:T(8,128)(2,1)S(1)}, bf16[256,512]{1,0:T(8,128)(2,1)S(1)}, bf16[2...) custom-call(bf16[1,1,4,512,512]{4,3,2,1,0:T(8,128)(2,1)} %inverse.3,, ...), custom_call_target="tpu_custom_call" | custom-call | flops 1000000000 | bytes 1048576 | tf_op jit(solution)/shard_map/plan/pallas_call | solution.py:282
  12.6 4.6 %all-to-all-done = bf16[160,2,128]{2,1,0:T(2,128)(2,1)S(1)} async-done(((bf16[160,2,128]{2,1,0:T(2,128)(2,1)}), bf16[160,2,128]{2,1,0:T(2,128)(2,1)S(1)}, u32[]{:S(2)}, u32[]{:S(2)}) %all-to-all-start) | async-done | bytes 81952 | tf_op jit(solution)/shard_map/all_to_all | solution.py:308
  17.3 0.7 %up_1.1 = (bf16[320,128]{1,0:T(8,128)(2,1)S(1)}, bf16[32,512]{1,0:T(8,128)(2,1)S(1)}) custom-call(bf16[320,128]{1,0:T(8,128)(2,1)S(1)} %bitcast.14, bf16[4,32,512]{2,1,0:T(8,128)(2,1)S(1)} %get-tuple-element.30.right, bf16[256,512]{1,0:T(8,128)(2,1)S(1)} %get-tuple-element.34.product, bf16[512,512]{1,0:T(8,128)(2,1)S(1)} %get-tuple-element.35.inverse, ...), custom_call_target="tpu_custom_call" | custom-call | flops 1000000 | bytes 1048576 | tf_op jit(solution)/shard_map/up_1/pallas_call | solution.py:282
  18.0 9.1 %all_to_all.30 = bf16[160,2,128]{2,1,0:T(2,128)(2,1)S(1)} all-to-all(bf16[160,2,128]{2,1,0:T(2,128)(2,1)S(1)} %bitcast.23), channel_id=1, replica_groups=mesh['leaf0'=2,'far'=4,'near'=4] {'near','leaf0','far'}, dimensions={0} | all-to-all | bytes 163840 | tf_op jit(solution)/shard_map/all_to_all | solution.py:308
  27.1 0.7 %up_2.1 = (bf16[320,128]{1,0:T(8,128)(2,1)S(1)}, bf16[32,512]{1,0:T(8,128)(2,1)S(1)}) custom-call(bf16[320,128]{1,0:T(8,128)(2,1)S(1)} %bitcast.15, bf16[4,32,512]{2,1,0:T(8,128)(2,1)S(1)} %get-tuple-element.30.right, bf16[256,512]{1,0:T(8,128)(2,1)S(1)} %get-tuple-element.39.product, bf16[512,512]{1,0:T(8,128)(2,1)S(1)} %get-tuple-element.40.inverse, ...), custom_call_target="tpu_custom_call" | custom-call | flops 1000000 | bytes 1048576 | tf_op jit(solution)/shard_map/up_2/pallas_call | solution.py:282
  27.8 9.1 %all_to_all.31 = bf16[160,2,128]{2,1,0:T(2,128)(2,1)S(1)} all-to-all(bf16[160,2,128]{2,1,0:T(2,128)(2,1)S(1)} %bitcast.24), channel_id=1, replica_groups=mesh['leaf0'=2,'far'=4,'near'=4] {'near','leaf0','far'}, dimensions={0} | all-to-all | bytes 163840 | tf_op jit(solution)/shard_map/all_to_all | solution.py:308
  37.0 0.7 %top.1 = (bf16[320,128]{1,0:T(8,128)(2,1)S(1)}, bf16[32,512]{1,0:T(8,128)(2,1)S(1)}) custom-call(bf16[320,128]{1,0:T(8,128)(2,1)S(1)} %bitcast.17, bf16[4,32,512]{2,1,0:T(8,128)(2,1)S(1)} %get-tuple-element.30.right, bf16[512,512]{1,0:T(8,128)(2,1)S(1)} %get-tuple-element.42.square, s32[3,1,320]{2,1,0:T(1,128)S(1)} %get-tuple-element.37.takes), custom_call_target="tpu_custom_call" | custom-call | flops 1000000 | bytes 1048576 | tf_op jit(solution)/shard_map/top/pallas_call | solution.py:282
  37.7 9.1 %all_to_all.32 = bf16[160,2,128]{2,1,0:T(2,128)(2,1)S(1)} all-to-all(bf16[160,2,128]{2,1,0:T(2,128)(2,1)S(1)} %bitcast.21), channel_id=1, replica_groups=mesh['leaf0'=2,'far'=4,'near'=4] {'near','leaf0','far'}, dimensions={0} | all-to-all | bytes 163840 | tf_op jit(solution)/shard_map/all_to_all | solution.py:308
  46.8 0.6 down_2.1
  47.4 9.1 %all_to_all.33 = bf16[160,2,128]{2,1,0:T(2,128)(2,1)S(1)} all-to-all(bf16[160,2,128]{2,1,0:T(2,128)(2,1)S(1)} %bitcast.22), channel_id=1, replica_groups=mesh['leaf0'=2,'far'=4,'near'=4] {'near','leaf0','far'}, dimensions={0} | all-to-all | bytes 163840 | tf_op jit(solution)/shard_map/all_to_all | solution.py:308
  56.5 0.6 down_1.1
  57.2 9.1 %all_to_all.34 = bf16[160,2,128]{2,1,0:T(2,128)(2,1)S(1)} all-to-all(bf16[160,2,128]{2,1,0:T(2,128)(2,1)S(1)} %bitcast.20), channel_id=1, replica_groups=mesh['leaf0'=2,'far'=4,'near'=4] {'near','leaf0','far'}, dimensions={0} | all-to-all | bytes 163840 | tf_op jit(solution)/shard_map/all_to_all | solution.py:308
  66.3 1.0 %last.1 = bf16[1,1,4,32,512]{4,3,2,1,0:T(8,128)(2,1)} custom-call(bf16[320,128]{1,0:T(8,128)(2,1)S(1)} %bitcast.16, bf16[32,512]{1,0:T(8,128)(2,1)S(1)} %get-tuple-element.48.start, bf16[256,512]{1,0:T(8,128)(2,1)S(1)} %get-tuple-element.49.product, s32[3,1,256]{2,1,0:T(1,128)S(1)} %get-tuple-element.36.sends, s32[4,1,128]{2,1,0:T(1,128)S(1)} %get-tuple-element.32.limits, ...), custom_call_target="tpu_custom_call" | custom-call | flops 1000000 | bytes 1048576 | tf_op jit(solution)/shard_map/last/pallas_call | solution.py:282
Async XLA Ops:
  2.5 14.8 %all-to-all-start = ((bf16[160,2,128]{2,1,0:T(2,128)(2,1)}), bf16[160,2,128]{2,1,0:T(2,128)(2,1)S(1)}, u32[]{:S(2)}, u32[]{:S(2)}) async-start(bf16[160,2,128]{2,1,0:T(2,128)(2,1)} %bitcast.1), calls=%async_computation | async-start | bytes 163840 | tf_op jit(solution)/shard_map/all_to_all | solution.py:308

commit v8 on v7

--- a/solution.py
+++ b/solution.py
@@ -177,57 +177,37 @@
 
 
 def start_kernel(sizes, right, inverse, coupling, widths, targets, buffer, forward, limits, *refs):
-    right_in, targets_in, inverse_in, coupling_in, widths_in, done = refs
-    first, others = pl.ds(0, 1), pl.ds(1, sizes.levels - 1)
+    right_in, targets_in, send, next_send, next_take, product = refs[:6]
+    held, below, widths_in, done = refs[6:-3], refs[-3], refs[-2], refs[-1]
+    held = (*held[:3], below, *held[3:])
     copies = [
-        fetch(targets.at[first], targets_in.at[first], done.at[0]),
-        fetch(right.at[0, 0, first], right_in.at[first], done.at[1]),
+        fetch(targets, targets_in, done.at[0]),
+        fetch(right.at[0, 0], right_in, done.at[1]),
         fetch(widths.at[0, 0], widths_in, done.at[2]),
-        fetch(inverse.at[0, 0, 0], inverse_in, done.at[3]),
-        fetch(coupling.at[0, 0, 0], coupling_in, done.at[4]),
-        fetch(right.at[0, 0, others], right_in.at[others], done.at[5]),
-        fetch(targets.at[pl.ds(1, sizes.levels - 2)], targets_in.at[pl.ds(1, sizes.levels - 2)], done.at[6]),
     ]
+    for at, target in enumerate(held):
+        copies.append(fetch((inverse, coupling)[at % 2].at[0, 0, at // 2], target, done.at[3 + at]))
     copies[0].wait()
-    sender = send_matrix(sizes, send_slots(sizes, 0, targets_in))
+    slots = send_slots(sizes, 0, targets_in)
+    send[...] = slots
+    sender = send_matrix(sizes, slots)
     copies[1].wait()
     copies[2].wait()
     for level in range(sizes.levels):
         limits[level] = jnp.full((1, LANES), widths_in[level] * BLOCK, jnp.int32)
-    copies[3].wait()
-    solved = solve_forward(sizes, 0, limits, right_in[0], inverse_in)
+    for copy in copies[3:5]:
+        copy.wait()
+    next_send[...] = send_slots(sizes, 1, targets_in)
+    next_take[...] = take_places(sizes, 0, targets_in)
+    solved = solve_forward(sizes, 0, limits, right_in[0], held[0])
     forward[...] = solved
-    copies[4].wait()
-    buffer[...] = send_pieces(sizes, sender, dot_trans(solved, coupling_in[...]))
-    copies[5].wait()
-    copies[6].wait()
-
-
-def plan_kernel(sizes, inverse, coupling, forward, limits, targets, *refs):
-    top = sizes.levels - 1
-    sends, takes, start = refs[:3]
-    products, blocks, square = refs[3 : 3 + top], refs[3 + top : 2 + 2 * top], refs[2 + 2 * top]
-    first_in, top_in, coupling_in, done = refs[-4:]
-    held = (first_in, *blocks, top_in)
-    copies = []
-    for level in (*range(1, top + 1), 0):
-        at = 2 * len(copies)
-        pair = [fetch(inverse.at[0, 0, level], held[level], done.at[at])]
-        if level < top:
-            pair.append(fetch(coupling.at[0, 0, level], coupling_in.at[level], done.at[at + 1]))
-        copies.append(pair)
-    for level in range(top):
-        sends[level] = send_slots(sizes, level, targets)
-        takes[level] = take_places(sizes, level, targets)
-    for level in (*range(1, top + 1), 0):
-        for copy in copies.pop(0):
-            copy.wait()
-        block = held[level][...]
-        if level < top:
-            products[level][...] = coupled_inverse(sizes, level, limits, block, coupling_in[level])
-        else:
-            square[...] = squared_inverse(sizes, level, limits, block)
-    start[...] = solve_back(sizes, 0, limits, forward[...], first_in)
+    pieces = dot_trans(solved, held[1][...])
+    for copy in copies[5:7]:
+        copy.wait()
+    product[...] = coupled_inverse(sizes, 1, limits, held[2][...], held[3][...])
+    buffer[...] = send_pieces(sizes, sender, pieces)
+    for copy in copies[7:]:
+        copy.wait()
 
 
 def residual_of(sizes, level, arrived, right, taker):
@@ -235,38 +215,45 @@
     return (right[level].astype(F32) - incoming).astype(BF16)
 
 
-def up_kernel(sizes, level, arrived, right, product, inverse, sends, limits, takes, buffer, start):
-    residual = residual_of(sizes, level, arrived, right, take_matrix(sizes, takes[level - 1]))
+def up_kernel(sizes, level, arrived, right, limits, targets, product, inverse, send, take, *refs):
+    block, below, buffer, start, next_take, next_product, *more = refs
+    next_take[...] = take_places(sizes, level, targets)
+    following = (level + 1) % (sizes.levels - 1)
+    if following:
+        more[0][...] = send_slots(sizes, following, targets)
+    residual = residual_of(sizes, level, arrived, right, take_matrix(sizes, take[...]))
     pieces = dot_trans(residual, product[...])
+    next_product[...] = coupled_inverse(sizes, following, limits, block[...], below[...])
     solved = solve_forward(sizes, level, limits, residual, inverse)
-    buffer[...] = send_pieces(sizes, send_matrix(sizes, sends[level]), pieces)
+    buffer[...] = send_pieces(sizes, send_matrix(sizes, send[...]), pieces)
     start[...] = solve_back(sizes, level, limits, solved, inverse)
 
 
-def top_kernel(sizes, level, arrived, right, square, takes, buffer, solved):
-    taker = take_matrix(sizes, takes[level - 1])
-    value = dot(residual_of(sizes, level, arrived, right, taker), square[...]).astype(BF16)
+def top_kernel(sizes, level, arrived, right, limits, inverse, take, forward, first, buffer, solution, start):
+    taker = take_matrix(sizes, take[...])
+    solved = solve_forward(sizes, level, limits, residual_of(sizes, level, arrived, right, taker), inverse)
+    start[...] = solve_back(sizes, 0, limits, forward[...], first)
+    value = solve_back(sizes, level, limits, solved, inverse)
     buffer[...] = cross_dot(taker, to_flat(sizes, value)).astype(BF16)
-    solved[...] = value
-
-
-def solution_of(sizes, level, arrived, start, product, sends, limits):
-    gathered = to_rows(sizes, dot(arrived[...].T, send_matrix(sizes, sends[level]))).astype(BF16)
+    solution[...] = value
+
+
+def solution_of(sizes, level, arrived, start, product, send, limits):
+    gathered = to_rows(sizes, dot(arrived[...].T, send_matrix(sizes, send[...]))).astype(BF16)
     update = keep_live(limits, level, dot(gathered, product[...]), 1)
     return (start[...].astype(F32) - update).astype(BF16)
 
 
-def down_kernel(sizes, level, arrived, start, product, sends, limits, takes, buffer, solved):
-    value = solution_of(sizes, level, arrived, start, product, sends, limits)
-    taker = take_matrix(sizes, takes[level - 1])
-    buffer[...] = dot(to_flat(sizes, value), taker).astype(BF16).T
+def down_kernel(sizes, level, arrived, start, product, send, limits, take, buffer, solved):
+    value = solution_of(sizes, level, arrived, start, product, send, limits)
+    buffer[...] = dot(to_flat(sizes, value), take_matrix(sizes, take[...])).astype(BF16).T
     solved[...] = value
 
 
-def last_kernel(sizes, arrived, start, product, sends, limits, *refs):
+def last_kernel(sizes, arrived, start, product, send, limits, *refs):
     above, out, held, done = refs[:-3], refs[-3], refs[-2], refs[-1]
     copies = [fetch(solved, out.at[0, 0, at + 1], done.at[at + 1]) for at, solved in enumerate(above)]
-    held[...] = solution_of(sizes, 0, arrived, start, product, sends, limits)
+    held[...] = solution_of(sizes, 0, arrived, start, product, send, limits)
     copies.append(fetch(held, out.at[0, 0, 0], done.at[0]))
     for copy in copies:
         copy.wait()
@@ -300,6 +287,7 @@
     message = ((slots, sizes.sub * columns), BF16)
     matrix = ((width, width), BF16)
     coupled = ((rows, width), BF16)
+    send_row, take_row = ((1, rows), jnp.int32), ((1, slots), jnp.int32)
     small, large = 10**6, 10**9
 
     def exchange(buffer, level):
@@ -309,7 +297,7 @@
         return moved.reshape(buffer.shape)
 
     inputs = (right_sides, inverses, couplings, widths, targets)
-    buffer, *held = call(
+    buffer, forward, limits, right, codes, send, next_send, take, product, *held = call(
         functools.partial(start_kernel, sizes),
         "start",
         inputs,
@@ -320,50 +308,45 @@
             ((levels, 1, LANES), jnp.int32),
             ((levels, columns, width), BF16),
             (targets.shape, jnp.int32),
+            send_row,
+            send_row,
+            take_row,
+            coupled,
+            matrix,
+            coupled,
+            matrix,
+            *(matrix, coupled) * (top - 2),
+            matrix,
         ),
         large,
-        (
-            pltpu.VMEM(*matrix),
-            pltpu.VMEM(*coupled),
-            pltpu.SMEM((levels,), jnp.int32),
-            pltpu.SemaphoreType.DMA((7,)),
-        ),
+        (pltpu.VMEM(*coupled), pltpu.SMEM((levels,), jnp.int32), pltpu.SemaphoreType.DMA((4 + 2 * top,))),
     )
-    forward, limits, right, codes = held
-    sends, takes, start, *planned = call(
-        functools.partial(plan_kernel, sizes),
-        "plan",
-        (inverses, couplings, forward, limits, codes),
-        2,
-        (((top, 1, rows), jnp.int32), ((top, 1, slots), jnp.int32), vector, *(coupled,) * top, *(matrix,) * top),
-        large,
-        (
-            pltpu.VMEM(*matrix),
-            pltpu.VMEM(*matrix),
-            pltpu.VMEM((top, rows, width), BF16),
-            pltpu.SemaphoreType.DMA((2 * levels,)),
-        ),
-    )
-    products, blocks = planned[:top], planned[top:]
-    starts = [start]
+    held.insert(3, None)
+    blocks, below = held[::2], held[1::2]
+    sends, takes, products, starts = [send, next_send], [take], [None, product], [None]
     for level in range(1, top):
         arrived = exchange(buffer, level - 1)
-        buffer, start = call(
+        following = (level + 1) % top
+        buffer, start, take, product, *more = call(
             functools.partial(up_kernel, sizes, level),
             f"up_{level}",
-            (arrived, right, products[level], blocks[level - 1], sends, limits, takes),
+            (arrived, right, limits, codes, products[level], blocks[level], sends[level], takes[-1], blocks[following], below[following]),
             0,
-            (message, vector),
+            (message, vector, take_row, coupled, *((send_row,) if following else ())),
             small,
         )
         starts.append(start)
+        takes.append(take)
+        sends.extend(more)
+        products.append(product)
     arrived = exchange(buffer, top - 1)
-    buffer, solved = call(
+    products[0] = products.pop()
+    buffer, solved, starts[0] = call(
         functools.partial(top_kernel, sizes, top),
         "top",
-        (arrived, right, blocks[-1], takes),
+        (arrived, right, limits, blocks[top], takes[-1], forward, blocks[0]),
         0,
-        (message, vector),
+        (message, vector, vector),
         small,
     )
     above = [solved]
@@ -372,7 +355,7 @@
         buffer, solved = call(
             functools.partial(down_kernel, sizes, level),
             f"down_{level}",
-            (arrived, starts[level], products[level], sends, limits, takes),
+            (arrived, starts[level], products[level], sends[level], limits, takes[level - 1]),
             0,
             (message, vector),
             small,
@@ -382,7 +365,7 @@
     (out,) = call(
         functools.partial(last_kernel, sizes),
         "last",
-        (arrived, starts[0], products[0], sends, limits, *above),
+        (arrived, starts[0], products[0], sends[0], limits, *above),
         0,
         ((right_sides.shape, BF16),),
         small,

time: 67.6 us -> 67.4 us (level)
  blocking collectives: 45.7 us -> 60.2 us
  starting transfers between devices: 7.3 us -> 0 us
  waiting for transfers between devices: 4.64 us -> 0 us
  Pallas kernels: 9.65 us -> 6.96 us
    all_to_all x5 -> x6, blocking collectives: 45.7 us -> 60.2 us  [exchange(): lax.all_to_all(blocks, ('near', pair, 'far'), split_axis=0, concat_axis=0...]
    all_to_all x1 -> x0, starting transfers between devices: 7.3 us -> none  [exchange(): lax.all_to_all(blocks, ('near', pair, 'far'), split_axis=0, concat_axis=0...]
    all_to_all x1 -> x0, waiting for transfers between devices: 4.64 us -> none  [exchange(): lax.all_to_all(blocks, ('near', pair, 'far'), split_axis=0, concat_axis=0...]
    pallas_call x8 -> x7, Pallas kernels: 9.65 us -> 6.96 us  [call(): pl.pallas_call(kernel, in_specs=[HBM] * far + [VMEM] * (len(operands) - f...]
  transfers between devices with their start and end apart: 1 -> 0, of which waited for: 1 -> 0; matrix products, arithmetic and copies ran while one was open for 0% -> 0% of each run, Pallas kernels for 4% -> 0%
where the time goes in v8:
time: 67.4 us; the launch traced here: 67.2 us
  blocking collectives  60.2 us (89%)
  Pallas kernels  6.96 us (10%)
    all_to_all x6, blocking collectives, exchange(): lax.all_to_all(blocks, ('near', pair, 'far'), split_axis=0, concat_axis=0...  60.2 us
    pallas_call x7, Pallas kernels, call(): pl.pallas_call(kernel, in_specs=[HBM] * far + [VMEM] * (len(operands) - f...  6.96 us

profile of v8, /device:TPU:0, one launch (start us, length us, event | category | flops | bytes accessed | tf_op | source)
XLA Modules:
  0.0 67.2 jit_solution(13513602348835014506)
XLA Ops:
  0.0 2.2 %start.1 = (bf16[320,128]{1,0:T(8,128)(2,1)S(1)}, bf16[32,512]{1,0:T(8,128)(2,1)S(1)}, s32[4,1,128]{2,1,0:T(1,128)S(1)}, bf16[4,32,512]{2,1,0:T(8,128)(2,1)S(1)}...) custom-call(bf16[1,1,4,32,512]{4,3,2,1,0:T(8,128)(2,1)} %bitcast.26,, ...), custom_call_target="tpu_custom_call" | custom-call | flops 1000000000 | bytes 1048576 | tf_op jit(solution)/shard_map/start/pallas_call | solution.py:269
  2.2 14.5 %all_to_all.30 = bf16[160,2,128]{2,1,0:T(2,128)(2,1)S(1)} all-to-all(bf16[160,2,128]{2,1,0:T(2,128)(2,1)S(1)} %bitcast.20), channel_id=1, replica_groups=mesh['leaf0'=2,'far'=4,'near'=4] {'near','leaf0','far'}, dimensions={0} | all-to-all | bytes 163840 | tf_op jit(solution)/shard_map/all_to_all | solution.py:296
  16.7 0.8 %up_1.1 = (bf16[320,128]{1,0:T(8,128)(2,1)S(1)}, bf16[32,512]{1,0:T(8,128)(2,1)S(1)}, s32[1,320]{1,0:T(1,128)S(1)}, bf16[256,512]{1,0:T(8,128)(2,1)S(1)}, s32[1,256]{1,0:T(1,128)S(1)}) custom-call(bf16[320,128]{1,0:T(8,128)(2,1)S(1)} %bitcast.14, bf16[4,32,512]{2,1,0:T(8,128)(2,1)S(1)} %get-tuple-element.37.right, ...), custom_call_target="tpu_custom_call" | custom-call | flops 1000000 | bytes 1048576 | tf_op jit(solution)/shard_map/up_1/pallas_call | solution.py:269
  17.6 9.1 %all_to_all.31 = bf16[160,2,128]{2,1,0:T(2,128)(2,1)S(1)} all-to-all(bf16[160,2,128]{2,1,0:T(2,128)(2,1)S(1)} %bitcast.22), channel_id=1, replica_groups=mesh['leaf0'=2,'far'=4,'near'=4] {'near','leaf0','far'}, dimensions={0} | all-to-all | bytes 163840 | tf_op jit(solution)/shard_map/all_to_all | solution.py:296
  26.7 0.8 %up_2.1 = (bf16[320,128]{1,0:T(8,128)(2,1)S(1)}, bf16[32,512]{1,0:T(8,128)(2,1)S(1)}, s32[1,320]{1,0:T(1,128)S(1)}, bf16[256,512]{1,0:T(8,128)(2,1)S(1)}) custom-call(bf16[320,128]{1,0:T(8,128)(2,1)S(1)} %bitcast.15, bf16[4,32,512]{2,1,0:T(8,128)(2,1)S(1)} %get-tuple-element.37.right, s32[4,1,128]{2,1,0:T(1,128)S(1)} %get-tuple-element.38.limits, ...), custom_call_target="tpu_custom_call" | custom-call | flops 1000000 | bytes 1048576 | tf_op jit(solution)/shard_map/up_2/pallas_call | solution.py:269
  27.5 9.1 %all_to_all.32 = bf16[160,2,128]{2,1,0:T(2,128)(2,1)S(1)} all-to-all(bf16[160,2,128]{2,1,0:T(2,128)(2,1)S(1)} %bitcast.23), channel_id=1, replica_groups=mesh['leaf0'=2,'far'=4,'near'=4] {'near','leaf0','far'}, dimensions={0} | all-to-all | bytes 163840 | tf_op jit(solution)/shard_map/all_to_all | solution.py:296
  36.6 0.9 %top.1 = (bf16[320,128]{1,0:T(8,128)(2,1)S(1)}, bf16[32,512]{1,0:T(8,128)(2,1)S(1)}, bf16[32,512]{1,0:T(8,128)(2,1)S(1)}) custom-call(bf16[320,128]{1,0:T(8,128)(2,1)S(1)} %bitcast.19, bf16[4,32,512]{2,1,0:T(8,128)(2,1)S(1)} %get-tuple-element.37.right, s32[4,1,128]{2,1,0:T(1,128)S(1)} %get-tuple-element.38.limits, ...), custom_call_target="tpu_custom_call" | custom-call | flops 1000000 | bytes 1048576 | tf_op jit(solution)/shard_map/top/pallas_call | solution.py:269
  37.5 9.1 %all_to_all.33 = bf16[160,2,128]{2,1,0:T(2,128)(2,1)S(1)} all-to-all(bf16[160,2,128]{2,1,0:T(2,128)(2,1)S(1)} %bitcast.21), channel_id=1, replica_groups=mesh['leaf0'=2,'far'=4,'near'=4] {'near','leaf0','far'}, dimensions={0} | all-to-all | bytes 163840 | tf_op jit(solution)/shard_map/all_to_all | solution.py:296
  46.7 0.6 down_2.1
  47.3 9.1 %all_to_all.34 = bf16[160,2,128]{2,1,0:T(2,128)(2,1)S(1)} all-to-all(bf16[160,2,128]{2,1,0:T(2,128)(2,1)S(1)} %bitcast.24), channel_id=1, replica_groups=mesh['leaf0'=2,'far'=4,'near'=4] {'near','leaf0','far'}, dimensions={0} | all-to-all | bytes 163840 | tf_op jit(solution)/shard_map/all_to_all | solution.py:296
  56.4 0.6 down_1.1
  57.0 9.1 %all_to_all.35 = bf16[160,2,128]{2,1,0:T(2,128)(2,1)S(1)} all-to-all(bf16[160,2,128]{2,1,0:T(2,128)(2,1)S(1)} %bitcast.25), channel_id=1, replica_groups=mesh['leaf0'=2,'far'=4,'near'=4] {'near','leaf0','far'}, dimensions={0} | all-to-all | bytes 163840 | tf_op jit(solution)/shard_map/all_to_all | solution.py:296
  66.2 1.0 %last.1 = bf16[1,1,4,32,512]{4,3,2,1,0:T(8,128)(2,1)} custom-call(bf16[320,128]{1,0:T(8,128)(2,1)S(1)} %bitcast.16, bf16[32,512]{1,0:T(8,128)(2,1)S(1)} %get-tuple-element.61.start, bf16[256,512]{1,0:T(8,128)(2,1)S(1)} %get-tuple-element.62.product, s32[1,256]{1,0:T(1,128)S(1)} %get-tuple-element.63.send, s32[4,1,128]{2,1,0:T(1,128)S(1)} %get-tuple-element.38.limits, ...), custom_call_target="tpu_custom_call" | custom-call | flops 1000000 | bytes 1048576 | tf_op jit(solution)/shard_map/last/pallas_call | solution.py:269

commit v9 on v8

--- a/solution.py
+++ b/solution.py
@@ -95,7 +95,27 @@
 
 
 def turn(sizes, half, owner):
-    return (within(owner, sizes.near) * 2 + half) * sizes.far + over(owner, sizes.near)
+    at = (within(owner, sizes.near) * 2 + half) * sizes.far + over(owner, sizes.near)
+    shift = 1
+    while shift < 2 * sizes.owners:
+        at = jnp.bitwise_xor(at, lax.shift_right_logical(at, shift))
+        shift *= 2
+    return at
+
+
+def turns(sizes, bit):
+    low = 2**bit
+    order = []
+    for group in range(2 ** sizes.leaf_bits):
+        if group & low:
+            continue
+        members = []
+        for at in range(2 * sizes.owners):
+            at ^= at >> 1
+            near, half, far = at // (2 * sizes.far), at // sizes.far % 2, at % sizes.far
+            members.append((group + half * low) * sizes.owners + far * sizes.near + near)
+        order.append(members)
+    return order
 
 
 def send_slots(sizes, level, targets):
@@ -291,9 +311,10 @@
     small, large = 10**6, 10**9
 
     def exchange(buffer, level):
-        pair = leaf_axes[len(leaf_axes) - 1 - level % sizes.leaf_bits]
+        order = turns(sizes, level % sizes.leaf_bits)
         blocks = buffer.reshape(slots // 2, 2, buffer.shape[1])
-        moved = lax.all_to_all(blocks, ("near", pair, "far"), split_axis=0, concat_axis=0, tiled=True)
+        axes = (*leaf_axes, "far", "near")
+        moved = lax.all_to_all(blocks, axes, split_axis=0, concat_axis=0, tiled=True, axis_index_groups=order)
         return moved.reshape(buffer.shape)
 
     inputs = (right_sides, inverses, couplings, widths, targets)

time: 67.4 us -> 65.8 us (0.976)
  blocking collectives: 60.2 us -> 58.5 us
    all_to_all x6, blocking collectives: 60.2 us -> 58.5 us  [exchange(): lax.all_to_all(blocks, axes, split_axis=0, concat_axis=0, tiled=True, axi...]
where the time goes in v9:
time: 65.8 us; the launch traced here: 65.5 us
  blocking collectives  58.5 us (89%)
  Pallas kernels  6.94 us (11%)
    all_to_all x6, blocking collectives, exchange(): lax.all_to_all(blocks, axes, split_axis=0, concat_axis=0, tiled=True, axi...  58.5 us
    pallas_call x7, Pallas kernels, call(): pl.pallas_call(kernel, in_specs=[HBM] * far + [VMEM] * (len(operands) - f...  6.94 us

profile of v9, /device:TPU:0, one launch (start us, length us, event | category | flops | bytes accessed | tf_op | source)
XLA Modules:
  0.0 65.5 jit_solution(10440730478717202637)
XLA Ops:
  0.0 2.2 %start.1 = (bf16[320,128]{1,0:T(8,128)(2,1)S(1)}, bf16[32,512]{1,0:T(8,128)(2,1)S(1)}, s32[4,1,128]{2,1,0:T(1,128)S(1)}, bf16[4,32,512]{2,1,0:T(8,128)(2,1)S(1)}...) custom-call(bf16[1,1,4,32,512]{4,3,2,1,0:T(8,128)(2,1)} %bitcast.26,, ...), custom_call_target="tpu_custom_call" | custom-call | flops 1000000000 | bytes 1048576 | tf_op jit(solution)/shard_map/start/pallas_call | solution.py:289
  2.2 14.3 %all_to_all.30 = bf16[160,2,128]{2,1,0:T(2,128)(2,1)S(1)} all-to-all(bf16[160,2,128]{2,1,0:T(2,128)(2,1)S(1)} %bitcast.20), channel_id=1, replica_groups={{0,4,12,8,24,28,20,16,17,21,29,25,9,13,5,1,3,7,15,11,27,31,23,19,18,22,..., dimensions={0} | all-to-all | bytes 163840 | tf_op jit(solution)/shard_map/all_to_all | solution.py:317
  16.5 0.8 %up_1.1 = (bf16[320,128]{1,0:T(8,128)(2,1)S(1)}, bf16[32,512]{1,0:T(8,128)(2,1)S(1)}, s32[1,320]{1,0:T(1,128)S(1)}, bf16[256,512]{1,0:T(8,128)(2,1)S(1)}, s32[1,256]{1,0:T(1,128)S(1)}) custom-call(bf16[320,128]{1,0:T(8,128)(2,1)S(1)} %bitcast.14, bf16[4,32,512]{2,1,0:T(8,128)(2,1)S(1)} %get-tuple-element.37.right, ...), custom_call_target="tpu_custom_call" | custom-call | flops 1000000 | bytes 1048576 | tf_op jit(solution)/shard_map/up_1/pallas_call | solution.py:289
  17.3 8.8 %all_to_all.31 = bf16[160,2,128]{2,1,0:T(2,128)(2,1)S(1)} all-to-all(bf16[160,2,128]{2,1,0:T(2,128)(2,1)S(1)} %bitcast.22), channel_id=1, replica_groups={{0,4,12,8,24,28,20,16,17,21,29,25,9,13,5,1,3,7,15,11,27,31,23,19,18,22,..., dimensions={0} | all-to-all | bytes 163840 | tf_op jit(solution)/shard_map/all_to_all | solution.py:317
  26.1 0.8 %up_2.1 = (bf16[320,128]{1,0:T(8,128)(2,1)S(1)}, bf16[32,512]{1,0:T(8,128)(2,1)S(1)}, s32[1,320]{1,0:T(1,128)S(1)}, bf16[256,512]{1,0:T(8,128)(2,1)S(1)}) custom-call(bf16[320,128]{1,0:T(8,128)(2,1)S(1)} %bitcast.15, bf16[4,32,512]{2,1,0:T(8,128)(2,1)S(1)} %get-tuple-element.37.right, s32[4,1,128]{2,1,0:T(1,128)S(1)} %get-tuple-element.38.limits, ...), custom_call_target="tpu_custom_call" | custom-call | flops 1000000 | bytes 1048576 | tf_op jit(solution)/shard_map/up_2/pallas_call | solution.py:289
  26.9 8.8 %all_to_all.32 = bf16[160,2,128]{2,1,0:T(2,128)(2,1)S(1)} all-to-all(bf16[160,2,128]{2,1,0:T(2,128)(2,1)S(1)} %bitcast.23), channel_id=1, replica_groups={{0,4,12,8,24,28,20,16,17,21,29,25,9,13,5,1,3,7,15,11,27,31,23,19,18,22,..., dimensions={0} | all-to-all | bytes 163840 | tf_op jit(solution)/shard_map/all_to_all | solution.py:317
  35.8 0.9 %top.1 = (bf16[320,128]{1,0:T(8,128)(2,1)S(1)}, bf16[32,512]{1,0:T(8,128)(2,1)S(1)}, bf16[32,512]{1,0:T(8,128)(2,1)S(1)}) custom-call(bf16[320,128]{1,0:T(8,128)(2,1)S(1)} %bitcast.19, bf16[4,32,512]{2,1,0:T(8,128)(2,1)S(1)} %get-tuple-element.37.right, s32[4,1,128]{2,1,0:T(1,128)S(1)} %get-tuple-element.38.limits, ...), custom_call_target="tpu_custom_call" | custom-call | flops 1000000 | bytes 1048576 | tf_op jit(solution)/shard_map/top/pallas_call | solution.py:289
  36.7 8.9 %all_to_all.33 = bf16[160,2,128]{2,1,0:T(2,128)(2,1)S(1)} all-to-all(bf16[160,2,128]{2,1,0:T(2,128)(2,1)S(1)} %bitcast.21), channel_id=1, replica_groups={{0,4,12,8,24,28,20,16,17,21,29,25,9,13,5,1,3,7,15,11,27,31,23,19,18,22,..., dimensions={0} | all-to-all | bytes 163840 | tf_op jit(solution)/shard_map/all_to_all | solution.py:317
  45.5 0.6 down_2.1
  46.2 8.9 %all_to_all.34 = bf16[160,2,128]{2,1,0:T(2,128)(2,1)S(1)} all-to-all(bf16[160,2,128]{2,1,0:T(2,128)(2,1)S(1)} %bitcast.24), channel_id=1, replica_groups={{0,4,12,8,24,28,20,16,17,21,29,25,9,13,5,1,3,7,15,11,27,31,23,19,18,22,..., dimensions={0} | all-to-all | bytes 163840 | tf_op jit(solution)/shard_map/all_to_all | solution.py:317
  55.0 0.6 down_1.1
  55.6 8.9 %all_to_all.35 = bf16[160,2,128]{2,1,0:T(2,128)(2,1)S(1)} all-to-all(bf16[160,2,128]{2,1,0:T(2,128)(2,1)S(1)} %bitcast.25), channel_id=1, replica_groups={{0,4,12,8,24,28,20,16,17,21,29,25,9,13,5,1,3,7,15,11,27,31,23,19,18,22,..., dimensions={0} | all-to-all | bytes 163840 | tf_op jit(solution)/shard_map/all_to_all | solution.py:317
  64.5 1.0 %last.1 = bf16[1,1,4,32,512]{4,3,2,1,0:T(8,128)(2,1)} custom-call(bf16[320,128]{1,0:T(8,128)(2,1)S(1)} %bitcast.16, bf16[32,512]{1,0:T(8,128)(2,1)S(1)} %get-tuple-element.61.start, bf16[256,512]{1,0:T(8,128)(2,1)S(1)} %get-tuple-element.62.product, s32[1,256]{1,0:T(1,128)S(1)} %get-tuple-element.63.send, s32[4,1,128]{2,1,0:T(1,128)S(1)} %get-tuple-element.38.limits, ...), custom_call_target="tpu_custom_call" | custom-call | flops 1000000 | bytes 1048576 | tf_op jit(solution)/shard_map/last/pallas_call | solution.py:289

commit v10 on v7

--- a/solution.py
+++ b/solution.py
@@ -95,7 +95,27 @@
 
 
 def turn(sizes, half, owner):
-    return (within(owner, sizes.near) * 2 + half) * sizes.far + over(owner, sizes.near)
+    at = (within(owner, sizes.near) * 2 + half) * sizes.far + over(owner, sizes.near)
+    shift = 1
+    while shift < 2 * sizes.owners:
+        at = jnp.bitwise_xor(at, lax.shift_right_logical(at, shift))
+        shift *= 2
+    return at
+
+
+def turns(sizes, bit):
+    low = 2**bit
+    order = []
+    for group in range(2 ** sizes.leaf_bits):
+        if group & low:
+            continue
+        members = []
+        for at in range(2 * sizes.owners):
+            at ^= at >> 1
+            near, half, far = at // (2 * sizes.far), at // sizes.far % 2, at % sizes.far
+            members.append((group + half * low) * sizes.owners + far * sizes.near + near)
+        order.append(members)
+    return order
 
 
 def send_slots(sizes, level, targets):
@@ -303,9 +323,10 @@
     small, large = 10**6, 10**9
 
     def exchange(buffer, level):
-        pair = leaf_axes[len(leaf_axes) - 1 - level % sizes.leaf_bits]
+        order = turns(sizes, level % sizes.leaf_bits)
         blocks = buffer.reshape(slots // 2, 2, buffer.shape[1])
-        moved = lax.all_to_all(blocks, ("near", pair, "far"), split_axis=0, concat_axis=0, tiled=True)
+        axes = (*leaf_axes, "far", "near")
+        moved = lax.all_to_all(blocks, axes, split_axis=0, concat_axis=0, tiled=True, axis_index_groups=order)
         return moved.reshape(buffer.shape)
 
     inputs = (right_sides, inverses, couplings, widths, targets)

time: 67.6 us -> 66.1 us (0.978)
  blocking collectives: 45.7 us -> 44.3 us
    all_to_all x5, blocking collectives: 45.7 us -> 44.3 us  [exchange(): lax.all_to_all(blocks, axes, split_axis=0, concat_axis=0, tiled=True, axi...]
where the time goes in v10:
time: 66.1 us; the launch traced here: 65.6 us
  blocking collectives  44.3 us (67%)
  Pallas kernels  9.65 us (15%)
  starting transfers between devices  7.3 us (11%)
  waiting for transfers between devices  4.36 us (7%)
    all_to_all x5, blocking collectives, exchange(): lax.all_to_all(blocks, axes, split_axis=0, concat_axis=0, tiled=True, axi...  44.3 us
    pallas_call x8, Pallas kernels, call(): pl.pallas_call(kernel, in_specs=[HBM] * far + [VMEM] * (len(operands) - f...  9.65 us
    all_to_all x1, starting transfers between devices, exchange(): lax.all_to_all(blocks, axes, split_axis=0, concat_axis=0, tiled=True, axi...  7.3 us
    all_to_all x1, waiting for transfers between devices, exchange(): lax.all_to_all(blocks, axes, split_axis=0, concat_axis=0, tiled=True, axi...  4.36 us
  transfers between devices with their start and end apart: 1, of which 1 were waited for; matrix products, arithmetic and copies ran while one was open for 0% of the time, Pallas kernels for 4%

profile of v10, /device:TPU:0, one launch (start us, length us, event | category | flops | bytes accessed | tf_op | source)
XLA Modules:
  0.0 65.6 jit_solution(7919049711007426943)
XLA Ops:
  0.0 2.5 %start.1 = (bf16[320,128]{1,0:T(8,128)(2,1)}, bf16[32,512]{1,0:T(8,128)(2,1)S(1)}, s32[4,1,128]{2,1,0:T(1,128)S(1)}, bf16[4,32,512]{2,1,0:T(8,128)(2,1)S(1)}, s32[3,2,16,64]{3,2,1,0:T(8,128)S(1)}) custom-call(bf16[1,1,4,32,512]{4,3,2,1,0:T(8,128)(2,1)} %bitcast.25, bf16[1,1,4,512,512]{4,3,2,1,0:T(8,128)(2,1)} %inverse.3, ...), custom_call_target="tpu_custom_call" | custom-call | flops 1000000000 | bytes 1048576 | tf_op jit(solution)/shard_map/start/pallas_call | solution.py:302
  2.5 7.3 %all-to-all-start = ((bf16[160,2,128]{2,1,0:T(2,128)(2,1)}), bf16[160,2,128]{2,1,0:T(2,128)(2,1)S(1)}, u32[]{:S(2)}, u32[]{:S(2)}) async-start(bf16[160,2,128]{2,1,0:T(2,128)(2,1)} %bitcast.1), calls=%async_computation | async-start | bytes 163840 | tf_op jit(solution)/shard_map/all_to_all | solution.py:329
  9.8 2.8 %plan.1 = (s32[3,1,256]{2,1,0:T(1,128)S(1)}, s32[3,1,320]{2,1,0:T(1,128)S(1)}, bf16[32,512]{1,0:T(8,128)(2,1)S(1)}, bf16[256,512]{1,0:T(8,128)(2,1)S(1)}, bf16[2...) custom-call(bf16[1,1,4,512,512]{4,3,2,1,0:T(8,128)(2,1)} %inverse.3,, ...), custom_call_target="tpu_custom_call" | custom-call | flops 1000000000 | bytes 1048576 | tf_op jit(solution)/shard_map/plan/pallas_call | solution.py:302
  12.6 4.4 %all-to-all-done = bf16[160,2,128]{2,1,0:T(2,128)(2,1)S(1)} async-done(((bf16[160,2,128]{2,1,0:T(2,128)(2,1)}), bf16[160,2,128]{2,1,0:T(2,128)(2,1)S(1)}, u32[]{:S(2)}, u32[]{:S(2)}) %all-to-all-start) | async-done | bytes 81952 | tf_op jit(solution)/shard_map/all_to_all | solution.py:329
  17.0 0.7 %up_1.1 = (bf16[320,128]{1,0:T(8,128)(2,1)S(1)}, bf16[32,512]{1,0:T(8,128)(2,1)S(1)}) custom-call(bf16[320,128]{1,0:T(8,128)(2,1)S(1)} %bitcast.14, bf16[4,32,512]{2,1,0:T(8,128)(2,1)S(1)} %get-tuple-element.30.right, bf16[256,512]{1,0:T(8,128)(2,1)S(1)} %get-tuple-element.34.product, bf16[512,512]{1,0:T(8,128)(2,1)S(1)} %get-tuple-element.35.inverse, ...), custom_call_target="tpu_custom_call" | custom-call | flops 1000000 | bytes 1048576 | tf_op jit(solution)/shard_map/up_1/pallas_call | solution.py:302
  17.7 8.9 %all_to_all.30 = bf16[160,2,128]{2,1,0:T(2,128)(2,1)S(1)} all-to-all(bf16[160,2,128]{2,1,0:T(2,128)(2,1)S(1)} %bitcast.23), channel_id=1, replica_groups={{0,4,12,8,24,28,20,16,17,21,29,25,9,13,5,1,3,7,15,11,27,31,23,19,18,22,..., dimensions={0} | all-to-all | bytes 163840 | tf_op jit(solution)/shard_map/all_to_all | solution.py:329
  26.6 0.7 %up_2.1 = (bf16[320,128]{1,0:T(8,128)(2,1)S(1)}, bf16[32,512]{1,0:T(8,128)(2,1)S(1)}) custom-call(bf16[320,128]{1,0:T(8,128)(2,1)S(1)} %bitcast.15, bf16[4,32,512]{2,1,0:T(8,128)(2,1)S(1)} %get-tuple-element.30.right, bf16[256,512]{1,0:T(8,128)(2,1)S(1)} %get-tuple-element.39.product, bf16[512,512]{1,0:T(8,128)(2,1)S(1)} %get-tuple-element.40.inverse, ...), custom_call_target="tpu_custom_call" | custom-call | flops 1000000 | bytes 1048576 | tf_op jit(solution)/shard_map/up_2/pallas_call | solution.py:302
  27.3 8.9 %all_to_all.31 = bf16[160,2,128]{2,1,0:T(2,128)(2,1)S(1)} all-to-all(bf16[160,2,128]{2,1,0:T(2,128)(2,1)S(1)} %bitcast.24), channel_id=1, replica_groups={{0,4,12,8,24,28,20,16,17,21,29,25,9,13,5,1,3,7,15,11,27,31,23,19,18,22,..., dimensions={0} | all-to-all | bytes 163840 | tf_op jit(solution)/shard_map/all_to_all | solution.py:329
  36.1 0.7 %top.1 = (bf16[320,128]{1,0:T(8,128)(2,1)S(1)}, bf16[32,512]{1,0:T(8,128)(2,1)S(1)}) custom-call(bf16[320,128]{1,0:T(8,128)(2,1)S(1)} %bitcast.17, bf16[4,32,512]{2,1,0:T(8,128)(2,1)S(1)} %get-tuple-element.30.right, bf16[512,512]{1,0:T(8,128)(2,1)S(1)} %get-tuple-element.42.square, s32[3,1,320]{2,1,0:T(1,128)S(1)} %get-tuple-element.37.takes), custom_call_target="tpu_custom_call" | custom-call | flops 1000000 | bytes 1048576 | tf_op jit(solution)/shard_map/top/pallas_call | solution.py:302
  36.8 8.9 %all_to_all.32 = bf16[160,2,128]{2,1,0:T(2,128)(2,1)S(1)} all-to-all(bf16[160,2,128]{2,1,0:T(2,128)(2,1)S(1)} %bitcast.21), channel_id=1, replica_groups={{0,4,12,8,24,28,20,16,17,21,29,25,9,13,5,1,3,7,15,11,27,31,23,19,18,22,..., dimensions={0} | all-to-all | bytes 163840 | tf_op jit(solution)/shard_map/all_to_all | solution.py:329
  45.7 0.6 down_2.1
  46.3 8.9 %all_to_all.33 = bf16[160,2,128]{2,1,0:T(2,128)(2,1)S(1)} all-to-all(bf16[160,2,128]{2,1,0:T(2,128)(2,1)S(1)} %bitcast.22), channel_id=1, replica_groups={{0,4,12,8,24,28,20,16,17,21,29,25,9,13,5,1,3,7,15,11,27,31,23,19,18,22,..., dimensions={0} | all-to-all | bytes 163840 | tf_op jit(solution)/shard_map/all_to_all | solution.py:329
  55.2 0.6 down_1.1
  55.8 8.9 %all_to_all.34 = bf16[160,2,128]{2,1,0:T(2,128)(2,1)S(1)} all-to-all(bf16[160,2,128]{2,1,0:T(2,128)(2,1)S(1)} %bitcast.20), channel_id=1, replica_groups={{0,4,12,8,24,28,20,16,17,21,29,25,9,13,5,1,3,7,15,11,27,31,23,19,18,22,..., dimensions={0} | all-to-all | bytes 163840 | tf_op jit(solution)/shard_map/all_to_all | solution.py:329
  64.6 1.0 %last.1 = bf16[1,1,4,32,512]{4,3,2,1,0:T(8,128)(2,1)} custom-call(bf16[320,128]{1,0:T(8,128)(2,1)S(1)} %bitcast.16, bf16[32,512]{1,0:T(8,128)(2,1)S(1)} %get-tuple-element.48.start, bf16[256,512]{1,0:T(8,128)(2,1)S(1)} %get-tuple-element.49.product, s32[3,1,256]{2,1,0:T(1,128)S(1)} %get-tuple-element.36.sends, s32[4,1,128]{2,1,0:T(1,128)S(1)} %get-tuple-element.32.limits, ...), custom_call_target="tpu_custom_call" | custom-call | flops 1000000 | bytes 1048576 | tf_op jit(solution)/shard_map/last/pallas_call | solution.py:302
Async XLA Ops:
  2.5 14.5 %all-to-all-start = ((bf16[160,2,128]{2,1,0:T(2,128)(2,1)}), bf16[160,2,128]{2,1,0:T(2,128)(2,1)S(1)}, u32[]{:S(2)}, u32[]{:S(2)}) async-start(bf16[160,2,128]{2,1,0:T(2,128)(2,1)} %bitcast.1), calls=%async_computation | async-start | bytes 163840 | tf_op jit(solution)/shard_map/all_to_all | solution.py:329

commit v11 on v9

--- a/solution.py
+++ b/solution.py
@@ -252,10 +252,10 @@
 def top_kernel(sizes, level, arrived, right, limits, inverse, take, forward, first, buffer, solution, start):
     taker = take_matrix(sizes, take[...])
     solved = solve_forward(sizes, level, limits, residual_of(sizes, level, arrived, right, taker), inverse)
+    value = solve_back(sizes, level, limits, solved, inverse)
+    solution[...] = value
     start[...] = solve_back(sizes, 0, limits, forward[...], first)
-    value = solve_back(sizes, level, limits, solved, inverse)
     buffer[...] = cross_dot(taker, to_flat(sizes, value)).astype(BF16)
-    solution[...] = value
 
 
 def solution_of(sizes, level, arrived, start, product, send, limits):

time: 65.8 us -> 65.8 us (level)
  no operation moved by 1% of the time
where the time goes in v11:
time: 65.8 us; the launch traced here: 65.5 us
  blocking collectives  58.5 us (89%)
  Pallas kernels  6.94 us (11%)
    all_to_all x6, blocking collectives, exchange(): lax.all_to_all(blocks, axes, split_axis=0, concat_axis=0, tiled=True, axi...  58.5 us
    pallas_call x7, Pallas kernels, call(): pl.pallas_call(kernel, in_specs=[HBM] * far + [VMEM] * (len(operands) - f...  6.94 us

profile of v11, /device:TPU:0, one launch (start us, length us, event | category | flops | bytes accessed | tf_op | source)
XLA Modules:
  0.0 65.5 jit_solution(14147108780722644738)
XLA Ops:
  0.0 2.2 %start.1 = (bf16[320,128]{1,0:T(8,128)(2,1)S(1)}, bf16[32,512]{1,0:T(8,128)(2,1)S(1)}, s32[4,1,128]{2,1,0:T(1,128)S(1)}, bf16[4,32,512]{2,1,0:T(8,128)(2,1)S(1)}...) custom-call(bf16[1,1,4,32,512]{4,3,2,1,0:T(8,128)(2,1)} %bitcast.26,, ...), custom_call_target="tpu_custom_call" | custom-call | flops 1000000000 | bytes 1048576 | tf_op jit(solution)/shard_map/start/pallas_call | solution.py:289
  2.2 14.3 %all_to_all.30 = bf16[160,2,128]{2,1,0:T(2,128)(2,1)S(1)} all-to-all(bf16[160,2,128]{2,1,0:T(2,128)(2,1)S(1)} %bitcast.20), channel_id=1, replica_groups={{0,4,12,8,24,28,20,16,17,21,29,25,9,13,5,1,3,7,15,11,27,31,23,19,18,22,..., dimensions={0} | all-to-all | bytes 163840 | tf_op jit(solution)/shard_map/all_to_all | solution.py:317
  16.5 0.8 %up_1.1 = (bf16[320,128]{1,0:T(8,128)(2,1)S(1)}, bf16[32,512]{1,0:T(8,128)(2,1)S(1)}, s32[1,320]{1,0:T(1,128)S(1)}, bf16[256,512]{1,0:T(8,128)(2,1)S(1)}, s32[1,256]{1,0:T(1,128)S(1)}) custom-call(bf16[320,128]{1,0:T(8,128)(2,1)S(1)} %bitcast.14, bf16[4,32,512]{2,1,0:T(8,128)(2,1)S(1)} %get-tuple-element.37.right, ...), custom_call_target="tpu_custom_call" | custom-call | flops 1000000 | bytes 1048576 | tf_op jit(solution)/shard_map/up_1/pallas_call | solution.py:289
  17.3 8.8 %all_to_all.31 = bf16[160,2,128]{2,1,0:T(2,128)(2,1)S(1)} all-to-all(bf16[160,2,128]{2,1,0:T(2,128)(2,1)S(1)} %bitcast.22), channel_id=1, replica_groups={{0,4,12,8,24,28,20,16,17,21,29,25,9,13,5,1,3,7,15,11,27,31,23,19,18,22,..., dimensions={0} | all-to-all | bytes 163840 | tf_op jit(solution)/shard_map/all_to_all | solution.py:317
  26.1 0.8 %up_2.1 = (bf16[320,128]{1,0:T(8,128)(2,1)S(1)}, bf16[32,512]{1,0:T(8,128)(2,1)S(1)}, s32[1,320]{1,0:T(1,128)S(1)}, bf16[256,512]{1,0:T(8,128)(2,1)S(1)}) custom-call(bf16[320,128]{1,0:T(8,128)(2,1)S(1)} %bitcast.15, bf16[4,32,512]{2,1,0:T(8,128)(2,1)S(1)} %get-tuple-element.37.right, s32[4,1,128]{2,1,0:T(1,128)S(1)} %get-tuple-element.38.limits, ...), custom_call_target="tpu_custom_call" | custom-call | flops 1000000 | bytes 1048576 | tf_op jit(solution)/shard_map/up_2/pallas_call | solution.py:289
  26.9 8.8 %all_to_all.32 = bf16[160,2,128]{2,1,0:T(2,128)(2,1)S(1)} all-to-all(bf16[160,2,128]{2,1,0:T(2,128)(2,1)S(1)} %bitcast.23), channel_id=1, replica_groups={{0,4,12,8,24,28,20,16,17,21,29,25,9,13,5,1,3,7,15,11,27,31,23,19,18,22,..., dimensions={0} | all-to-all | bytes 163840 | tf_op jit(solution)/shard_map/all_to_all | solution.py:317
  35.8 0.9 %top.1 = (bf16[320,128]{1,0:T(8,128)(2,1)S(1)}, bf16[32,512]{1,0:T(8,128)(2,1)S(1)}, bf16[32,512]{1,0:T(8,128)(2,1)S(1)}) custom-call(bf16[320,128]{1,0:T(8,128)(2,1)S(1)} %bitcast.19, bf16[4,32,512]{2,1,0:T(8,128)(2,1)S(1)} %get-tuple-element.37.right, s32[4,1,128]{2,1,0:T(1,128)S(1)} %get-tuple-element.38.limits, ...), custom_call_target="tpu_custom_call" | custom-call | flops 1000000 | bytes 1048576 | tf_op jit(solution)/shard_map/top/pallas_call | solution.py:289
  36.7 8.9 %all_to_all.33 = bf16[160,2,128]{2,1,0:T(2,128)(2,1)S(1)} all-to-all(bf16[160,2,128]{2,1,0:T(2,128)(2,1)S(1)} %bitcast.21), channel_id=1, replica_groups={{0,4,12,8,24,28,20,16,17,21,29,25,9,13,5,1,3,7,15,11,27,31,23,19,18,22,..., dimensions={0} | all-to-all | bytes 163840 | tf_op jit(solution)/shard_map/all_to_all | solution.py:317
  45.5 0.6 down_2.1
  46.2 8.9 %all_to_all.34 = bf16[160,2,128]{2,1,0:T(2,128)(2,1)S(1)} all-to-all(bf16[160,2,128]{2,1,0:T(2,128)(2,1)S(1)} %bitcast.24), channel_id=1, replica_groups={{0,4,12,8,24,28,20,16,17,21,29,25,9,13,5,1,3,7,15,11,27,31,23,19,18,22,..., dimensions={0} | all-to-all | bytes 163840 | tf_op jit(solution)/shard_map/all_to_all | solution.py:317
  55.0 0.6 down_1.1
  55.6 8.9 %all_to_all.35 = bf16[160,2,128]{2,1,0:T(2,128)(2,1)S(1)} all-to-all(bf16[160,2,128]{2,1,0:T(2,128)(2,1)S(1)} %bitcast.25), channel_id=1, replica_groups={{0,4,12,8,24,28,20,16,17,21,29,25,9,13,5,1,3,7,15,11,27,31,23,19,18,22,..., dimensions={0} | all-to-all | bytes 163840 | tf_op jit(solution)/shard_map/all_to_all | solution.py:317
  64.5 1.0 %last.1 = bf16[1,1,4,32,512]{4,3,2,1,0:T(8,128)(2,1)} custom-call(bf16[320,128]{1,0:T(8,128)(2,1)S(1)} %bitcast.16, bf16[32,512]{1,0:T(8,128)(2,1)S(1)} %get-tuple-element.61.start, bf16[256,512]{1,0:T(8,128)(2,1)S(1)} %get-tuple-element.62.product, s32[1,256]{1,0:T(1,128)S(1)} %get-tuple-element.63.send, s32[4,1,128]{2,1,0:T(1,128)S(1)} %get-tuple-element.38.limits, ...), custom_call_target="tpu_custom_call" | custom-call | flops 1000000 | bytes 1048576 | tf_op jit(solution)/shard_map/last/pallas_call | solution.py:289
